TPU v7x, 32 devices: a whole 2x2x4 slice. The times are simulated.
32 devices in a mesh: league: 2 (over y), snap: 4 (over z), tp: 4 (over x, core).
Axes of the slice: x: 2, y: 2, z: 4, core: 2. Of those that a mesh axis runs over, the one named last changes fastest.
Arguments:
- block_states: bfloat16 [8, 128, 4096], P(('league', 'snap'), None, 'tp'), parts along dimension 0, may hold values from -6 to 6
- lengths: int32 [8], P('league'), parts along dimension 0, may hold values from 1 to 128, as said below
- norm_gain: float32 [4, 4096], P('snap'), may hold values from 0.5 to 2
- query_weight: bfloat16 [4, 4096, 4096], P('snap', None, 'tp'), may hold values from -4 to 4
- keyval_weight: bfloat16 [4, 4096, 512], P('snap', 'tp'), may hold values from -0.09375 to 0.09375
Outputs:
- ensemble_out: bfloat16 [8, 128, 4096], P(('league', 'snap'), None, 'tp'), parts along dimension 0
There are 2 independent parts, one for each index of `league`. A program takes and returns all parts, laid end to end along the dimension named above; an argument that names none is the same for every part. Nothing has to cross between parts.
Inputs may be any that keep to these rules, and one draw needn't show every extreme that they name: `lengths`: some block has exactly 128 valid tokens.
All inputs are finite; a program needn't handle non-finite values.
Results may differ from a plain program's by a relative error of at most 0.008.
The roundings to bfloat16 on the way count: a program that leaves them out, or rounds other values in their place, can miss the bound.
Values may be sent and summed in bfloat16 or wider, within the bound.
No kernel may reach another device: no remote copies, remote signals or barrier semaphores. Data moves between devices by JAX's collectives and lax.ppermute only.
A program may use at most 64 MiB of HBM per device.

v0:
```python
import jax
import jax.numpy as jnp
from jax import lax
from jax.sharding import PartitionSpec as P

QHEADS = 64
KVHEADS = 4
HD = 64
VISITS = 4


EPSILON = 1e-05
ROPE_BASE = 500000.0


def passed_along(array, axis, by):
    devices = lax.axis_size(axis)
    return lax.ppermute(array, axis, [(i, (i + by) % devices) for i in range(devices)])


def rope_tables(row_count, head_width):
    half_width = head_width // 2
    positions = jnp.arange(row_count, dtype=jnp.float32)[:, None]
    frequency = ROPE_BASE ** (-jnp.arange(half_width, dtype=jnp.float32) * 2.0 / head_width)
    angles = positions * frequency[None, :]
    return (jnp.cos(angles), jnp.sin(angles))


def rotate(head_vectors, cosine_table, sine_table):
    half_width = head_vectors.shape[-1] // 2
    first_half = head_vectors[..., :half_width]
    second_half = head_vectors[..., half_width:]
    cosine_part = cosine_table[:, None, :]
    sine_part = sine_table[:, None, :]
    return jnp.concatenate(
        [
            first_half * cosine_part - second_half * sine_part,
            first_half * sine_part + second_half * cosine_part,
        ],
        axis=-1,
    )


def local_term(states, length, gain_row, query_proj, keyval_proj, tp_rank):
    row_count = states.shape[0]
    states_f32 = states.astype(jnp.float32)
    normed = (
        states_f32
        * lax.rsqrt(jnp.mean(states_f32 * states_f32, axis=1, keepdims=True) + EPSILON)
        * gain_row[None, :]
    ).astype(jnp.bfloat16)
    feature_count = keyval_proj.shape[0]
    normed_part = lax.dynamic_slice_in_dim(normed, tp_rank * feature_count, feature_count, 1)
    keyval_term = jnp.dot(normed_part, keyval_proj, preferred_element_type=jnp.float32)
    keyval = lax.psum(keyval_term, "tp").astype(jnp.bfloat16)
    cosine_table, sine_table = rope_tables(row_count, HD)
    queries = jnp.dot(normed, query_proj, preferred_element_type=jnp.float32)
    heads_here = query_proj.shape[1] // HD
    queries = rotate(queries.reshape(row_count, heads_here, HD), cosine_table, sine_table).astype(
        jnp.bfloat16
    )
    keyval = keyval.reshape(row_count, KVHEADS, 2, HD)
    key_heads = rotate(keyval[:, :, 0].astype(jnp.float32), cosine_table, sine_table).astype(
        jnp.bfloat16
    )
    value_heads = keyval[:, :, 1]
    group_size = QHEADS // KVHEADS
    kv_ids = (tp_rank * heads_here + jnp.arange(heads_here, dtype=jnp.int32)) // group_size
    my_keys = jnp.take(key_heads, kv_ids, axis=1)
    my_values = jnp.take(value_heads, kv_ids, axis=1)
    scores = jnp.einsum(
        "qhd,khd->hqk", queries, my_keys, preferred_element_type=jnp.float32
    ) * HD ** (-0.5)
    positions = jnp.arange(row_count, dtype=jnp.int32)
    allowed = (positions[None, :] <= positions[:, None]) & (positions[None, :] < length)
    masked = jnp.where(allowed[None], scores, jnp.float32(-1e30))
    row_top = jnp.max(masked, axis=2, keepdims=True)
    weights = jnp.where(allowed[None], jnp.exp(masked - row_top), 0.0)
    probabilities = (weights / jnp.sum(weights, axis=2, keepdims=True)).astype(jnp.bfloat16)
    context = jnp.einsum(
        "hqk,khd->qhd", probabilities, my_values, preferred_element_type=jnp.float32
    ).astype(jnp.bfloat16)
    return context.reshape(row_count, heads_here * HD).astype(jnp.float32)


def on_device(block_states, lengths, norm_gain, query_weight, keyval_weight):
    snap_rank = lax.axis_index("snap")
    snap_count = lax.axis_size("snap")
    tp_rank = lax.axis_index("tp")
    own_shard = block_states[0]
    gain_row = norm_gain[0]
    query_proj = query_weight[0]
    keyval_proj = keyval_weight[0]

    def widen_block(carried):
        return lax.all_gather(carried, "tp", axis=1, tiled=True)

    def visit_term(carried, visit_step):
        block_id = (snap_rank - visit_step) % snap_count
        return local_term(
            widen_block(carried), lengths[block_id], gain_row, query_proj, keyval_proj, tp_rank
        )

    partial_value = visit_term(own_shard, 0)
    for visit_step in range(1, VISITS):
        visiting = passed_along(own_shard, "snap", visit_step)
        partial_value = partial_value + passed_along(
            visit_term(visiting, visit_step).astype(jnp.bfloat16), "snap", -visit_step
        ).astype(jnp.float32)
    home_length = lengths[snap_rank]
    row_keep = (jnp.arange(partial_value.shape[0], dtype=jnp.int32) < home_length)[:, None]
    ensemble = jnp.where(row_keep, partial_value / VISITS, 0.0).astype(jnp.bfloat16)
    return ensemble[None]


def solution(mesh):
    placed = (
        P(("league", "snap"), None, "tp"),
        P("league"),
        P("snap", None),
        P("snap", None, "tp"),
        P("snap", "tp", None),
    )
    return jax.shard_map(
        on_device,
        mesh=mesh,
        in_specs=placed,
        out_specs=P(("league", "snap"), None, "tp"),
        check_vma=False,
    )
```

profile of v0, /device:TPU:0, one launch (start us, length us, event | category | flops | bytes accessed | tf_op | source)
XLA Modules:
  0.0 180.0 jit_solution(13805838939467484217)
XLA Ops:
  7.3 5.1 %collective-permute-start.4 = (bf16[128,1024]{1,0:T(8,128)(2,1)}, bf16[128,1024]{1,0:T(8,128)(2,1)S(1)}, u32[]{:S(2)}, u32[]{:S(2)}) collective-permute-start(bf16[128,1024]{1,0:T(8,128)(2,1)} %bitcast.152), channel_id=1, source_target_pairs={{0,12},{4,0},{8,4},{12,8},{1,13},{5,1},{9,5},{13,9},{2,14},{6,2},{... | collective-permute-start | bytes 786440 | tf_op jit(solution)/shard_map/ppermute | solution.py:18
  12.4 5.9 %collective-permute-done.4 = bf16[128,1024]{1,0:T(8,128)(2,1)S(1)} collective-permute-done((bf16[128,1024]{1,0:T(8,128)(2,1)}, bf16[128,1024]{1,0:T(8,128)(2,1)S(1)}, u32[]{:S(2)}, u32[]{:S(2)}) %collective-permute-start.4) | collective-permute-done | bytes 262176 | tf_op jit(solution)/shard_map/ppermute | solution.py:18
  20.5 3.4 %collective-permute-start = (bf16[128,1024]{1,0:T(8,128)(2,1)}, bf16[128,1024]{1,0:T(8,128)(2,1)S(1)}, u32[]{:S(2)}, u32[]{:S(2)}) collective-permute-start(bf16[128,1024]{1,0:T(8,128)(2,1)} %bitcast.154), channel_id=1, source_target_pairs={{0,4},{4,8},{8,12},{12,0},{1,5},{5,9},{9,13},{13,1},{2,6},{6,10},{... | collective-permute-start | bytes 786440 | tf_op jit(solution)/shard_map/ppermute | solution.py:18
  23.9 14.8 %collective-permute-done.2 = bf16[128,1024]{1,0:T(8,128)(2,1)S(1)} collective-permute-done((bf16[128,1024]{1,0:T(8,128)(2,1)}, bf16[128,1024]{1,0:T(8,128)(2,1)S(1)}, u32[]{:S(2)}, u32[]{:S(2)}) %collective-permute-start.2) | collective-permute-done | bytes 262176 | tf_op jit(solution)/shard_map/ppermute | solution.py:18
  48.8 11.4 %copy.24 = bf16[1,4096,1024]{1,2,0:T(8,128)(2,1)} copy(bf16[1,4096,1024]{2,1,0:T(8,128)(2,1)} %param.10) | data formatting | bytes 16777216 | tf_op args[3]
  63.1 1.6 fusion.10
  66.6 16.6 %all-gather.6.cloned.1.call-done = bf16[128,4096]{1,0:T(8,128)(2,1)} async-done(((bf16[128,1024]{1,0:T(8,128)(2,1)}), bf16[128,4096]{1,0:T(8,128)(2,1)}) %all-gather.6.cloned.1.call-update) | async-done | bytes 1048592 | tf_op jit(solution)/shard_map/all_gather | solution.py:96
  84.8 3.2 %fusion.6 = (bf16[128,4096]{1,0:T(8,128)(2,1)S(1)}, bf16[128,4096]{1,0:T(8,128)(2,1)S(1)}, bf16[128,4096]{1,0:T(8,128)(2,1)S(1)}, bf16[128,4096]{1,0:T(8,128)(2,1)S(1)}) fusion(bf16[128,4096]{1,0:T(8,128)(2,1)} %all-gather.6.cloned.1.call-done, f32[128]{0:T(128)S(1)} %add_rsqrt_fusion.2, f32[4096]{0:T(1024)S(1)} %bitcast.158, f32[128]{0:T(128)S(1)} %add_rsqrt_fusion.1, ...), kind=kLoop, calls=%fused_computation.22 | loop fusion | flops 8388608 | bytes 8407040 | tf_op jit(solution)/shard_map/convert_element_type | solution.py:51
  89.3 2.3 %fusion.33 = f32[128,16,64]{0,2,1:T(8,128)S(1)} fusion(bf16[16,64,4096]{2,1,0:T(8,128)(2,1)S(1)} %bitcast.143, bf16[128,4096]{1,0:T(8,128)(2,1)S(1)} %get-tuple-element.48), kind=kOutput, calls=%fused_computation.57 | convolution fusion | flops 1073741824 | bytes 9961472 | tf_op jit(solution)/shard_map/dot_general | solution.py:57
  91.6 2.3 %fusion.39 = f32[128,16,64]{0,2,1:T(8,128)S(1)} fusion(bf16[16,64,4096]{2,1,0:T(8,128)(2,1)S(1)} %bitcast.144, bf16[128,4096]{1,0:T(8,128)(2,1)S(1)} %get-tuple-element.49), kind=kOutput, calls=%fused_computation.63 | convolution fusion | flops 1073741824 | bytes 9961472 | tf_op jit(solution)/shard_map/dot_general | solution.py:57
  95.0 2.3 %fusion.35 = f32[128,16,64]{0,2,1:T(8,128)S(1)} fusion(bf16[16,64,4096]{2,1,0:T(8,128)(2,1)S(1)} %bitcast.145, bf16[128,4096]{1,0:T(8,128)(2,1)S(1)} %get-tuple-element.47), kind=kOutput, calls=%fused_computation.59 | convolution fusion | flops 1073741824 | bytes 9961472 | tf_op jit(solution)/shard_map/dot_general | solution.py:57
  98.4 2.5 %fusion.37 = f32[128,16,64]{0,2,1:T(8,128)S(1)} fusion(bf16[16,64,4096]{2,1,0:T(8,128)(2,1)S(1)} %bitcast.146, bf16[128,4096]{1,0:T(8,128)(2,1)S(1)} %get-tuple-element.46), kind=kOutput, calls=%fused_computation.61 | convolution fusion | flops 1073741824 | bytes 9961472 | tf_op jit(solution)/shard_map/dot_general | solution.py:57
  100.9 26.7 %all-reduce.2 = (bf16[128,512]{1,0:T(8,128)(2,1)}, bf16[128,512]{1,0:T(8,128)(2,1)}, bf16[128,512]{1,0:T(8,128)(2,1)}, bf16[128,512]{1,0:T(8,128)(2,1)S(1)}) all-reduce(f32[128,512]{1,0:T(8,128)S(1)} %fusion.41, f32[128,512]{1,0:T(8,128)} %fusion.43, f32[128,512]{1,0:T(8,128)} %fusion.47, ...), channel_id=1, replica_groups=mesh['league'=2,'snap'=4,'tp'=4] {'tp'}, use_global_device_ids=true, to_apply=%region_13.15 | all-reduce | flops 262144 | bytes 1572864 | tf_op jit(solution)/shard_map/psum | solution.py:55
  129.5 1.7 copy.32
  132.7 1.7 copy.36
  135.2 1.7 subtract_convert_fusion.6
  139.7 1.9 %subtract_convert_fusion.2 = (bf16[128,16,32]{0,2,1:T(8,128)(2,1)}, bf16[128,16,32]{0,2,1:T(8,128)(2,1)}, bf16[128,16,32]{0,2,1:T(8,128)(2,1)}, bf16[128,16,32]{...) fusion(f32[128,16,64]{0,2,1:T(8,128)S(1)} %fusion.37, ...), kind=kLoop, calls=%fused_computation.115 | loop fusion | flops 2097152 | bytes 3178496 | tf_op jit(solution)/shard_map/convert.16
  141.6 1.8 fusion.201
  143.9 3.6 %collective-permute-start.1 = (bf16[128,1024]{1,0:T(8,128)(2,1)S(1)}, bf16[128,1024]{1,0:T(8,128)(2,1)S(1)}, u32[]{:S(2)}, u32[]{:S(2)}) collective-permute-start(bf16[128,1024]{1,0:T(8,128)(2,1)S(1)} %copy.30), channel_id=1, source_target_pairs={{0,12},{4,0},{8,4},{12,8},{1,13},{5,1},{9,5},{13,9},{2,14},{6,2},{... | collective-permute-start | bytes 786440 | tf_op jit(solution)/shard_map/ppermute | solution.py:18
  150.1 1.6 fusion.191
  154.8 2.5 %fusion.186 = (f32[16,128]{1,0:T(8,128)S(1)}, f32[16,128,128]{1,2,0:T(8,128)}) fusion(pred[128,128]{0,1:T(8,128)(4,1)S(1)} %copy-done.20, bf16[128,16,32]{0,2,1:T(8,128)(2,1)S(1)} %copy-done.10, bf16[128,16,32]{0,2,1:T(8,128)(2,1)} %get-tuple-element.43, bf16[16,128,64]{1,2,0:T(8,128)(2,1)S(1)} %gather_fusion.7, pred[16]{0:T(512)(128)(4,1)S(1)} %copy-done.25), kind=kOutput, calls=%fused_computation.222 | convolution fusion | flops 35520640 | bytes 1597456 | tf_op jit(solution)/shard_map/sub | solution.py:78
  160.2 1.6 fusion.196
  163.6 8.1 %collective-permute-done.3 = bf16[128,1024]{1,0:T(8,128)(2,1)S(1)} collective-permute-done((bf16[128,1024]{1,0:T(8,128)(2,1)S(1)}, bf16[128,1024]{1,0:T(8,128)(2,1)S(1)}, u32[]{:S(2)}, u32[]{:S(2)}) %collective-permute-start.3) | collective-permute-done | bytes 262176 | tf_op jit(solution)/shard_map/ppermute | solution.py:18
  171.7 1.8 %fusion.50 = bf16[1,128,1024]{2,1,0:T(8,128)(2,1)} fusion(bf16[128,1024]{1,0:T(8,128)(2,1)} %collective-permute-done.5, bf16[128,1024]{1,0:T(8,128)(2,1)S(1)} %collective-permute-done.3, f32[128,1024]{1,0:T(8,128)S(1)} %copy.31, bf16[128,1024]{1,0:T(8,128)(2,1)S(1)} %collective-permute-done.1, pred[128]{0:T(512)(128)(4,1)S(1)} %copy-done.23), kind=kLoop, calls=%fused_computation.79 | loop fusion | flops 1179648 | bytes 1572992 | tf_op jit(solution)/shard_map/broadcast_in_dim | solution.py:113
  (119 shorter events, 40.2 us)
Async XLA Ops:
  6.5 81.4 %copy-start = (bf16[1,1024,512]{2,1,0:T(8,128)(2,1)S(1)}, bf16[1,1024,512]{2,1,0:T(8,128)(2,1)}, u32[]{:S(2)}) copy-start(bf16[1,1024,512]{2,1,0:T(8,128)(2,1)} %param.11) | copy-start | bytes 3145732
  6.5 55.0 %all-gather.12.cloned.1.call-start = ((), (), s32[]{:S(2)}) async-start(), calls=%async_computation.3 | async-start | bytes 1310720 | tf_op jit(solution)/shard_map/all_gather | solution.py:96
  7.3 55.9 %all-gather.10.cloned.1.call-start = ((), (), s32[]{:S(2)}) async-start(), calls=%async_computation.2 | async-start | bytes 1310720 | tf_op jit(solution)/shard_map/all_gather | solution.py:96
  7.3 11.0 %collective-permute-start.4 = (bf16[128,1024]{1,0:T(8,128)(2,1)}, bf16[128,1024]{1,0:T(8,128)(2,1)S(1)}, u32[]{:S(2)}, u32[]{:S(2)}) collective-permute-start(bf16[128,1024]{1,0:T(8,128)(2,1)} %bitcast.152), channel_id=1, source_target_pairs={{0,12},{4,0},{8,4},{12,8},{1,13},{5,1},{9,5},{13,9},{2,14},{6,2},{... | collective-permute-start | bytes 786440 | tf_op jit(solution)/shard_map/ppermute | solution.py:18
  19.0 46.0 %all-gather.8.cloned.1.call-start = ((), (), s32[]{:S(2)}) async-start(), calls=%async_computation.1 | async-start | bytes 1310720 | tf_op jit(solution)/shard_map/all_gather | solution.py:96
  19.1 19.6 %collective-permute-start.2 = (bf16[128,1024]{1,0:T(8,128)(2,1)}, bf16[128,1024]{1,0:T(8,128)(2,1)S(1)}, u32[]{:S(2)}, u32[]{:S(2)}) collective-permute-start(bf16[128,1024]{1,0:T(8,128)(2,1)} %bitcast.153), channel_id=1, source_target_pairs={{0,8},{4,12},{8,0},{12,4},{1,9},{5,13},{9,1},{13,5},{2,10},{6,14},... | collective-permute-start | bytes 786440 | tf_op jit(solution)/shard_map/ppermute | solution.py:18
  20.5 26.4 %collective-permute-start = (bf16[128,1024]{1,0:T(8,128)(2,1)}, bf16[128,1024]{1,0:T(8,128)(2,1)S(1)}, u32[]{:S(2)}, u32[]{:S(2)}) collective-permute-start(bf16[128,1024]{1,0:T(8,128)(2,1)} %bitcast.154), channel_id=1, source_target_pairs={{0,4},{4,8},{8,12},{12,0},{1,5},{5,9},{9,13},{13,1},{2,6},{6,10},{... | collective-permute-start | bytes 786440 | tf_op jit(solution)/shard_map/ppermute | solution.py:18
  39.4 43.8 %all-gather.6.cloned.1.call-start = ((), (), s32[]{:S(2)}) async-start(), calls=%async_computation | async-start | bytes 1310720 | tf_op jit(solution)/shard_map/all_gather | solution.py:96
  61.5 23.2 %copy-start.17 = (f32[1,4096]{1,0:T(1,128)S(1)}, f32[1,4096]{1,0:T(1,128)}, u32[]{:S(2)}) copy-start(f32[1,4096]{1,0:T(1,128)} %param.9) | copy-start | bytes 49156
  61.5 23.2 %copy-start.2 = (bf16[1,128,4096]{2,1,0:T(8,128)(2,1)S(1)}, bf16[1,128,4096]{2,1,0:T(8,128)(2,1)}, u32[]{:S(2)}) copy-start(bf16[1,128,4096]{2,1,0:T(8,128)(2,1)} %all-gather.12.cloned.1.call-done) | copy-start | bytes 3145732
  63.1 21.6 %copy-start.3 = (bf16[128,4096]{1,0:T(8,128)(2,1)S(1)}, bf16[128,4096]{1,0:T(8,128)(2,1)}, u32[]{:S(2)}) copy-start(bf16[128,4096]{1,0:T(8,128)(2,1)} %all-gather.10.cloned.1.call-done) | copy-start | bytes 3145732
  84.8 4.5 %copy-start.1 = (bf16[1,4096,1024]{1,2,0:T(8,128)(2,1)S(1)}, bf16[1,4096,1024]{1,2,0:T(8,128)(2,1)}, u32[]{:S(2)}) copy-start(bf16[1,4096,1024]{1,2,0:T(8,128)(2,1)} %copy.24) | copy-start | bytes 25165828
  143.4 4.2 %copy-start.18 = (s32[1024]{0:T(1024)S(1)}, s32[1024]{0:T(1024)}, u32[]{:S(2)}) copy-start(s32[1024]{0:T(1024)} %pad_clamp_fusion) | copy-start | bytes 12292
  143.7 5.1 %copy-start.13 = (bf16[128,4,32]{0,2,1:T(8,128)(2,1)S(1)}, bf16[128,4,32]{0,2,1:T(8,128)(2,1)}, u32[]{:S(2)}) copy-start(bf16[128,4,32]{0,2,1:T(8,128)(2,1)} %get-tuple-element.34) | copy-start | bytes 98308
  143.8 5.1 %copy-start.14 = (bf16[128,4,32]{0,2,1:T(8,128)(2,1)S(1)}, bf16[128,4,32]{0,2,1:T(8,128)(2,1)}, u32[]{:S(2)}) copy-start(bf16[128,4,32]{0,2,1:T(8,128)(2,1)} %get-tuple-element.35) | copy-start | bytes 98308
  143.8 5.1 %copy-start.15 = (bf16[128,4,32]{0,2,1:T(8,128)(2,1)S(1)}, bf16[128,4,32]{0,2,1:T(8,128)(2,1)}, u32[]{:S(2)}) copy-start(bf16[128,4,32]{0,2,1:T(8,128)(2,1)} %get-tuple-element.36) | copy-start | bytes 98308
  143.8 5.1 %copy-start.16 = (bf16[128,4,32]{0,2,1:T(8,128)(2,1)S(1)}, bf16[128,4,32]{0,2,1:T(8,128)(2,1)}, u32[]{:S(2)}) copy-start(bf16[128,4,32]{0,2,1:T(8,128)(2,1)} %get-tuple-element.37) | copy-start | bytes 98308
  143.9 19.6 %collective-permute-start.1 = (bf16[128,1024]{1,0:T(8,128)(2,1)S(1)}, bf16[128,1024]{1,0:T(8,128)(2,1)S(1)}, u32[]{:S(2)}, u32[]{:S(2)}) collective-permute-start(bf16[128,1024]{1,0:T(8,128)(2,1)S(1)} %copy.30), channel_id=1, source_target_pairs={{0,12},{4,0},{8,4},{12,8},{1,13},{5,1},{9,5},{13,9},{2,14},{6,2},{... | collective-permute-start | bytes 786440 | tf_op jit(solution)/shard_map/ppermute | solution.py:18
  153.5 18.2 %collective-permute-start.3 = (bf16[128,1024]{1,0:T(8,128)(2,1)S(1)}, bf16[128,1024]{1,0:T(8,128)(2,1)S(1)}, u32[]{:S(2)}, u32[]{:S(2)}) collective-permute-start(bf16[128,1024]{1,0:T(8,128)(2,1)S(1)} %copy.35), channel_id=1, source_target_pairs={{0,8},{4,12},{8,0},{12,4},{1,9},{5,13},{9,1},{13,5},{2,10},{6,14},... | collective-permute-start | bytes 786440 | tf_op jit(solution)/shard_map/ppermute | solution.py:18
  157.3 2.9 %copy-start.8 = (bf16[128,16,32]{0,2,1:T(8,128)(2,1)S(1)}, bf16[128,16,32]{0,2,1:T(8,128)(2,1)}, u32[]{:S(2)}) copy-start(bf16[128,16,32]{0,2,1:T(8,128)(2,1)} %get-tuple-element.44) | copy-start | bytes 393220
  157.3 2.9 %copy-start.9 = (bf16[128,16,32]{0,2,1:T(8,128)(2,1)S(1)}, bf16[128,16,32]{0,2,1:T(8,128)(2,1)}, u32[]{:S(2)}) copy-start(bf16[128,16,32]{0,2,1:T(8,128)(2,1)} %get-tuple-element.45) | copy-start | bytes 393220
  157.3 2.9 %copy-start.19 = (pred[128,128]{0,1:T(8,128)(4,1)S(1)}, pred[128,128]{0,1:T(8,128)(4,1)}, u32[]{:S(2)}) copy-start(pred[128,128]{0,1:T(8,128)(4,1)} %fusion.122) | copy-start | bytes 49156
  159.1 12.6 %collective-permute-start.5 = (bf16[128,1024]{1,0:T(8,128)(2,1)S(1)}, bf16[128,1024]{1,0:T(8,128)(2,1)}, u32[]{:S(2)}, u32[]{:S(2)}) collective-permute-start(bf16[128,1024]{1,0:T(8,128)(2,1)S(1)} %copy.39), channel_id=1, source_target_pairs={{0,4},{4,8},{8,12},{12,0},{1,5},{5,9},{9,13},{13,1},{2,6},{6,10},{... | collective-permute-start | bytes 786440 | tf_op jit(solution)/shard_map/ppermute | solution.py:18
  161.8 9.8 %copy-start.23 = (pred[128]{0:T(512)(128)(4,1)S(1)}, pred[128]{0:T(512)(128)(4,1)}, u32[]{:S(2)}) copy-start(pred[128]{0:T(512)(128)(4,1)} %iota_compare_fusion.5) | copy-start | bytes 388
  (12 other events, 20.8 us)
Sparse Core Ops, SparseCore 0:
  8.9 19.4 all-gather.11
  29.9 16.7 all-gather.9
  48.3 16.7 all-gather.7
  66.4 16.7 all-gather.5
where the time goes:
time: 181 us; the launch traced here: 180 us
  waiting for transfers between devices  46.4 us (26%)
  blocking collectives  26.7 us (15%)
  local copies, waits for them, and re-layouts  26.6 us (15%)
  other arithmetic  26.2 us (14%)
  matrix products  25.5 us (14%)
  starting transfers between devices  14.9 us (8%)
  between operations  13.7 us (8%)
    ppermute x6, waiting for transfers between devices, passed_along(): lax.ppermute(array, axis, [(i, (i + by) % devices) for i in range(devices)])  28.7 us
    psum x1, blocking collectives, local_term(): keyval = lax.psum(keyval_term, 'tp').astype(jnp.bfloat16)  26.7 us
    all_gather x4, waiting for transfers between devices, widen_block(): return lax.all_gather(carried, 'tp', axis=1, tiled=True)  16.9 us
    ppermute x6, starting transfers between devices, passed_along(): lax.ppermute(array, axis, [(i, (i + by) % devices) for i in range(devices)])  14.7 us
    unnamed x53, local copies, waits for them, and re-layouts  13.6 us
    dot_general x4, matrix products, local_term(): queries = jnp.dot(normed, query_proj, preferred_element_type=jnp.float32)  9.51 us
    sub x4, matrix products, local_term(): weights = jnp.where(allowed[None], jnp.exp(masked - row_top), 0.0)  7.54 us
    reduce_sum x4, other arithmetic, local_term(): jnp.mean(states_f32 * states_f32, axis=1, keepdims=True) + EPSILON  6.26 us
  transfers between devices with their start and end apart: 10, of which 5 were waited for; matrix products, arithmetic and copies ran while one was open for 23% of the time, Pallas kernels for 0%

commit v1 on v0

v1 whole, which is shorter than its diff:
```python
import functools

import jax
import jax.numpy as jnp
from jax import lax
from jax.experimental import pallas as pl
from jax.experimental.pallas import tpu as pltpu
from jax.sharding import PartitionSpec as P

QHEADS = 64
KVHEADS = 4
HD = 64
VISITS = 4
LANES = 128

EPSILON = 1e-05
ROPE_BASE = 500000.0
LOG2E = 1.4426950408889634


def ring_pairs(count, by):
    return [(i, (i + by) % count) for i in range(count)]


def swapped(array, with_bits):
    count = lax.axis_size("tp")
    return lax.ppermute(array, "tp", [(i, i ^ with_bits) for i in range(count)])


def rope_tables(row_count):
    half = HD // 2
    positions = jnp.arange(row_count, dtype=jnp.float32)[:, None]
    frequency = ROPE_BASE ** (-jnp.arange(half, dtype=jnp.float32) * 2.0 / HD)
    angles = positions * frequency[None, :]
    cosine, sine = jnp.cos(angles), jnp.sin(angles)
    repeats = LANES // HD
    return (
        jnp.concatenate([cosine, cosine] * repeats, axis=1),
        jnp.concatenate([-sine, sine] * repeats, axis=1),
    )


def rotated(pair, cosine, signed_sine, in_first_half):
    half = HD // 2
    partner = jnp.where(
        in_first_half, pltpu.roll(pair, LANES - half, 1), pltpu.roll(pair, half, 1)
    )
    return pair * cosine + partner * signed_sine


def visit_kernel(parts, visit, lengths_ref, *refs):
    shards = refs[:parts]
    gain_ref, query_ref = refs[parts : parts + 2]
    keyvals = refs[parts + 2 : 2 * parts + 2]
    cosine_ref, sine_ref, out_ref, normed_ref, query_out_ref = refs[2 * parts + 2 :]
    rows, features = shards[0].shape
    width = parts * features
    rank = lax.axis_index("tp")
    snaps = lax.axis_size("snap")
    block = lax.rem(lax.axis_index("snap") + (snaps - visit), snaps)
    length = lengths_ref[block]

    squares = jnp.zeros((rows, 1), jnp.float32)
    for shard in shards:
        values = shard[...].astype(jnp.float32)
        squares += jnp.sum(values * values, axis=1, keepdims=True)
    scale = lax.rsqrt(squares / width + EPSILON)
    keyval = jnp.zeros((rows, keyvals[0].shape[1]), jnp.float32)
    for bits, shard in enumerate(shards):
        owner = lax.bitwise_xor(rank, jnp.int32(bits))
        normed = (shard[...].astype(jnp.float32) * scale * gain_ref[pl.ds(owner, 1), :]).astype(
            jnp.bfloat16
        )
        normed_ref[owner] = normed
        keyval += jnp.dot(normed, keyvals[bits][...], preferred_element_type=jnp.float32)

    cosine, sine = cosine_ref[...], sine_ref[...]
    lane = lax.broadcasted_iota(jnp.int32, (rows, LANES), 1)
    in_first_half = lax.rem(lane, HD) < HD // 2
    in_first_head = lane < HD
    keyval = keyval.astype(jnp.bfloat16).astype(jnp.float32)
    keys = jnp.where(in_first_head, rotated(keyval, cosine, sine, in_first_half), 0.0)
    keys = jnp.concatenate([keys, pltpu.roll(keys, HD, 1)], axis=0).astype(jnp.bfloat16)
    values = jnp.where(in_first_head, 0.0, keyval)
    values = jnp.concatenate([pltpu.roll(values, HD, 1), values], axis=0).astype(jnp.bfloat16)

    row = lax.broadcasted_iota(jnp.int32, (rows, rows), 0)
    column = lax.broadcasted_iota(jnp.int32, (rows, rows), 1)
    allowed = (column <= row) & (column < length)
    step = 2 * LANES
    for start in range(0, query_ref.shape[2], step):
        total = jnp.zeros((rows, step), jnp.float32)
        for part in range(parts):
            total += jnp.dot(
                normed_ref[part],
                query_ref[part, :, start : start + step],
                preferred_element_type=jnp.float32,
            )
        for pair in range(0, step, LANES):
            queries = rotated(
                total[:, pair : pair + LANES], cosine, sine, in_first_half
            ).astype(jnp.bfloat16)
            scores = lax.dot_general(
                queries, keys, (((1,), (1,)), ((), ())), preferred_element_type=jnp.float32
            )
            halves = []
            for head in range(2):
                mine = jnp.where(allowed, scores[:, head * rows : (head + 1) * rows], -1e30)
                top = jnp.max(mine, axis=1, keepdims=True)
                weights = jnp.exp2((mine - top) * (LOG2E * HD**-0.5))
                whole = jnp.sum(weights, axis=1, keepdims=True)
                halves.append((weights * (1.0 / whole)).astype(jnp.bfloat16))
            context = jnp.dot(
                jnp.concatenate(halves, axis=1), values, preferred_element_type=jnp.float32
            )
            out_ref[:, start + pair : start + pair + LANES] = context.astype(jnp.bfloat16)


def visit_context(visit, lengths, shards, gain, query, keyvals, cosine, sine):
    parts = len(shards)
    rows, features = shards[0].shape
    columns = query.shape[2]
    vmem = pl.BlockSpec(memory_space=pltpu.VMEM)
    operands = (*shards, gain, query, *keyvals, cosine, sine)
    return pl.pallas_call(
        functools.partial(visit_kernel, parts, visit),
        out_shape=jax.ShapeDtypeStruct((rows, columns), jnp.bfloat16),
        in_specs=[pl.BlockSpec(memory_space=pltpu.SMEM)] + [vmem] * len(operands),
        out_specs=vmem,
        scratch_shapes=[
            pltpu.VMEM((parts, rows, features), jnp.bfloat16),
            pltpu.VMEM((rows, columns), jnp.float32),
        ],
        compiler_params=pltpu.CompilerParams(vmem_limit_bytes=24 * 1024 * 1024),
        cost_estimate=pl.CostEstimate(
            flops=2 * rows * parts * features * (columns + LANES),
            bytes_accessed=2 * parts * features * columns,
            transcendentals=rows * rows * columns // HD,
        ),
        name=f"visit_{visit}",
    )(lengths, *operands)


def mean_kernel(lengths_ref, *refs):
    terms, out_ref = refs[:-1], refs[-1]
    rows = out_ref.shape[0]
    length = lengths_ref[lax.axis_index("snap")]
    total = terms[0][...].astype(jnp.float32)
    for term in terms[1:]:
        total += term[...].astype(jnp.float32)
    keep = lax.broadcasted_iota(jnp.int32, (rows, 1), 0) < length
    out_ref[...] = jnp.where(keep, total / len(terms), 0.0).astype(jnp.bfloat16)


def mean_of(lengths, terms):
    vmem = pl.BlockSpec(memory_space=pltpu.VMEM)
    return pl.pallas_call(
        mean_kernel,
        out_shape=jax.ShapeDtypeStruct(terms[0].shape, jnp.bfloat16),
        in_specs=[pl.BlockSpec(memory_space=pltpu.SMEM)] + [vmem] * len(terms),
        out_specs=vmem,
        name="mean_of_visits",
    )(lengths, *terms)


def on_device(block_states, lengths, norm_gain, query_weight, keyval_weight):
    snaps = lax.axis_size("snap")
    parts = lax.axis_size("tp")
    rank = lax.axis_index("tp")
    own = block_states[0]
    rows, features = own.shape
    gain = norm_gain[0].reshape(parts, features)
    query = query_weight[0].reshape(parts, features, query_weight.shape[2])
    heads_here = query.shape[2] // HD
    group = QHEADS // KVHEADS
    cosine, sine = rope_tables(rows)

    keyvals = []
    for bits in range(parts):
        head = (lax.bitwise_xor(rank, jnp.int32(bits)) * heads_here) // group
        columns = lax.dynamic_slice_in_dim(keyval_weight[0], head * 2 * HD, 2 * HD, 1)
        keyvals.append(swapped(columns, bits) if bits else columns)

    blocks = [own]
    for _ in range(1, VISITS):
        blocks.append(lax.ppermute(blocks[-1], "snap", ring_pairs(snaps, 1)))

    terms = [None] * VISITS
    for visit in (*range(1, VISITS), 0):
        shards = {0: blocks[visit]}
        for bits in range(2, parts, 2):
            shards[bits] = swapped(blocks[visit], bits)
        for bits in range(1, parts, 2):
            shards[bits] = swapped(shards[bits - 1], 1)
        context = visit_context(
            visit,
            lengths,
            [shards[bits] for bits in range(parts)],
            gain,
            query,
            keyvals,
            cosine,
            sine,
        )
        terms[visit] = (
            lax.ppermute(context, "snap", ring_pairs(snaps, -visit)) if visit else context
        )
    return mean_of(lengths, terms)[None]


def solution(mesh):
    placed = (
        P(("league", "snap"), None, "tp"),
        P("league"),
        P("snap", None),
        P("snap", None, "tp"),
        P("snap", "tp", None),
    )
    return jax.shard_map(
        on_device,
        mesh=mesh,
        in_specs=placed,
        out_specs=P(("league", "snap"), None, "tp"),
        check_vma=False,
    )
```

time: 181 us -> 93.8 us (0.52)
  Pallas kernels: 0 us -> 30 us
  blocking collectives: 26.7 us -> 0 us
  matrix products: 25.5 us -> 0 us
  other arithmetic: 26.2 us -> 2.33 us
  local copies, waits for them, and re-layouts: 26.6 us -> 10.3 us
  between operations: 13.7 us -> 0.19 us
  waiting for transfers between devices: 46.4 us -> 33.5 us
  starting transfers between devices: 14.9 us -> 17.1 us
    pallas_call x0 -> x5, Pallas kernels: none -> 30 us  [the longest x4 28 us: visit_context(): pl.pallas_call(functools.partial(visit_kernel, parts, visit), out_shape=j...]
    psum x1 -> x0, blocking collectives: 26.7 us -> none  [local_term(): keyval = lax.psum(keyval_term, 'tp').astype(jnp.bfloat16)]
    dot_general x12 -> x0, matrix products: 17.9 us -> none  [the longest x4 9.51 us: local_term(): queries = jnp.dot(normed, query_proj, preferred_element_type=jnp.float32)]
    all_gather x4 -> x0, waiting for transfers between devices: 16.9 us -> none  [widen_block(): return lax.all_gather(carried, 'tp', axis=1, tiled=True)]
    sub x4 -> x0, matrix products: 7.54 us -> none  [local_term(): weights = jnp.where(allowed[None], jnp.exp(masked - row_top), 0.0)]
    gather x8 -> x0, local copies, waits for them, and re-layouts: 6.38 us -> none  [the longest x4 3.2 us: local_term(): my_keys = jnp.take(key_heads, kv_ids, axis=1)]
    reduce_sum x4 -> x0, other arithmetic: 6.26 us -> none  [local_term(): jnp.mean(states_f32 * states_f32, axis=1, keepdims=True) + EPSILON]
    unnamed x53 -> x23, local copies, waits for them, and re-layouts: 13.6 us -> 8.28 us
  transfers between devices with their start and end apart: 10 -> 21, of which waited for: 5 -> 8; matrix products, arithmetic and copies ran while one was open for 23% -> 5% of each run, Pallas kernels for 0% -> 30%
where the time goes in v1:
time: 93.8 us; the launch traced here: 93.4 us
  waiting for transfers between devices  33.5 us (36%)
  Pallas kernels  30 us (32%)
  starting transfers between devices  17.1 us (18%)
  local copies, waits for them, and re-layouts  10.3 us (11%)
  other arithmetic  2.33 us (2%)
    pallas_call x4, Pallas kernels, visit_context(): pl.pallas_call(functools.partial(visit_kernel, parts, visit), out_shape=j...  28 us
    ppermute x3, waiting for transfers between devices, on_device(): blocks.append(lax.ppermute(blocks[-1], 'snap', ring_pairs(snaps, 1)))  15.9 us
    ppermute x15, waiting for transfers between devices, swapped(): return lax.ppermute(array, 'tp', [(i, i ^ with_bits) for i in range(count)])  14.9 us
    ppermute x15, starting transfers between devices, swapped(): return lax.ppermute(array, 'tp', [(i, i ^ with_bits) for i in range(count)])  9.15 us
    unnamed x23, local copies, waits for them, and re-layouts  8.28 us
    ppermute x3, starting transfers between devices, on_device(): lax.ppermute(context, 'snap', ring_pairs(snaps, -visit))  4.9 us
    ppermute x3, starting transfers between devices, on_device(): blocks.append(lax.ppermute(blocks[-1], 'snap', ring_pairs(snaps, 1)))  3.03 us
    ppermute x3, waiting for transfers between devices, on_device(): lax.ppermute(context, 'snap', ring_pairs(snaps, -visit))  2.61 us
  transfers between devices with their start and end apart: 21, of which 8 were waited for; matrix products, arithmetic and copies ran while one was open for 5% of the time, Pallas kernels for 30%

profile of v1, /device:TPU:0, one launch (start us, length us, event | category | flops | bytes accessed | tf_op | source)
XLA Modules:
  0.0 93.4 jit_solution(253160590079101014)
XLA Ops:
  0.0 3.0 %collective-permute-start.6 = (bf16[128,1024]{1,0:T(8,128)(2,1)}, bf16[128,1024]{1,0:T(8,128)(2,1)S(1)}, u32[]{:S(2)}, u32[]{:S(2)}) collective-permute-start(bf16[128,1024]{1,0:T(8,128)(2,1)} %bitcast.17), channel_id=1, source_target_pairs={{0,4},{4,8},{8,12},{12,0},{1,5},{5,9},{9,13},{13,1},{2,6},{6,10},{... | collective-permute-start | bytes 786440 | tf_op jit(solution)/shard_map/ppermute | solution.py:186
  3.0 8.6 %collective-permute-done.6.refs_0_ = bf16[128,1024]{1,0:T(8,128)(2,1)S(1)} collective-permute-done((bf16[128,1024]{1,0:T(8,128)(2,1)}, bf16[128,1024]{1,0:T(8,128)(2,1)S(1)}, u32[]{:S(2)}, u32[]{:S(2)}) %collective-permute-start.6) | collective-permute-done | bytes 262176 | tf_op jit(solution)/shard_map/ppermute | solution.py:186
  11.6 1.3 %dynamic-slice_bitcast_fusion = (bf16[1024,128]{1,0:T(8,128)(2,1)S(1)}, bf16[1024,128]{1,0:T(8,128)(2,1)S(1)}, bf16[1024,128]{1,0:T(8,128)(2,1)S(1)}, bf16[1024,128]{1,0:T(8,128)(2,1)S(1)}) fusion(bf16[1,1024,512]{2,1,0:T(8,128)(2,1)} %param.9, s32[]{:T(128)S(6)} %select_n.33, s32[]{:T(128)S(6)} %select_n.29, s32[]{:T(128)S(6)} %select_n.27, s32[]{:T(128)S(6)} %select_n.31), kind=kLoop, calls=%fused_computation | loop fusion | bytes 2097168 | tf_op jit(solution)/shard_map/dynamic_slice | solution.py:181
  13.0 1.6 %collective-permute-start.4 = (bf16[1024,128]{1,0:T(8,128)(2,1)S(1)}, bf16[1024,128]{1,0:T(8,128)(2,1)S(1)}, u32[]{:S(2)}, u32[]{:S(2)}) collective-permute-start(bf16[1024,128]{1,0:T(8,128)(2,1)S(1)} %get-tuple-element.8), channel_id=1, source_target_pairs={{0,2},{1,3},{2,0},{3,1},{4,6},{5,7},{6,4},{7,5},{8,10},{9,11},{10,... | collective-permute-start | bytes 786440 | tf_op jit(solution)/shard_map/ppermute | solution.py:27
  15.1 5.8 %collective-permute-done.11.refs_0_ = bf16[128,1024]{1,0:T(8,128)(2,1)S(1)} collective-permute-done((bf16[128,1024]{1,0:T(8,128)(2,1)S(1)}, bf16[128,1024]{1,0:T(8,128)(2,1)S(1)}, u32[]{:S(2)}, u32[]{:S(2)}) %collective-permute-start.11) | collective-permute-done | bytes 262176 | tf_op jit(solution)/shard_map/ppermute | solution.py:186
  20.9 1.4 %collective-permute-start.7 = (bf16[128,1024]{1,0:T(8,128)(2,1)S(1)}, bf16[128,1024]{1,0:T(8,128)(2,1)S(1)}, u32[]{:S(2)}, u32[]{:S(2)}) collective-permute-start(bf16[128,1024]{1,0:T(8,128)(2,1)S(1)} %collective-permute-done.6.refs_0_), channel_id=1, source_target_pairs={{0,1},{1,0},{2,3},{3,2},{4,5},{5,4},{6,7},{7,6},{8,9},{9,8},{10,11... | collective-permute-start | bytes 786440 | tf_op jit(solution)/shard_map/ppermute | solution.py:27
  22.4 1.3 %collective-permute-start.13 = (bf16[128,1024]{1,0:T(8,128)(2,1)S(1)}, bf16[128,1024]{1,0:T(8,128)(2,1)S(1)}, u32[]{:S(2)}, u32[]{:S(2)}) collective-permute-start(bf16[128,1024]{1,0:T(8,128)(2,1)S(1)} %collective-permute-done.11.refs_0_), channel_id=1, source_target_pairs={{0,2},{1,3},{2,0},{3,1},{4,6},{5,7},{6,4},{7,5},{8,10},{9,11},{10,... | collective-permute-start | bytes 786440 | tf_op jit(solution)/shard_map/ppermute | solution.py:27
  23.7 4.1 %collective-permute-done.8.refs_2_ = bf16[128,1024]{1,0:T(8,128)(2,1)S(1)} collective-permute-done((bf16[128,1024]{1,0:T(8,128)(2,1)S(1)}, bf16[128,1024]{1,0:T(8,128)(2,1)S(1)}, u32[]{:S(2)}, u32[]{:S(2)}) %collective-permute-start.8) | collective-permute-done | bytes 262176 | tf_op jit(solution)/shard_map/ppermute | solution.py:27
  27.8 1.5 %collective-permute-done.16.refs_0_ = bf16[128,1024]{1,0:T(8,128)(2,1)S(1)} collective-permute-done((bf16[128,1024]{1,0:T(8,128)(2,1)S(1)}, bf16[128,1024]{1,0:T(8,128)(2,1)S(1)}, u32[]{:S(2)}, u32[]{:S(2)}) %collective-permute-start.16) | collective-permute-done | bytes 262176 | tf_op jit(solution)/shard_map/ppermute | solution.py:186
  29.3 1.2 %collective-permute-start.18 = (bf16[128,1024]{1,0:T(8,128)(2,1)S(1)}, bf16[128,1024]{1,0:T(8,128)(2,1)S(1)}, u32[]{:S(2)}, u32[]{:S(2)}) collective-permute-start(bf16[128,1024]{1,0:T(8,128)(2,1)S(1)} %collective-permute-done.16.refs_0_), channel_id=1, source_target_pairs={{0,2},{1,3},{2,0},{3,1},{4,6},{5,7},{6,4},{7,5},{8,10},{9,11},{10,... | collective-permute-start | bytes 786440 | tf_op jit(solution)/shard_map/ppermute | solution.py:27
  30.5 2.1 %collective-permute-done.5.refs_9_ = bf16[1024,128]{1,0:T(8,128)(2,1)S(1)} collective-permute-done((bf16[1024,128]{1,0:T(8,128)(2,1)S(1)}, bf16[1024,128]{1,0:T(8,128)(2,1)S(1)}, u32[]{:S(2)}, u32[]{:S(2)}) %collective-permute-start.5) | collective-permute-done | bytes 262176 | tf_op jit(solution)/shard_map/ppermute | solution.py:27
  32.5 1.5 %collective-permute-start.1 = (bf16[128,1024]{1,0:T(8,128)(2,1)}, bf16[128,1024]{1,0:T(8,128)(2,1)S(1)}, u32[]{:S(2)}, u32[]{:S(2)}) collective-permute-start(bf16[128,1024]{1,0:T(8,128)(2,1)} %bitcast.18), channel_id=1, source_target_pairs={{0,2},{1,3},{2,0},{3,1},{4,6},{5,7},{6,4},{7,5},{8,10},{9,11},{10,... | collective-permute-start | bytes 786440 | tf_op jit(solution)/shard_map/ppermute | solution.py:27
  34.5 4.6 %collective-permute-done.13.refs_2_ = bf16[128,1024]{1,0:T(8,128)(2,1)S(1)} collective-permute-done((bf16[128,1024]{1,0:T(8,128)(2,1)S(1)}, bf16[128,1024]{1,0:T(8,128)(2,1)S(1)}, u32[]{:S(2)}, u32[]{:S(2)}) %collective-permute-start.13) | collective-permute-done | bytes 262176 | tf_op jit(solution)/shard_map/ppermute | solution.py:27
  40.5 4.1 %collective-permute-done.18.refs_2_ = bf16[128,1024]{1,0:T(8,128)(2,1)S(1)} collective-permute-done((bf16[128,1024]{1,0:T(8,128)(2,1)S(1)}, bf16[128,1024]{1,0:T(8,128)(2,1)S(1)}, u32[]{:S(2)}, u32[]{:S(2)}) %collective-permute-start.18) | collective-permute-done | bytes 262176 | tf_op jit(solution)/shard_map/ppermute | solution.py:27
  45.3 1.9 %reduce.3 = f32[4096]{0:T(1024)} reduce(f32[1,4096]{1,0:T(1,128)} %param.7, f32[]{:T(128)} %broadcast.18), dimensions={0}, to_apply=%param.7.reduce_sub_computation.3 | reduce | bytes 32772 | tf_op args[2]
  47.9 3.4 %copy-done = bf16[1,4096,1024]{2,1,0:T(8,128)(2,1)S(1)} copy-done((bf16[1,4096,1024]{2,1,0:T(8,128)(2,1)S(1)}, bf16[1,4096,1024]{2,1,0:T(8,128)(2,1)}, u32[]{:S(2)}) %copy-start) | copy-done | bytes 8388632
  51.3 0.9 %copy-done.4 = bf16[128,1024]{1,0:T(8,128)(2,1)S(1)} copy-done((bf16[128,1024]{1,0:T(8,128)(2,1)S(1)}, bf16[128,1024]{1,0:T(8,128)(2,1)}, u32[]{:S(2)}) %copy-start.4) | copy-done | bytes 262168
  52.9 6.7 %visit_1.1 = bf16[128,1024]{1,0:T(8,128)(2,1)S(1)} custom-call(s32[4]{0:T(128)S(1)} %copy-done.5, bf16[128,1024]{1,0:T(8,128)(2,1)S(1)} %collective-permute-done.6.refs_0_, bf16[128,1024]{1,0:T(8,128)(2,1)S(1)} %collective-permute-done.7.refs_1_, bf16[128,1024]{1,0:T(8,128)(2,1)S(1)} %collective-permute-done.8.refs_2_, bf16[128,1024]{1,0:T(8,128)(2,1)S(1)} %copy-done.4, ...), custom_call_target="tpu_custom_call" | custom-call | flops 1207959552 | bytes 8388608 | tf_op jit(solution)/shard_map/visit_1/pallas_call | solution.py:125
  60.3 4.0 %collective-permute-start.10 = (bf16[128,1024]{1,0:T(8,128)(2,1)S(1)}, bf16[128,1024]{1,0:T(8,128)(2,1)S(1)}, u32[]{:S(2)}, u32[]{:S(2)}) collective-permute-start(bf16[128,1024]{1,0:T(8,128)(2,1)S(1)} %visit_1.1), channel_id=1, source_target_pairs={{0,12},{4,0},{8,4},{12,8},{1,13},{5,1},{9,5},{13,9},{2,14},{6,2},{... | collective-permute-start | bytes 786440 | tf_op jit(solution)/shard_map/ppermute | solution.py:206
  64.3 7.2 %visit_2.1 = bf16[128,1024]{1,0:T(8,128)(2,1)S(1)} custom-call(s32[4]{0:T(128)S(1)} %copy-done.5, bf16[128,1024]{1,0:T(8,128)(2,1)S(1)} %collective-permute-done.11.refs_0_, bf16[128,1024]{1,0:T(8,128)(2,1)} %collective-permute-done.12.refs_1_, bf16[128,1024]{1,0:T(8,128)(2,1)S(1)} %collective-permute-done.13.refs_2_, ...), custom_call_target="tpu_custom_call" | custom-call | flops 1207959552 | bytes 8388608 | tf_op jit(solution)/shard_map/visit_2/pallas_call | solution.py:125
  71.6 7.4 %visit_3.1 = bf16[128,1024]{1,0:T(8,128)(2,1)S(1)} custom-call(s32[4]{0:T(128)S(1)} %copy-done.5, bf16[128,1024]{1,0:T(8,128)(2,1)S(1)} %collective-permute-done.16.refs_0_, bf16[128,1024]{1,0:T(8,128)(2,1)} %collective-permute-done.17.refs_1_, bf16[128,1024]{1,0:T(8,128)(2,1)S(1)} %collective-permute-done.18.refs_2_, ...), custom_call_target="tpu_custom_call" | custom-call | flops 1207959552 | bytes 8388608 | tf_op jit(solution)/shard_map/visit_3/pallas_call | solution.py:125
  79.9 6.7 %visit_0.1.refs_0_ = bf16[128,1024]{1,0:T(8,128)(2,1)S(1)} custom-call(s32[4]{0:T(128)S(1)} %copy-done.5, bf16[128,1024]{1,0:T(8,128)(2,1)S(1)} %bitcast.20, bf16[128,1024]{1,0:T(8,128)(2,1)S(1)} %collective-permute-done.refs_1_, bf16[128,1024]{1,0:T(8,128)(2,1)S(1)} %collective-permute-done.1.refs_2_, bf16[128,1024]{1,0:T(8,128)(2,1)S(1)} %collective-permute-done.2.refs_3_, ...), custom_call_target="tpu_custom_call" | custom-call | flops 1207959552 | bytes 8388608 | tf_op jit(solution)/shard_map/visit_0/pallas_call | solution.py:125
  87.3 2.6 %collective-permute-done.15.refs_2_ = bf16[128,1024]{1,0:T(8,128)(2,1)S(1)} collective-permute-done((bf16[128,1024]{1,0:T(8,128)(2,1)S(1)}, bf16[128,1024]{1,0:T(8,128)(2,1)S(1)}, u32[]{:S(2)}, u32[]{:S(2)}) %collective-permute-start.15) | collective-permute-done | bytes 262176 | tf_op jit(solution)/shard_map/ppermute | solution.py:206
  91.3 2.1 %mean_of_visits.1 = bf16[128,1024]{1,0:T(8,128)(2,1)} custom-call(s32[4]{0:T(128)} %lengths_ref.9, bf16[128,1024]{1,0:T(8,128)(2,1)} %copy-done.1, bf16[128,1024]{1,0:T(8,128)(2,1)} %copy-done.6, bf16[128,1024]{1,0:T(8,128)(2,1)} %copy-done.7, bf16[128,1024]{1,0:T(8,128)(2,1)} %copy-done.8), custom_call_target="tpu_custom_call" | custom-call | tf_op jit(solution)/shard_map/mean_of_visits/pallas_call | solution.py:157
  (53 shorter events, 8.3 us)
Async XLA Ops:
  0.0 59.7 %copy-start.2 = (bf16[1,128,1024]{2,1,0:T(8,128)(2,1)S(1)}, bf16[1,128,1024]{2,1,0:T(8,128)(2,1)}, u32[]{:S(2)}) copy-start(bf16[1,128,1024]{2,1,0:T(8,128)(2,1)} %param.5) | copy-start | bytes 786436
  0.0 11.6 %collective-permute-start.6 = (bf16[128,1024]{1,0:T(8,128)(2,1)}, bf16[128,1024]{1,0:T(8,128)(2,1)S(1)}, u32[]{:S(2)}, u32[]{:S(2)}) collective-permute-start(bf16[128,1024]{1,0:T(8,128)(2,1)} %bitcast.17), channel_id=1, source_target_pairs={{0,4},{4,8},{8,12},{12,0},{1,5},{5,9},{9,13},{13,1},{2,6},{6,10},{... | collective-permute-start | bytes 786440 | tf_op jit(solution)/shard_map/ppermute | solution.py:186
  11.6 9.3 %collective-permute-start.11 = (bf16[128,1024]{1,0:T(8,128)(2,1)S(1)}, bf16[128,1024]{1,0:T(8,128)(2,1)S(1)}, u32[]{:S(2)}, u32[]{:S(2)}) collective-permute-start(bf16[128,1024]{1,0:T(8,128)(2,1)S(1)} %collective-permute-done.6.refs_0_), channel_id=1, source_target_pairs={{0,4},{4,8},{8,12},{12,0},{1,5},{5,9},{9,13},{13,1},{2,6},{6,10},{... | collective-permute-start | bytes 786440 | tf_op jit(solution)/shard_map/ppermute | solution.py:186
  12.9 8.0 %collective-permute-start.3 = (bf16[1024,128]{1,0:T(8,128)(2,1)S(1)}, bf16[1024,128]{1,0:T(8,128)(2,1)S(1)}, u32[]{:S(2)}, u32[]{:S(2)}) collective-permute-start(bf16[1024,128]{1,0:T(8,128)(2,1)S(1)} %get-tuple-element.6), channel_id=1, source_target_pairs={{0,1},{1,0},{2,3},{3,2},{4,5},{5,4},{6,7},{7,6},{8,9},{9,8},{10,11... | collective-permute-start | bytes 786440 | tf_op jit(solution)/shard_map/ppermute | solution.py:27
  13.0 9.4 %collective-permute-start.4 = (bf16[1024,128]{1,0:T(8,128)(2,1)S(1)}, bf16[1024,128]{1,0:T(8,128)(2,1)S(1)}, u32[]{:S(2)}, u32[]{:S(2)}) collective-permute-start(bf16[1024,128]{1,0:T(8,128)(2,1)S(1)} %get-tuple-element.8), channel_id=1, source_target_pairs={{0,2},{1,3},{2,0},{3,1},{4,6},{5,7},{6,4},{7,5},{8,10},{9,11},{10,... | collective-permute-start | bytes 786440 | tf_op jit(solution)/shard_map/ppermute | solution.py:27
  14.6 13.2 %collective-permute-start.8 = (bf16[128,1024]{1,0:T(8,128)(2,1)S(1)}, bf16[128,1024]{1,0:T(8,128)(2,1)S(1)}, u32[]{:S(2)}, u32[]{:S(2)}) collective-permute-start(bf16[128,1024]{1,0:T(8,128)(2,1)S(1)} %collective-permute-done.6.refs_0_), channel_id=1, source_target_pairs={{0,2},{1,3},{2,0},{3,1},{4,6},{5,7},{6,4},{7,5},{8,10},{9,11},{10,... | collective-permute-start | bytes 786440 | tf_op jit(solution)/shard_map/ppermute | solution.py:27
  20.9 8.4 %collective-permute-start.16 = (bf16[128,1024]{1,0:T(8,128)(2,1)S(1)}, bf16[128,1024]{1,0:T(8,128)(2,1)S(1)}, u32[]{:S(2)}, u32[]{:S(2)}) collective-permute-start(bf16[128,1024]{1,0:T(8,128)(2,1)S(1)} %collective-permute-done.11.refs_0_), channel_id=1, source_target_pairs={{0,4},{4,8},{8,12},{12,0},{1,5},{5,9},{9,13},{13,1},{2,6},{6,10},{... | collective-permute-start | bytes 786440 | tf_op jit(solution)/shard_map/ppermute | solution.py:186
  20.9 11.6 %collective-permute-start.5 = (bf16[1024,128]{1,0:T(8,128)(2,1)S(1)}, bf16[1024,128]{1,0:T(8,128)(2,1)S(1)}, u32[]{:S(2)}, u32[]{:S(2)}) collective-permute-start(bf16[1024,128]{1,0:T(8,128)(2,1)S(1)} %get-tuple-element.5), channel_id=1, source_target_pairs={{0,3},{1,2},{2,1},{3,0},{4,7},{5,6},{6,5},{7,4},{8,11},{9,10},{10,... | collective-permute-start | bytes 786440 | tf_op jit(solution)/shard_map/ppermute | solution.py:27
  20.9 13.1 %collective-permute-start.7 = (bf16[128,1024]{1,0:T(8,128)(2,1)S(1)}, bf16[128,1024]{1,0:T(8,128)(2,1)S(1)}, u32[]{:S(2)}, u32[]{:S(2)}) collective-permute-start(bf16[128,1024]{1,0:T(8,128)(2,1)S(1)} %collective-permute-done.6.refs_0_), channel_id=1, source_target_pairs={{0,1},{1,0},{2,3},{3,2},{4,5},{5,4},{6,7},{7,6},{8,9},{9,8},{10,11... | collective-permute-start | bytes 786440 | tf_op jit(solution)/shard_map/ppermute | solution.py:27
  22.4 16.7 %collective-permute-start.13 = (bf16[128,1024]{1,0:T(8,128)(2,1)S(1)}, bf16[128,1024]{1,0:T(8,128)(2,1)S(1)}, u32[]{:S(2)}, u32[]{:S(2)}) collective-permute-start(bf16[128,1024]{1,0:T(8,128)(2,1)S(1)} %collective-permute-done.11.refs_0_), channel_id=1, source_target_pairs={{0,2},{1,3},{2,0},{3,1},{4,6},{5,7},{6,4},{7,5},{8,10},{9,11},{10,... | collective-permute-start | bytes 786440 | tf_op jit(solution)/shard_map/ppermute | solution.py:27
  27.8 11.5 %collective-permute-start.9 = (bf16[128,1024]{1,0:T(8,128)(2,1)S(1)}, bf16[128,1024]{1,0:T(8,128)(2,1)S(1)}, u32[]{:S(2)}, u32[]{:S(2)}) collective-permute-start(bf16[128,1024]{1,0:T(8,128)(2,1)S(1)} %collective-permute-done.8.refs_2_), channel_id=1, source_target_pairs={{0,1},{1,0},{2,3},{3,2},{4,5},{5,4},{6,7},{7,6},{8,9},{9,8},{10,11... | collective-permute-start | bytes 786440 | tf_op jit(solution)/shard_map/ppermute | solution.py:27
  29.3 15.4 %collective-permute-start.18 = (bf16[128,1024]{1,0:T(8,128)(2,1)S(1)}, bf16[128,1024]{1,0:T(8,128)(2,1)S(1)}, u32[]{:S(2)}, u32[]{:S(2)}) collective-permute-start(bf16[128,1024]{1,0:T(8,128)(2,1)S(1)} %collective-permute-done.16.refs_0_), channel_id=1, source_target_pairs={{0,2},{1,3},{2,0},{3,1},{4,6},{5,7},{6,4},{7,5},{8,10},{9,11},{10,... | collective-permute-start | bytes 786440 | tf_op jit(solution)/shard_map/ppermute | solution.py:27
  32.5 27.2 %collective-permute-start.1 = (bf16[128,1024]{1,0:T(8,128)(2,1)}, bf16[128,1024]{1,0:T(8,128)(2,1)S(1)}, u32[]{:S(2)}, u32[]{:S(2)}) collective-permute-start(bf16[128,1024]{1,0:T(8,128)(2,1)} %bitcast.18), channel_id=1, source_target_pairs={{0,2},{1,3},{2,0},{3,1},{4,6},{5,7},{6,4},{7,5},{8,10},{9,11},{10,... | collective-permute-start | bytes 786440 | tf_op jit(solution)/shard_map/ppermute | solution.py:27
  34.0 26.2 %collective-permute-start.12 = (bf16[128,1024]{1,0:T(8,128)(2,1)S(1)}, bf16[128,1024]{1,0:T(8,128)(2,1)}, u32[]{:S(2)}, u32[]{:S(2)}) collective-permute-start(bf16[128,1024]{1,0:T(8,128)(2,1)S(1)} %collective-permute-done.11.refs_0_), channel_id=1, source_target_pairs={{0,1},{1,0},{2,3},{3,2},{4,5},{5,4},{6,7},{7,6},{8,9},{9,8},{10,11... | collective-permute-start | bytes 786440 | tf_op jit(solution)/shard_map/ppermute | solution.py:27
  39.0 21.3 %collective-permute-start.14 = (bf16[128,1024]{1,0:T(8,128)(2,1)S(1)}, bf16[128,1024]{1,0:T(8,128)(2,1)}, u32[]{:S(2)}, u32[]{:S(2)}) collective-permute-start(bf16[128,1024]{1,0:T(8,128)(2,1)S(1)} %collective-permute-done.13.refs_2_), channel_id=1, source_target_pairs={{0,1},{1,0},{2,3},{3,2},{4,5},{5,4},{6,7},{7,6},{8,9},{9,8},{10,11... | collective-permute-start | bytes 786440 | tf_op jit(solution)/shard_map/ppermute | solution.py:27
  40.0 31.5 %collective-permute-start.17 = (bf16[128,1024]{1,0:T(8,128)(2,1)S(1)}, bf16[128,1024]{1,0:T(8,128)(2,1)}, u32[]{:S(2)}, u32[]{:S(2)}) collective-permute-start(bf16[128,1024]{1,0:T(8,128)(2,1)S(1)} %collective-permute-done.16.refs_0_), channel_id=1, source_target_pairs={{0,1},{1,0},{2,3},{3,2},{4,5},{5,4},{6,7},{7,6},{8,9},{9,8},{10,11... | collective-permute-start | bytes 786440 | tf_op jit(solution)/shard_map/ppermute | solution.py:27
  44.7 27.0 %collective-permute-start.19 = (bf16[128,1024]{1,0:T(8,128)(2,1)S(1)}, bf16[128,1024]{1,0:T(8,128)(2,1)}, u32[]{:S(2)}, u32[]{:S(2)}) collective-permute-start(bf16[128,1024]{1,0:T(8,128)(2,1)S(1)} %collective-permute-done.18.refs_2_), channel_id=1, source_target_pairs={{0,1},{1,0},{2,3},{3,2},{4,5},{5,4},{6,7},{7,6},{8,9},{9,8},{10,11... | collective-permute-start | bytes 786440 | tf_op jit(solution)/shard_map/ppermute | solution.py:27
  59.7 20.2 %slice-start = ((s8[8388608]{0:T(1024)(128)(4,1)}), s8[4194304]{0:T(1024)(128)(4,1)S(1)}, s32[]{:S(2)}) async-start(s8[8388608]{0:T(1024)(128)(4,1)} %bitcast.14), calls=%async_computation | async-start | bytes 8388608
  59.7 20.2 %collective-permute-start = (bf16[128,1024]{1,0:T(8,128)(2,1)S(1)}, bf16[128,1024]{1,0:T(8,128)(2,1)S(1)}, u32[]{:S(2)}, u32[]{:S(2)}) collective-permute-start(bf16[128,1024]{1,0:T(8,128)(2,1)S(1)} %bitcast.19), channel_id=1, source_target_pairs={{0,1},{1,0},{2,3},{3,2},{4,5},{5,4},{6,7},{7,6},{8,9},{9,8},{10,11... | collective-permute-start | bytes 786440 | tf_op jit(solution)/shard_map/ppermute | solution.py:27
  60.3 19.6 %collective-permute-start.2 = (bf16[128,1024]{1,0:T(8,128)(2,1)S(1)}, bf16[128,1024]{1,0:T(8,128)(2,1)S(1)}, u32[]{:S(2)}, u32[]{:S(2)}) collective-permute-start(bf16[128,1024]{1,0:T(8,128)(2,1)S(1)} %collective-permute-done.1.refs_2_), channel_id=1, source_target_pairs={{0,1},{1,0},{2,3},{3,2},{4,5},{5,4},{6,7},{7,6},{8,9},{9,8},{10,11... | collective-permute-start | bytes 786440 | tf_op jit(solution)/shard_map/ppermute | solution.py:27
  60.3 27.0 %collective-permute-start.10 = (bf16[128,1024]{1,0:T(8,128)(2,1)S(1)}, bf16[128,1024]{1,0:T(8,128)(2,1)S(1)}, u32[]{:S(2)}, u32[]{:S(2)}) collective-permute-start(bf16[128,1024]{1,0:T(8,128)(2,1)S(1)} %visit_1.1), channel_id=1, source_target_pairs={{0,12},{4,0},{8,4},{12,8},{1,13},{5,1},{9,5},{13,9},{2,14},{6,2},{... | collective-permute-start | bytes 786440 | tf_op jit(solution)/shard_map/ppermute | solution.py:206
  71.5 8.3 %slice-start.1 = ((s8[8388608]{0:T(1024)(128)(4,1)}), s8[4194304]{0:T(1024)(128)(4,1)S(1)}, s32[]{:S(2)}) async-start(s8[8388608]{0:T(1024)(128)(4,1)} %bitcast.14), calls=%async_computation.1 | async-start | bytes 8388608
  71.6 18.4 %collective-permute-start.15 = (bf16[128,1024]{1,0:T(8,128)(2,1)S(1)}, bf16[128,1024]{1,0:T(8,128)(2,1)S(1)}, u32[]{:S(2)}, u32[]{:S(2)}) collective-permute-start(bf16[128,1024]{1,0:T(8,128)(2,1)S(1)} %visit_2.1), channel_id=1, source_target_pairs={{0,8},{4,12},{8,0},{12,4},{1,9},{5,13},{9,1},{13,5},{2,10},{6,14},... | collective-permute-start | bytes 786440 | tf_op jit(solution)/shard_map/ppermute | solution.py:206
  79.0 10.9 %collective-permute-start.20 = (bf16[128,1024]{1,0:T(8,128)(2,1)S(1)}, bf16[128,1024]{1,0:T(8,128)(2,1)S(1)}, u32[]{:S(2)}, u32[]{:S(2)}) collective-permute-start(bf16[128,1024]{1,0:T(8,128)(2,1)S(1)} %visit_3.1), channel_id=1, source_target_pairs={{0,4},{4,8},{8,12},{12,0},{1,5},{5,9},{9,13},{13,1},{2,6},{6,10},{... | collective-permute-start | bytes 786440 | tf_op jit(solution)/shard_map/ppermute | solution.py:206
  (8 other events, 10.4 us)

commit v2 on v1

v2 whole, which is shorter than its diff:
```python
import functools

import jax
import jax.numpy as jnp
import numpy as np
from jax import lax
from jax.experimental import pallas as pl
from jax.experimental.pallas import tpu as pltpu
from jax.sharding import PartitionSpec as P

QHEADS = 64
KVHEADS = 4
HD = 64
VISITS = 4
LANES = 128
VMEM_LIMIT = 16 * 1024 * 1024

EPSILON = 1e-05
ROPE_BASE = 500000.0
LOG2E = 1.4426950408889634


def visit_pairs(snaps, visit, back=False):
    if snaps == VISITS:
        return [(i, i ^ visit) for i in range(snaps)]
    return [(i, (i + (-visit if back else visit)) % snaps) for i in range(snaps)]


def visiting_block(snap, snaps, visit):
    if snaps == VISITS:
        return lax.bitwise_xor(snap, jnp.int32(visit))
    return lax.rem(snap + (snaps - visit), snaps)


def swapped(array, with_bits):
    count = lax.axis_size("tp")
    return lax.ppermute(array, "tp", [(i, i ^ with_bits) for i in range(count)])


def rope_tables(row_count):
    half = HD // 2
    positions = np.arange(row_count, dtype=np.float32)[:, None]
    frequency = np.float32(ROPE_BASE) ** (-np.arange(half, dtype=np.float32) * np.float32(2.0 / HD))
    angles = positions * frequency[None, :].astype(np.float32)
    cosine, sine = np.cos(angles), np.sin(angles)
    repeats = LANES // HD
    return (
        jnp.asarray(np.concatenate([cosine, cosine] * repeats, axis=1)),
        jnp.asarray(np.concatenate([-sine, sine] * repeats, axis=1)),
    )


def rotated(pair, cosine, signed_sine, in_first_half):
    half = HD // 2
    partner = jnp.where(
        in_first_half, pltpu.roll(pair, LANES - half, 1), pltpu.roll(pair, half, 1)
    )
    return pair * cosine + partner * signed_sine


def visit_kernel(parts, visits, *refs):
    held = 1 + parts // 2
    blocks = [refs[number * held : (number + 1) * held] for number in range(visits)]
    refs = refs[visits * held :]
    gain_ref, query_ref, keyval_ref, cosine_ref, sine_ref = refs[:5]
    biases = refs[5 : 5 + visits]
    outs = refs[5 + visits : -4]
    normed_ref, queries_ref, scores_ref, probabilities_ref = refs[-4:]
    rows, features = blocks[0][0].shape
    columns = query_ref.shape[2]
    width = parts * features
    step = 2 * LANES
    pairs = columns // LANES
    rank = lax.axis_index("tp")
    spans = [slice(number * rows, (number + 1) * rows) for number in range(visits)]

    for (own, beside, *chips), span in zip(blocks, spans):
        shards = [(own, 0, rank), (beside, 0, lax.bitwise_xor(rank, jnp.int32(1)))]
        for number, chip in enumerate(chips):
            first = lax.bitwise_xor(rank, jnp.int32(2 * (number + 1)))
            first = first - lax.rem(first, 2)
            shards += [(chip, 0, first), (chip, rows, first + 1)]
        squares = jnp.zeros((rows, 1), jnp.float32)
        for shard, start, _ in shards:
            values = shard[start : start + rows].astype(jnp.float32)
            squares += jnp.sum(values * values, axis=1, keepdims=True)
        scale = lax.rsqrt(squares / width + EPSILON)
        for shard, start, owner in shards:
            values = shard[start : start + rows].astype(jnp.float32)
            gain = gain_ref[:, pl.ds(pl.multiple_of(owner * features, LANES), features)]
            normed_ref[owner, span] = (values * scale * gain).astype(jnp.bfloat16)
    keyval = jnp.zeros((visits * rows, keyval_ref.shape[2]), jnp.float32)
    for part in range(parts):
        keyval += jnp.dot(normed_ref[part], keyval_ref[part], preferred_element_type=jnp.float32)

    cosine, sine = cosine_ref[...], sine_ref[...]
    lane = lax.broadcasted_iota(jnp.int32, (rows, LANES), 1)
    in_first_half = lax.rem(lane, HD) < HD // 2
    in_first_head = lane < HD
    all_keys, all_values = [], []
    for span in spans:
        mine = keyval[span].astype(jnp.bfloat16).astype(jnp.float32)
        keys = jnp.where(in_first_head, rotated(mine, cosine, sine, in_first_half), 0.0)
        all_keys.append(
            jnp.concatenate([keys, pltpu.roll(keys, HD, 1)], axis=0).astype(jnp.bfloat16)
        )
        values = jnp.where(in_first_head, 0.0, mine)
        values = jnp.concatenate([pltpu.roll(values, HD, 1), values], axis=0)
        all_values.append(values.T.astype(jnp.bfloat16))

    for start in range(0, columns, step):
        total = jnp.zeros((visits * rows, step), jnp.float32)
        for part in range(parts):
            total += jnp.dot(
                normed_ref[part],
                query_ref[part, :, start : start + step],
                preferred_element_type=jnp.float32,
            )
        for pair in range(0, step, LANES):
            for span in spans:
                queries_ref[span, start + pair : start + pair + LANES] = rotated(
                    total[span, pair : pair + LANES], cosine, sine, in_first_half
                ).astype(jnp.bfloat16)
    for number, span in enumerate(spans):
        for pair in range(pairs):
            scores_ref[number * pairs + pair] = lax.dot_general(
                all_keys[number],
                queries_ref[span, pair * LANES : (pair + 1) * LANES],
                (((1,), (1,)), ((), ())),
                preferred_element_type=jnp.float32,
            )
    for number in range(visits):
        for pair in range(number * pairs, (number + 1) * pairs):
            for head in range(2):
                mine = scores_ref[pair, head * rows : (head + 1) * rows] + biases[number][...]
                top = jnp.max(mine, axis=0, keepdims=True)
                weights = jnp.exp2((mine - top) * (LOG2E * HD**-0.5))
                whole = jnp.sum(weights, axis=0, keepdims=True)
                probabilities_ref[pair, head * rows : (head + 1) * rows] = (
                    weights * (1.0 / whole)
                ).astype(jnp.bfloat16)
    for number in range(visits):
        for pair in range(pairs):
            place = slice(pair * LANES, (pair + 1) * LANES)
            context = jnp.dot(
                all_values[number],
                probabilities_ref[number * pairs + pair],
                preferred_element_type=jnp.float32,
            )
            context = context.T.astype(jnp.bfloat16)
            outs[number][:, place] = context


def visit_contexts(blocks, biases, name, gain, query, keyval, cosine, sine):
    visits, parts = len(blocks), query.shape[0]
    rows, features = blocks[0][0].shape
    columns = query.shape[2]
    vmem = pl.BlockSpec(memory_space=pltpu.VMEM)
    operands = (
        *(shard for shards in blocks for shard in shards),
        gain,
        query,
        keyval,
        cosine,
        sine,
        *biases,
    )
    scores = (visits * columns // LANES, 2 * rows, rows)
    return pl.pallas_call(
        functools.partial(visit_kernel, parts, visits),
        out_shape=[pltpu.VMEM((rows, columns), jnp.bfloat16)] * visits,
        in_specs=[vmem] * len(operands),
        out_specs=[vmem] * visits,
        scratch_shapes=[
            pltpu.VMEM((parts, visits * rows, features), jnp.bfloat16),
            pltpu.VMEM((visits * rows, columns), jnp.bfloat16),
            pltpu.VMEM(scores, jnp.float32),
            pltpu.VMEM(scores, jnp.bfloat16),
        ],
        compiler_params=pltpu.CompilerParams(vmem_limit_bytes=VMEM_LIMIT),
        cost_estimate=pl.CostEstimate(flops=1, bytes_accessed=1, transcendentals=0),
        name=name,
    )(*operands)


def mean_kernel(keep_ref, *refs):
    terms, (out_any, out_ref, sems) = refs[:-3], refs[-3:]
    rows, _ = out_ref.shape
    strips = 2
    strip = rows // strips
    leaving = []
    for number in range(strips):
        place = pl.ds(number * strip, strip)
        total = terms[0][place].astype(jnp.float32)
        for term in terms[1:]:
            total += term[place].astype(jnp.float32)
        keep = keep_ref[place, :1] > 0.0
        out_ref[place] = jnp.where(keep, total / VISITS, 0.0).astype(jnp.bfloat16)
        leaving.append(
            pltpu.make_async_copy(out_ref.at[place], out_any.at[place], sems.at[number])
        )
        leaving[-1].start()
    for copy in leaving:
        copy.wait()


def mean_of(keep, terms):
    vmem = pl.BlockSpec(memory_space=pltpu.VMEM)
    operands = [pltpu.with_memory_space_constraint(term, pltpu.VMEM) for term in terms]
    return pl.pallas_call(
        mean_kernel,
        out_shape=jax.ShapeDtypeStruct(terms[0].shape, jnp.bfloat16),
        in_specs=[vmem] * (1 + len(operands)),
        out_specs=pl.BlockSpec(memory_space=pl.ANY),
        scratch_shapes=[
            pltpu.VMEM(terms[0].shape, jnp.bfloat16),
            pltpu.SemaphoreType.DMA((2,)),
        ],
        compiler_params=pltpu.CompilerParams(vmem_limit_bytes=VMEM_LIMIT),
        name="mean_of_visits",
    )(keep, *operands)


def stage_kernel(lengths_ref, query_any, gain_any, cosine_any, sine_any, *refs):
    query_ref, gain_ref, cosine_ref, sine_ref, keep_ref, token_ref, *biases = refs[:-1]
    sems = refs[-1]
    parts = query_ref.shape[0]
    moves = [(gain_any, gain_ref), (cosine_any, cosine_ref), (sine_any, sine_ref)]
    moves += [(query_any.at[part], query_ref.at[part]) for part in range(parts)]
    copies = [
        pltpu.make_async_copy(source, target, sems.at[number])
        for number, (source, target) in enumerate(moves)
    ]
    for copy in copies:
        copy.start()
    snap = lax.axis_index("snap")
    snaps = lax.axis_size("snap")
    rows = keep_ref.shape[0]
    token_ref[...] = jnp.zeros(token_ref.shape, token_ref.dtype)
    row = lax.broadcasted_iota(jnp.int32, keep_ref.shape, 0)
    keep_ref[...] = jnp.where(row < lengths_ref[snap], 1.0, 0.0)
    row = lax.broadcasted_iota(jnp.int32, (rows, rows), 1)
    key = lax.broadcasted_iota(jnp.int32, (rows, rows), 0)
    for visit, bias_ref in enumerate(biases):
        length = lengths_ref[visiting_block(snap, snaps, visit)]
        bias_ref[...] = jnp.where((key <= row) & (key < length), 0.0, -1e30)
    for copy in copies:
        copy.wait()


def staged(lengths, query, gain, cosine, sine, rows):
    hbm = pl.BlockSpec(memory_space=pltpu.HBM)
    vmem = pl.BlockSpec(memory_space=pltpu.VMEM)
    held = [(array.shape, array.dtype) for array in (query, gain, cosine, sine)]
    held += [((rows, LANES), jnp.float32)]
    biases = [((rows, rows), jnp.float32)] * VISITS
    return pl.pallas_call(
        stage_kernel,
        out_shape=[
            *(pltpu.VMEM(*each) for each in held),
            jax.ShapeDtypeStruct((8, LANES), jnp.float32),
            *(pltpu.VMEM(*each) for each in biases),
        ],
        in_specs=[pl.BlockSpec(memory_space=pltpu.SMEM)] + [hbm] * 4,
        out_specs=[vmem] * (len(held) + 1 + len(biases)),
        scratch_shapes=[pltpu.SemaphoreType.DMA((3 + query.shape[0],))],
        compiler_params=pltpu.CompilerParams(vmem_limit_bytes=VMEM_LIMIT),
        name="stage_weights",
    )(
        lengths,
        *(
            pltpu.with_memory_space_constraint(array, pltpu.HBM)
            for array in (query, gain, cosine, sine)
        ),
    )


def head_of(rank, heads_here):
    return (rank * heads_here) // (QHEADS // KVHEADS)


def cut_kernel(heads_here, keyval_ref, own_ref, beside_ref, *chip_refs):
    rank = lax.axis_index("tp")
    league = lax.axis_index("league")
    width = own_ref.shape[1]

    def columns(other):
        head = head_of(lax.bitwise_xor(rank, jnp.int32(other)), heads_here)
        return pl.ds(pl.multiple_of(head * width, LANES), width)

    own_ref[...] = keyval_ref[:, columns(0)]
    beside_ref[...] = keyval_ref[:, columns(1)]
    core = lax.rem(rank, 2)
    for number, chip_ref in enumerate(chip_refs):
        rows = chip_ref.shape[1]
        mine = pl.ds(pl.multiple_of(league * rows, 16), rows)
        for beside in range(2):
            chip_ref[lax.bitwise_xor(core, jnp.int32(beside))] = keyval_ref[
                mine, columns(2 * (number + 1) + beside)
            ]


def cut_keyval(keyval, heads_here, parts, leagues):
    features, width = keyval.shape[0], 2 * HD
    column = jax.ShapeDtypeStruct((features, width), keyval.dtype)
    chip = jax.ShapeDtypeStruct((2, features // leagues, width), keyval.dtype)
    chips = parts // 2 - 1
    vmem = pl.BlockSpec(memory_space=pltpu.VMEM)
    return pl.pallas_call(
        functools.partial(cut_kernel, heads_here),
        out_shape=[column, column] + [chip] * chips,
        in_specs=[vmem],
        out_specs=[vmem] * (2 + chips),
        compiler_params=pltpu.CompilerParams(vmem_limit_bytes=VMEM_LIMIT),
        name="cut_keyval",
    )(keyval)


def join_kernel(leagues, own_ref, beside_ref, *refs):
    pieces, out_ref, sems = refs[:-2], refs[-2], refs[-1]
    rank = lax.axis_index("tp")
    league = lax.axis_index("league")
    core = lax.rem(rank, 2)
    copies = [(own_ref, out_ref.at[rank]), (beside_ref, out_ref.at[lax.bitwise_xor(rank, 1)])]
    number = 0
    for chip in range(1, out_ref.shape[0] // 2):
        for beside in range(2):
            owner = lax.bitwise_xor(rank, jnp.int32(2 * chip + beside))
            for by in range(leagues):
                piece = pieces[number]
                rows = piece.shape[1]
                source = lax.rem(league + (leagues - by), leagues)
                place = pl.ds(pl.multiple_of(source * rows, 16), rows)
                copies.append((piece.at[core], out_ref.at[owner, place]))
                number += 1
    started = [
        pltpu.make_async_copy(source, target, sems.at[i])
        for i, (source, target) in enumerate(copies)
    ]
    for copy in started:
        copy.start()
    for copy in started:
        copy.wait()


def join_keyval(own, beside, pieces, parts, leagues):
    any_space = pl.BlockSpec(memory_space=pl.ANY)
    return pl.pallas_call(
        functools.partial(join_kernel, leagues),
        out_shape=pltpu.VMEM((parts, *own.shape), own.dtype),
        in_specs=[any_space] * (2 + len(pieces)),
        out_specs=pl.BlockSpec(memory_space=pltpu.VMEM),
        scratch_shapes=[pltpu.SemaphoreType.DMA((2 + len(pieces),))],
        compiler_params=pltpu.CompilerParams(vmem_limit_bytes=VMEM_LIMIT),
        name="join_keyval",
    )(own, beside, *pieces)


def kept_order(array, *earlier):
    return lax.optimization_barrier((array, *earlier))[0]


def on_device(block_states, lengths, norm_gain, query_weight, keyval_weight):
    snaps = lax.axis_size("snap")
    parts = lax.axis_size("tp")
    leagues = lax.axis_size("league")
    own = block_states[0]
    rows, features = own.shape
    query = query_weight[0].reshape(parts, features, query_weight.shape[2])
    heads_here = query.shape[2] // HD
    cosine, sine = rope_tables(rows)

    own_columns, beside_columns, *chip_columns = cut_keyval(
        keyval_weight[0], heads_here, parts, leagues
    )
    query_held, gain_held, cosine_held, sine_held, keep, token, *biases = staged(
        lengths, query, norm_gain, cosine, sine, rows
    )
    def moved(block, visit):
        return lax.ppermute(block, "snap", visit_pairs(snaps, visit))

    if snaps == VISITS:
        block_2 = moved(own, 2)
        block_1 = moved(own, 1)
        block_3 = moved(block_2, 1)
    else:
        block_1 = moved(own, 1)
        block_2 = moved(block_1, 1)
        block_3 = moved(block_2, 1)
    beside = swapped(beside_columns, 1)
    arrived = [swapped(columns, 2 * (i + 1)) for i, columns in enumerate(chip_columns)]
    pieces = []
    for columns in arrived:
        by_league = [kept_order(columns, token)]
        for _ in range(1, leagues):
            by_league.append(lax.ppermute(by_league[-1], "league", [(i, (i + 1) % leagues) for i in range(leagues)]))
        pieces += by_league + [swapped(piece, 1) for piece in by_league]
    keyval = join_keyval(own_columns, beside, pieces, parts, leagues)

    def over_chips(block):
        return [block] + [swapped(block, bits) for bits in range(2, parts, 2)]

    pairs_of_cores = [[i, i + 1] for i in range(0, parts, 2)]

    def over_cores(shards, *earlier):
        own_shard, *chips = shards
        gathered = [own_shard, swapped(own_shard, 1)]
        for shard in chips:
            shard = kept_order(shard, *earlier) if earlier else shard
            gathered.append(
                lax.all_gather(shard, "tp", axis=0, tiled=True, axis_index_groups=pairs_of_cores)
            )
        return gathered

    def scored(visits, blocks):
        return visit_contexts(
            blocks,
            [biases[visit] for visit in visits],
            "visit_" + "_".join(str(visit) for visit in visits),
            gain_held,
            query_held,
            keyval,
            cosine_held,
            sine_held,
        )

    def sent_home(visit, array):
        return lax.ppermute(array, "snap", visit_pairs(snaps, visit, back=True))

    shards_2 = over_chips(kept_order(block_2, token, *arrived))
    shards_3 = over_chips(kept_order(block_3, *shards_2[1:]))
    [context_2] = scored([2], [over_cores(shards_2)])
    shards_1 = over_chips(kept_order(block_1, context_2, *shards_3[1:]))
    shards_0 = over_chips(kept_order(own, *shards_1[1:]))
    home_2 = sent_home(2, context_2)
    [context_3] = scored([3], [over_cores(shards_3, context_2)])
    home_3 = sent_home(3, context_3)
    [context_1] = scored([1], [over_cores(shards_1, context_3)])
    home_1 = sent_home(1, context_1)
    [context_0] = scored([0], [over_cores(shards_0, context_1)])
    return mean_of(keep, [context_0, home_1, home_2, home_3])[None]


def solution(mesh):
    placed = (
        P(("league", "snap"), None, "tp"),
        P("league"),
        P("snap", None),
        P("snap", None, "tp"),
        P("snap", "tp", None),
    )
    return jax.shard_map(
        on_device,
        mesh=mesh,
        in_specs=placed,
        out_specs=P(("league", "snap"), None, "tp"),
        check_vma=False,
    )

NEWGAIN=1
```

time: 93.8 us -> 65 us (0.69)
  waiting for transfers between devices: 33.5 us -> 15.7 us
  Pallas kernels: 30 us -> 18.2 us
  blocking collectives: 0 us -> 8.99 us
  local copies, waits for them, and re-layouts: 10.3 us -> 1.88 us
  starting transfers between devices: 17.1 us -> 19.7 us
  other arithmetic: 2.33 us -> 0 us
    pallas_call x4 -> x7, Pallas kernels: 28 us -> 17.3 us  [the longest x4 11.7 us: visit_contexts(): pl.pallas_call(functools.partial(visit_kernel, parts, visits), out_shape=...]
    all_gather x0 -> x4, blocking collectives: none -> 8.99 us  [over_cores(): lax.all_gather(shard, 'tp', axis=0, tiled=True, axis_index_groups=pairs_o...]
    ppermute x15 -> x12, waiting for transfers between devices: 14.9 us -> 6 us  [swapped(): return lax.ppermute(array, 'tp', [(i, i ^ with_bits) for i in range(count)])]
    ppermute x6 -> x7, waiting for transfers between devices: 18.5 us -> 9.7 us  [the longest x3 5.26 us: moved(): return lax.ppermute(block, 'snap', visit_pairs(snaps, visit))]
    unnamed x23 -> x6, local copies, waits for them, and re-layouts: 8.28 us -> 1.88 us
    ppermute x6 -> x7, starting transfers between devices: 7.93 us -> 12 us  [the longest x3 5.26 us: sent_home(): return lax.ppermute(array, 'snap', visit_pairs(snaps, visit, back=True))]
    unnamed x2 -> x0, other arithmetic: 1.9 us -> none
    ppermute x15 -> x12, starting transfers between devices: 9.15 us -> 7.74 us  [swapped(): return lax.ppermute(array, 'tp', [(i, i ^ with_bits) for i in range(count)])]
  transfers between devices with their start and end apart: 21 -> 19, of which waited for: 8 -> 5; matrix products, arithmetic and copies ran while one was open for 5% -> 0% of each run, Pallas kernels for 30% -> 27%
where the time goes in v2:
time: 65 us; the launch traced here: 64.8 us
  starting transfers between devices  19.7 us (30%)
  Pallas kernels  18.2 us (28%)
  waiting for transfers between devices  15.7 us (24%)
  blocking collectives  8.99 us (14%)
  local copies, waits for them, and re-layouts  1.88 us (3%)
    pallas_call x4, Pallas kernels, visit_contexts(): pl.pallas_call(functools.partial(visit_kernel, parts, visits), out_shape=...  11.7 us
    all_gather x4, blocking collectives, over_cores(): lax.all_gather(shard, 'tp', axis=0, tiled=True, axis_index_groups=pairs_o...  8.99 us
    ppermute x12, starting transfers between devices, swapped(): return lax.ppermute(array, 'tp', [(i, i ^ with_bits) for i in range(count)])  7.74 us
    ppermute x12, waiting for transfers between devices, swapped(): return lax.ppermute(array, 'tp', [(i, i ^ with_bits) for i in range(count)])  6 us
    ppermute x3, waiting for transfers between devices, moved(): return lax.ppermute(block, 'snap', visit_pairs(snaps, visit))  5.26 us
    ppermute x3, starting transfers between devices, sent_home(): return lax.ppermute(array, 'snap', visit_pairs(snaps, visit, back=True))  5.26 us
    ppermute x3, starting transfers between devices, moved(): return lax.ppermute(block, 'snap', visit_pairs(snaps, visit))  5.16 us
    pallas_call x1, Pallas kernels, staged(): pl.pallas_call(stage_kernel, out_shape=[*(pltpu.VMEM(*each) for each in h...  4.74 us
  transfers between devices with their start and end apart: 19, of which 5 were waited for; matrix products, arithmetic and copies ran while one was open for 0% of the time, Pallas kernels for 27%

profile of v2, /device:TPU:0, one launch (start us, length us, event | category | flops | bytes accessed | tf_op | source)
XLA Modules:
  0.0 64.8 jit_solution(5523357591569959955)
XLA Ops:
  0.0 1.2 %copy-done = bf16[1,1024,512]{2,1,0:T(8,128)(2,1)S(1)} copy-done((bf16[1,1024,512]{2,1,0:T(8,128)(2,1)S(1)}, bf16[1,1024,512]{2,1,0:T(8,128)(2,1)}, u32[]{:S(2)}) %copy-start) | copy-done | bytes 1048600
  1.4 3.0 %collective-permute-start.2 = (bf16[2,512,128]{2,1,0:T(8,128)(2,1)S(1)}, bf16[2,512,128]{2,1,0:T(8,128)(2,1)S(1)}, u32[]{:S(2)}, u32[]{:S(2)}) collective-permute-start(bf16[2,512,128]{2,1,0:T(8,128)(2,1)S(1)} %get-tuple-element.28), channel_id=1, source_target_pairs={{0,2},{1,3},{2,0},{3,1},{4,6},{5,7},{6,4},{7,5},{8,10},{9,11},{10,... | collective-permute-start | bytes 786440 | tf_op jit(solution)/shard_map/ppermute | solution.py:37
  4.4 2.6 %collective-permute-start.1 = (bf16[128,1024]{1,0:T(8,128)(2,1)}, bf16[128,1024]{1,0:T(8,128)(2,1)S(1)}, u32[]{:S(2)}, u32[]{:S(2)}) collective-permute-start(bf16[128,1024]{1,0:T(8,128)(2,1)} %bitcast.5), channel_id=1, source_target_pairs={{0,8},{4,12},{8,0},{12,4},{1,9},{5,13},{9,1},{13,5},{2,10},{6,14},... | collective-permute-start | bytes 786440 | tf_op jit(solution)/shard_map/ppermute | solution.py:380
  7.6 4.7 %stage_weights.1 = (bf16[4,1024,1024]{2,1,0:T(8,128)(2,1)S(1)}, f32[1,4096]{1,0:T(1,128)S(1)}, f32[128,128]{1,0:T(8,128)S(1)}, f32[128,128]{1,0:T(8,128)S(1)}, f...) custom-call(s32[4]{0:T(128)S(1)} %copy-done.2, ...), custom_call_target="tpu_custom_call" | custom-call | tf_op jit(solution)/shard_map/stage_weights/pallas_call | solution.py:257
  12.4 1.6 %collective-permute-start.6 = (bf16[2,512,128]{2,1,0:T(8,128)(2,1)S(1)}, bf16[2,512,128]{2,1,0:T(8,128)(2,1)S(1)}, u32[]{:S(2)}, u32[]{:S(2)}) collective-permute-start(bf16[2,512,128]{2,1,0:T(8,128)(2,1)S(1)} %collective-permute-done.2.refs_0_), channel_id=1, source_target_pairs={{0,16},{16,0},{1,17},{17,1},{2,18},{18,2},{3,19},{19,3},{4,20},{20... | collective-permute-start | bytes 786440 | tf_op jit(solution)/shard_map/ppermute | solution.py:396
  14.0 4.9 %collective-permute-done.1.refs_0_ = bf16[128,1024]{1,0:T(8,128)(2,1)S(1)} collective-permute-done((bf16[128,1024]{1,0:T(8,128)(2,1)}, bf16[128,1024]{1,0:T(8,128)(2,1)S(1)}, u32[]{:S(2)}, u32[]{:S(2)}) %collective-permute-start.1) | collective-permute-done | bytes 262176 | tf_op jit(solution)/shard_map/ppermute | solution.py:380
  19.4 0.8 %collective-permute-start.9 = (bf16[128,1024]{1,0:T(8,128)(2,1)S(1)}, bf16[128,1024]{1,0:T(8,128)(2,1)S(1)}, u32[]{:S(2)}, u32[]{:S(2)}) collective-permute-start(bf16[128,1024]{1,0:T(8,128)(2,1)S(1)} %collective-permute-done.1.refs_0_), channel_id=1, source_target_pairs={{0,4},{4,0},{8,12},{12,8},{1,5},{5,1},{9,13},{13,9},{2,6},{6,2},{1... | collective-permute-start | bytes 786440 | tf_op jit(solution)/shard_map/ppermute | solution.py:380
  20.7 5.3 %collective-permute-done.4 = bf16[128,1024]{1,0:T(8,128)(2,1)S(1)} collective-permute-done((bf16[128,1024]{1,0:T(8,128)(2,1)S(1)}, bf16[128,1024]{1,0:T(8,128)(2,1)S(1)}, u32[]{:S(2)}, u32[]{:S(2)}) %collective-permute-start.4) | collective-permute-done | bytes 262176 | tf_op jit(solution)/shard_map/ppermute | solution.py:37
  26.4 1.7 %collective-permute-start = (bf16[128,1024]{1,0:T(8,128)(2,1)S(1)}, bf16[128,1024]{1,0:T(8,128)(2,1)S(1)}, u32[]{:S(2)}, u32[]{:S(2)}) collective-permute-start(bf16[128,1024]{1,0:T(8,128)(2,1)S(1)} %bitcast.6), channel_id=1, source_target_pairs={{0,4},{4,0},{8,12},{12,8},{1,5},{5,1},{9,13},{13,9},{2,6},{6,2},{1... | collective-permute-start | bytes 786440 | tf_op jit(solution)/shard_map/ppermute | solution.py:380
  28.1 1.5 %collective-permute-start.10 = (bf16[128,1024]{1,0:T(8,128)(2,1)S(1)}, bf16[128,1024]{1,0:T(8,128)(2,1)S(1)}, u32[]{:S(2)}, u32[]{:S(2)}) collective-permute-start(bf16[128,1024]{1,0:T(8,128)(2,1)S(1)} %collective-permute-done.9.refs_0_), channel_id=1, source_target_pairs={{0,2},{1,3},{2,0},{3,1},{4,6},{5,7},{6,4},{7,5},{8,10},{9,11},{10,... | collective-permute-start | bytes 786440 | tf_op jit(solution)/shard_map/ppermute | solution.py:37
  29.6 2.2 %all_gather.12.refs_2_ = bf16[256,1024]{1,0:T(8,128)(2,1)S(1)} all-gather(bf16[128,1024]{1,0:T(8,128)(2,1)S(1)} %collective-permute-done.4), channel_id=1, replica_groups={{0,1},{2,3},{4,5},{6,7},{8,9},{10,11},{12,13},{14,15},{16,17},{18,19},{..., dimensions={0}, use_global_device_ids=true | all-gather | bytes 786432 | tf_op jit(solution)/shard_map/all_gather | solution.py:411
  32.7 2.9 %visit_2.1 = bf16[128,1024]{1,0:T(8,128)(2,1)S(1)} custom-call(bf16[128,1024]{1,0:T(8,128)(2,1)S(1)} %collective-permute-done.1.refs_0_, bf16[128,1024]{1,0:T(8,128)(2,1)S(1)} %collective-permute-done.3.refs_1_, bf16[256,1024]{1,0:T(8,128)(2,1)S(1)} %all_gather.12.refs_2_, f32[1,4096]{1,0:T(1,128)S(1)} %get-tuple-element.30.refs_3_, ...), custom_call_target="tpu_custom_call" | custom-call | flops 1 | bytes 1 | tf_op jit(solution)/shard_map/visit_2/pallas_call | solution.py:169
  36.9 3.3 %collective-permute-start.17 = (bf16[128,1024]{1,0:T(8,128)(2,1)S(1)}, bf16[128,1024]{1,0:T(8,128)(2,1)S(1)}, u32[]{:S(2)}, u32[]{:S(2)}) collective-permute-start(bf16[128,1024]{1,0:T(8,128)(2,1)S(1)} %visit_2.1), channel_id=1, source_target_pairs={{0,8},{4,12},{8,0},{12,4},{1,9},{5,13},{9,1},{13,5},{2,10},{6,14},... | collective-permute-start | bytes 786440 | tf_op jit(solution)/shard_map/ppermute | solution.py:428
  40.1 2.2 %all_gather.13.refs_2_ = bf16[256,1024]{1,0:T(8,128)(2,1)S(1)} all-gather(bf16[128,1024]{1,0:T(8,128)(2,1)S(1)} %collective-permute-done.10), channel_id=1, replica_groups={{0,1},{2,3},{4,5},{6,7},{8,9},{10,11},{12,13},{14,15},{16,17},{18,19},{..., dimensions={0}, use_global_device_ids=true | all-gather | bytes 786432 | tf_op jit(solution)/shard_map/all_gather | solution.py:411
  42.3 2.9 %visit_3.1 = bf16[128,1024]{1,0:T(8,128)(2,1)S(1)} custom-call(bf16[128,1024]{1,0:T(8,128)(2,1)S(1)} %collective-permute-done.9.refs_0_, bf16[128,1024]{1,0:T(8,128)(2,1)S(1)} %collective-permute-done.15.refs_1_, bf16[256,1024]{1,0:T(8,128)(2,1)S(1)} %all_gather.13.refs_2_, f32[1,4096]{1,0:T(1,128)S(1)} %get-tuple-element.30.refs_3_, ...), custom_call_target="tpu_custom_call" | custom-call | flops 1 | bytes 1 | tf_op jit(solution)/shard_map/visit_3/pallas_call | solution.py:169
  45.2 1.6 %collective-permute-start.13 = (bf16[128,1024]{1,0:T(8,128)(2,1)S(1)}, bf16[128,1024]{1,0:T(8,128)(2,1)S(1)}, u32[]{:S(2)}, u32[]{:S(2)}) collective-permute-start(bf16[128,1024]{1,0:T(8,128)(2,1)S(1)} %bitcast.7), channel_id=1, source_target_pairs={{0,2},{1,3},{2,0},{3,1},{4,6},{5,7},{6,4},{7,5},{8,10},{9,11},{10,... | collective-permute-start | bytes 786440 | tf_op jit(solution)/shard_map/ppermute | solution.py:37
  46.8 1.1 %collective-permute-start.18 = (bf16[128,1024]{1,0:T(8,128)(2,1)S(1)}, bf16[128,1024]{1,0:T(8,128)(2,1)S(1)}, u32[]{:S(2)}, u32[]{:S(2)}) collective-permute-start(bf16[128,1024]{1,0:T(8,128)(2,1)S(1)} %visit_3.1), channel_id=1, source_target_pairs={{0,12},{4,8},{8,4},{12,0},{1,13},{5,9},{9,5},{13,1},{2,14},{6,10},... | collective-permute-start | bytes 786440 | tf_op jit(solution)/shard_map/ppermute | solution.py:428
  47.9 2.3 %all_gather.14.refs_2_ = bf16[256,1024]{1,0:T(8,128)(2,1)S(1)} all-gather(bf16[128,1024]{1,0:T(8,128)(2,1)S(1)} %collective-permute-done.11), channel_id=1, replica_groups={{0,1},{2,3},{4,5},{6,7},{8,9},{10,11},{12,13},{14,15},{16,17},{18,19},{..., dimensions={0}, use_global_device_ids=true | all-gather | bytes 786432 | tf_op jit(solution)/shard_map/all_gather | solution.py:411
  50.2 2.9 %visit_1.1 = bf16[128,1024]{1,0:T(8,128)(2,1)S(1)} custom-call(bf16[128,1024]{1,0:T(8,128)(2,1)S(1)} %collective-permute-done.refs_0_, bf16[128,1024]{1,0:T(8,128)(2,1)S(1)} %collective-permute-done.14.refs_1_, bf16[256,1024]{1,0:T(8,128)(2,1)S(1)} %all_gather.14.refs_2_, f32[1,4096]{1,0:T(1,128)S(1)} %get-tuple-element.30.refs_3_, ...), custom_call_target="tpu_custom_call" | custom-call | flops 1 | bytes 1 | tf_op jit(solution)/shard_map/visit_1/pallas_call | solution.py:169
  53.1 0.9 %collective-permute-start.16 = (bf16[128,1024]{1,0:T(8,128)(2,1)S(1)}, bf16[128,1024]{1,0:T(8,128)(2,1)S(1)}, u32[]{:S(2)}, u32[]{:S(2)}) collective-permute-start(bf16[128,1024]{1,0:T(8,128)(2,1)S(1)} %visit_1.1), channel_id=1, source_target_pairs={{0,4},{4,0},{8,12},{12,8},{1,5},{5,1},{9,13},{13,9},{2,6},{6,2},{1... | collective-permute-start | bytes 786440 | tf_op jit(solution)/shard_map/ppermute | solution.py:428
  54.0 2.4 %all_gather.15.refs_2_ = bf16[256,1024]{1,0:T(8,128)(2,1)S(1)} all-gather(bf16[128,1024]{1,0:T(8,128)(2,1)S(1)} %collective-permute-done.13), channel_id=1, replica_groups={{0,1},{2,3},{4,5},{6,7},{8,9},{10,11},{12,13},{14,15},{16,17},{18,19},{..., dimensions={0}, use_global_device_ids=true | all-gather | bytes 786432 | tf_op jit(solution)/shard_map/all_gather | solution.py:411
  56.4 2.9 %visit_0.1.refs_0_ = bf16[128,1024]{1,0:T(8,128)(2,1)S(1)} custom-call(bf16[128,1024]{1,0:T(8,128)(2,1)S(1)} %bitcast.9, bf16[128,1024]{1,0:T(8,128)(2,1)S(1)} %collective-permute-done.12.refs_1_, bf16[256,1024]{1,0:T(8,128)(2,1)S(1)} %all_gather.15.refs_2_, f32[1,4096]{1,0:T(1,128)S(1)} %get-tuple-element.30.refs_3_, ...), custom_call_target="tpu_custom_call" | custom-call | flops 1 | bytes 1 | tf_op jit(solution)/shard_map/visit_0/pallas_call | solution.py:169
  59.3 4.4 %collective-permute-done.16.refs_1_ = bf16[128,1024]{1,0:T(8,128)(2,1)S(1)} collective-permute-done((bf16[128,1024]{1,0:T(8,128)(2,1)S(1)}, bf16[128,1024]{1,0:T(8,128)(2,1)S(1)}, u32[]{:S(2)}, u32[]{:S(2)}) %collective-permute-start.16) | collective-permute-done | bytes 262176 | tf_op jit(solution)/shard_map/ppermute | solution.py:428
  63.8 0.8 %mean_of_visits.1 = bf16[128,1024]{1,0:T(8,128)(2,1)} custom-call(f32[128,128]{1,0:T(8,128)S(1)} %get-tuple-element.26.keep_ref, bf16[128,1024]{1,0:T(8,128)(2,1)S(1)} %visit_0.1.refs_0_, bf16[128,1024]{1,0:T(8,128)(2,1)S(1)} %collective-permute-done.16.refs_1_, bf16[128,1024]{1,0:T(8,128)(2,1)S(1)} %collective-permute-done.17.refs_2_, ...), custom_call_target="tpu_custom_call" | custom-call | tf_op jit(solution)/shard_map/mean_of_visits/pallas_call | solution.py:210
  (32 shorter events, 4.3 us)
Async XLA Ops:
  0.0 1.2 %copy-start = (bf16[1,1024,512]{2,1,0:T(8,128)(2,1)S(1)}, bf16[1,1024,512]{2,1,0:T(8,128)(2,1)}, u32[]{:S(2)}) copy-start(bf16[1,1024,512]{2,1,0:T(8,128)(2,1)} %param.11) | copy-start | bytes 3145732
  1.2 25.2 %copy-start.1 = (bf16[1,128,1024]{2,1,0:T(8,128)(2,1)S(1)}, bf16[1,128,1024]{2,1,0:T(8,128)(2,1)}, u32[]{:S(2)}) copy-start(bf16[1,128,1024]{2,1,0:T(8,128)(2,1)} %param.7) | copy-start | bytes 786436
  1.4 11.0 %collective-permute-start.2 = (bf16[2,512,128]{2,1,0:T(8,128)(2,1)S(1)}, bf16[2,512,128]{2,1,0:T(8,128)(2,1)S(1)}, u32[]{:S(2)}, u32[]{:S(2)}) collective-permute-start(bf16[2,512,128]{2,1,0:T(8,128)(2,1)S(1)} %get-tuple-element.28), channel_id=1, source_target_pairs={{0,2},{1,3},{2,0},{3,1},{4,6},{5,7},{6,4},{7,5},{8,10},{9,11},{10,... | collective-permute-start | bytes 786440 | tf_op jit(solution)/shard_map/ppermute | solution.py:37
  4.4 14.5 %collective-permute-start.1 = (bf16[128,1024]{1,0:T(8,128)(2,1)}, bf16[128,1024]{1,0:T(8,128)(2,1)S(1)}, u32[]{:S(2)}, u32[]{:S(2)}) collective-permute-start(bf16[128,1024]{1,0:T(8,128)(2,1)} %bitcast.5), channel_id=1, source_target_pairs={{0,8},{4,12},{8,0},{12,4},{1,9},{5,13},{9,1},{13,5},{2,10},{6,14},... | collective-permute-start | bytes 786440 | tf_op jit(solution)/shard_map/ppermute | solution.py:380
  7.0 0.7 %copy-start.2 = (s32[4]{0:T(128)S(1)}, s32[4]{0:T(128)}, u32[]{:S(2)}) copy-start(s32[4]{0:T(128)} %lengths_ref.1) | copy-start | bytes 52
  12.4 8.3 %collective-permute-start.6 = (bf16[2,512,128]{2,1,0:T(8,128)(2,1)S(1)}, bf16[2,512,128]{2,1,0:T(8,128)(2,1)S(1)}, u32[]{:S(2)}, u32[]{:S(2)}) collective-permute-start(bf16[2,512,128]{2,1,0:T(8,128)(2,1)S(1)} %collective-permute-done.2.refs_0_), channel_id=1, source_target_pairs={{0,16},{16,0},{1,17},{17,1},{2,18},{18,2},{3,19},{19,3},{4,20},{20... | collective-permute-start | bytes 786440 | tf_op jit(solution)/shard_map/ppermute | solution.py:396
  18.9 7.2 %collective-permute-start.4 = (bf16[128,1024]{1,0:T(8,128)(2,1)S(1)}, bf16[128,1024]{1,0:T(8,128)(2,1)S(1)}, u32[]{:S(2)}, u32[]{:S(2)}) collective-permute-start(bf16[128,1024]{1,0:T(8,128)(2,1)S(1)} %collective-permute-done.1.refs_0_), channel_id=1, source_target_pairs={{0,2},{1,3},{2,0},{3,1},{4,6},{5,7},{6,4},{7,5},{8,10},{9,11},{10,... | collective-permute-start | bytes 786440 | tf_op jit(solution)/shard_map/ppermute | solution.py:37
  19.4 7.0 %collective-permute-start.9 = (bf16[128,1024]{1,0:T(8,128)(2,1)S(1)}, bf16[128,1024]{1,0:T(8,128)(2,1)S(1)}, u32[]{:S(2)}, u32[]{:S(2)}) collective-permute-start(bf16[128,1024]{1,0:T(8,128)(2,1)S(1)} %collective-permute-done.1.refs_0_), channel_id=1, source_target_pairs={{0,4},{4,0},{8,12},{12,8},{1,5},{5,1},{9,13},{13,9},{2,6},{6,2},{1... | collective-permute-start | bytes 786440 | tf_op jit(solution)/shard_map/ppermute | solution.py:380
  20.2 8.0 %collective-permute-start.5 = (bf16[1024,128]{1,0:T(8,128)(2,1)S(1)}, bf16[1024,128]{1,0:T(8,128)(2,1)S(1)}, u32[]{:S(2)}, u32[]{:S(2)}) collective-permute-start(bf16[1024,128]{1,0:T(8,128)(2,1)S(1)} %get-tuple-element.33), channel_id=1, source_target_pairs={{0,1},{1,0},{2,3},{3,2},{4,5},{5,4},{6,7},{7,6},{8,9},{9,8},{10,11... | collective-permute-start | bytes 786440 | tf_op jit(solution)/shard_map/ppermute | solution.py:37
  20.2 11.6 %collective-permute-start.7 = (bf16[2,512,128]{2,1,0:T(8,128)(2,1)S(1)}, bf16[2,512,128]{2,1,0:T(8,128)(2,1)S(1)}, u32[]{:S(2)}, u32[]{:S(2)}) collective-permute-start(bf16[2,512,128]{2,1,0:T(8,128)(2,1)S(1)} %collective-permute-done.2.refs_0_), channel_id=1, source_target_pairs={{0,1},{1,0},{2,3},{3,2},{4,5},{5,4},{6,7},{7,6},{8,9},{9,8},{10,11... | collective-permute-start | bytes 786440 | tf_op jit(solution)/shard_map/ppermute | solution.py:37
  20.7 11.2 %collective-permute-start.8 = (bf16[2,512,128]{2,1,0:T(8,128)(2,1)S(1)}, bf16[2,512,128]{2,1,0:T(8,128)(2,1)S(1)}, u32[]{:S(2)}, u32[]{:S(2)}) collective-permute-start(bf16[2,512,128]{2,1,0:T(8,128)(2,1)S(1)} %collective-permute-done.6.refs_1_), channel_id=1, source_target_pairs={{0,1},{1,0},{2,3},{3,2},{4,5},{5,4},{6,7},{7,6},{8,9},{9,8},{10,11... | collective-permute-start | bytes 786440 | tf_op jit(solution)/shard_map/ppermute | solution.py:37
  26.0 6.7 %collective-permute-start.3 = (bf16[128,1024]{1,0:T(8,128)(2,1)S(1)}, bf16[128,1024]{1,0:T(8,128)(2,1)S(1)}, u32[]{:S(2)}, u32[]{:S(2)}) collective-permute-start(bf16[128,1024]{1,0:T(8,128)(2,1)S(1)} %collective-permute-done.1.refs_0_), channel_id=1, source_target_pairs={{0,1},{1,0},{2,3},{3,2},{4,5},{5,4},{6,7},{7,6},{8,9},{9,8},{10,11... | collective-permute-start | bytes 786440 | tf_op jit(solution)/shard_map/ppermute | solution.py:37
  26.4 9.3 %collective-permute-start = (bf16[128,1024]{1,0:T(8,128)(2,1)S(1)}, bf16[128,1024]{1,0:T(8,128)(2,1)S(1)}, u32[]{:S(2)}, u32[]{:S(2)}) collective-permute-start(bf16[128,1024]{1,0:T(8,128)(2,1)S(1)} %bitcast.6), channel_id=1, source_target_pairs={{0,4},{4,0},{8,12},{12,8},{1,5},{5,1},{9,13},{13,9},{2,6},{6,2},{1... | collective-permute-start | bytes 786440 | tf_op jit(solution)/shard_map/ppermute | solution.py:380
  28.1 8.2 %collective-permute-start.10 = (bf16[128,1024]{1,0:T(8,128)(2,1)S(1)}, bf16[128,1024]{1,0:T(8,128)(2,1)S(1)}, u32[]{:S(2)}, u32[]{:S(2)}) collective-permute-start(bf16[128,1024]{1,0:T(8,128)(2,1)S(1)} %collective-permute-done.9.refs_0_), channel_id=1, source_target_pairs={{0,2},{1,3},{2,0},{3,1},{4,6},{5,7},{6,4},{7,5},{8,10},{9,11},{10,... | collective-permute-start | bytes 786440 | tf_op jit(solution)/shard_map/ppermute | solution.py:37
  31.8 10.5 %collective-permute-start.15 = (bf16[128,1024]{1,0:T(8,128)(2,1)S(1)}, bf16[128,1024]{1,0:T(8,128)(2,1)S(1)}, u32[]{:S(2)}, u32[]{:S(2)}) collective-permute-start(bf16[128,1024]{1,0:T(8,128)(2,1)S(1)} %collective-permute-done.9.refs_0_), channel_id=1, source_target_pairs={{0,1},{1,0},{2,3},{3,2},{4,5},{5,4},{6,7},{7,6},{8,9},{9,8},{10,11... | collective-permute-start | bytes 786440 | tf_op jit(solution)/shard_map/ppermute | solution.py:37
  36.3 8.9 %collective-permute-start.11 = (bf16[128,1024]{1,0:T(8,128)(2,1)S(1)}, bf16[128,1024]{1,0:T(8,128)(2,1)S(1)}, u32[]{:S(2)}, u32[]{:S(2)}) collective-permute-start(bf16[128,1024]{1,0:T(8,128)(2,1)S(1)} %collective-permute-done.refs_0_), channel_id=1, source_target_pairs={{0,2},{1,3},{2,0},{3,1},{4,6},{5,7},{6,4},{7,5},{8,10},{9,11},{10,... | collective-permute-start | bytes 786440 | tf_op jit(solution)/shard_map/ppermute | solution.py:37
  36.9 13.3 %collective-permute-start.14 = (bf16[128,1024]{1,0:T(8,128)(2,1)S(1)}, bf16[128,1024]{1,0:T(8,128)(2,1)S(1)}, u32[]{:S(2)}, u32[]{:S(2)}) collective-permute-start(bf16[128,1024]{1,0:T(8,128)(2,1)S(1)} %collective-permute-done.refs_0_), channel_id=1, source_target_pairs={{0,1},{1,0},{2,3},{3,2},{4,5},{5,4},{6,7},{7,6},{8,9},{9,8},{10,11... | collective-permute-start | bytes 786440 | tf_op jit(solution)/shard_map/ppermute | solution.py:37
  36.9 22.5 %collective-permute-start.17 = (bf16[128,1024]{1,0:T(8,128)(2,1)S(1)}, bf16[128,1024]{1,0:T(8,128)(2,1)S(1)}, u32[]{:S(2)}, u32[]{:S(2)}) collective-permute-start(bf16[128,1024]{1,0:T(8,128)(2,1)S(1)} %visit_2.1), channel_id=1, source_target_pairs={{0,8},{4,12},{8,0},{12,4},{1,9},{5,13},{9,1},{13,5},{2,10},{6,14},... | collective-permute-start | bytes 786440 | tf_op jit(solution)/shard_map/ppermute | solution.py:428
  45.2 8.8 %collective-permute-start.13 = (bf16[128,1024]{1,0:T(8,128)(2,1)S(1)}, bf16[128,1024]{1,0:T(8,128)(2,1)S(1)}, u32[]{:S(2)}, u32[]{:S(2)}) collective-permute-start(bf16[128,1024]{1,0:T(8,128)(2,1)S(1)} %bitcast.7), channel_id=1, source_target_pairs={{0,2},{1,3},{2,0},{3,1},{4,6},{5,7},{6,4},{7,5},{8,10},{9,11},{10,... | collective-permute-start | bytes 786440 | tf_op jit(solution)/shard_map/ppermute | solution.py:37
  46.8 12.5 %collective-permute-start.18 = (bf16[128,1024]{1,0:T(8,128)(2,1)S(1)}, bf16[128,1024]{1,0:T(8,128)(2,1)S(1)}, u32[]{:S(2)}, u32[]{:S(2)}) collective-permute-start(bf16[128,1024]{1,0:T(8,128)(2,1)S(1)} %visit_3.1), channel_id=1, source_target_pairs={{0,12},{4,8},{8,4},{12,0},{1,13},{5,9},{9,5},{13,1},{2,14},{6,10},... | collective-permute-start | bytes 786440 | tf_op jit(solution)/shard_map/ppermute | solution.py:428
  47.9 8.5 %collective-permute-start.12 = (bf16[128,1024]{1,0:T(8,128)(2,1)S(1)}, bf16[128,1024]{1,0:T(8,128)(2,1)S(1)}, u32[]{:S(2)}, u32[]{:S(2)}) collective-permute-start(bf16[128,1024]{1,0:T(8,128)(2,1)S(1)} %bitcast.8), channel_id=1, source_target_pairs={{0,1},{1,0},{2,3},{3,2},{4,5},{5,4},{6,7},{7,6},{8,9},{9,8},{10,11... | collective-permute-start | bytes 786440 | tf_op jit(solution)/shard_map/ppermute | solution.py:37
  53.1 10.7 %collective-permute-start.16 = (bf16[128,1024]{1,0:T(8,128)(2,1)S(1)}, bf16[128,1024]{1,0:T(8,128)(2,1)S(1)}, u32[]{:S(2)}, u32[]{:S(2)}) collective-permute-start(bf16[128,1024]{1,0:T(8,128)(2,1)S(1)} %visit_1.1), channel_id=1, source_target_pairs={{0,4},{4,0},{8,12},{12,8},{1,5},{5,1},{9,13},{13,9},{2,6},{6,2},{1... | collective-permute-start | bytes 786440 | tf_op jit(solution)/shard_map/ppermute | solution.py:428

commit v3 on v2

--- a/solution.py
+++ b/solution.py
@@ -58,38 +58,37 @@
     return pair * cosine + partner * signed_sine
 
 
-def visit_kernel(parts, visits, *refs):
-    held = 1 + parts // 2
-    blocks = [refs[number * held : (number + 1) * held] for number in range(visits)]
-    refs = refs[visits * held :]
-    gain_ref, query_ref, keyval_ref, cosine_ref, sine_ref = refs[:5]
-    biases = refs[5 : 5 + visits]
-    outs = refs[5 + visits : -4]
-    normed_ref, queries_ref, scores_ref, probabilities_ref = refs[-4:]
-    rows, features = blocks[0][0].shape
+def visit_kernel(parts, held, *refs):
+    (own, beside, *chips), refs = refs[:held], refs[held:]
+    gain_ref, query_ref, keyval_ref, cosine_ref, sine_ref, bias_ref = refs[:6]
+    out_ref, normed_ref, queries_ref, scores_ref, probabilities_ref = refs[6:]
+    rows, features = own.shape
     columns = query_ref.shape[2]
     width = parts * features
     step = 2 * LANES
     pairs = columns // LANES
     rank = lax.axis_index("tp")
-    spans = [slice(number * rows, (number + 1) * rows) for number in range(visits)]
-
-    for (own, beside, *chips), span in zip(blocks, spans):
-        shards = [(own, 0, rank), (beside, 0, lax.bitwise_xor(rank, jnp.int32(1)))]
+
+    shards = [(own, 0, rank), (beside, 0, lax.bitwise_xor(rank, jnp.int32(1)))]
+    if held == parts:
+        for bits, shard in enumerate(chips, 2):
+            shards.append((shard, 0, lax.bitwise_xor(rank, jnp.int32(bits))))
+    else:
         for number, chip in enumerate(chips):
             first = lax.bitwise_xor(rank, jnp.int32(2 * (number + 1)))
             first = first - lax.rem(first, 2)
             shards += [(chip, 0, first), (chip, rows, first + 1)]
-        squares = jnp.zeros((rows, 1), jnp.float32)
-        for shard, start, _ in shards:
-            values = shard[start : start + rows].astype(jnp.float32)
-            squares += jnp.sum(values * values, axis=1, keepdims=True)
-        scale = lax.rsqrt(squares / width + EPSILON)
-        for shard, start, owner in shards:
-            values = shard[start : start + rows].astype(jnp.float32)
-            gain = gain_ref[:, pl.ds(pl.multiple_of(owner * features, LANES), features)]
-            normed_ref[owner, span] = (values * scale * gain).astype(jnp.bfloat16)
-    keyval = jnp.zeros((visits * rows, keyval_ref.shape[2]), jnp.float32)
+
+    squares = jnp.zeros((rows, 1), jnp.float32)
+    for shard, start, _ in shards:
+        values = shard[start : start + rows].astype(jnp.float32)
+        squares += jnp.sum(values * values, axis=1, keepdims=True)
+    scale = lax.rsqrt(squares / width + EPSILON)
+    for shard, start, owner in shards:
+        values = shard[start : start + rows].astype(jnp.float32)
+        gain = gain_ref[:, pl.ds(pl.multiple_of(owner * features, LANES), features)]
+        normed_ref[owner] = (values * scale * gain).astype(jnp.bfloat16)
+    keyval = jnp.zeros((rows, keyval_ref.shape[2]), jnp.float32)
     for part in range(parts):
         keyval += jnp.dot(normed_ref[part], keyval_ref[part], preferred_element_type=jnp.float32)
 
@@ -97,19 +96,14 @@
     lane = lax.broadcasted_iota(jnp.int32, (rows, LANES), 1)
     in_first_half = lax.rem(lane, HD) < HD // 2
     in_first_head = lane < HD
-    all_keys, all_values = [], []
-    for span in spans:
-        mine = keyval[span].astype(jnp.bfloat16).astype(jnp.float32)
-        keys = jnp.where(in_first_head, rotated(mine, cosine, sine, in_first_half), 0.0)
-        all_keys.append(
-            jnp.concatenate([keys, pltpu.roll(keys, HD, 1)], axis=0).astype(jnp.bfloat16)
-        )
-        values = jnp.where(in_first_head, 0.0, mine)
-        values = jnp.concatenate([pltpu.roll(values, HD, 1), values], axis=0)
-        all_values.append(values.T.astype(jnp.bfloat16))
+    keyval = keyval.astype(jnp.bfloat16).astype(jnp.float32)
+    keys = jnp.where(in_first_head, rotated(keyval, cosine, sine, in_first_half), 0.0)
+    keys = jnp.concatenate([keys, pltpu.roll(keys, HD, 1)], axis=0).astype(jnp.bfloat16)
+    values = jnp.where(in_first_head, 0.0, keyval)
+    values = jnp.concatenate([pltpu.roll(values, HD, 1), values], axis=0).T.astype(jnp.bfloat16)
 
     for start in range(0, columns, step):
-        total = jnp.zeros((visits * rows, step), jnp.float32)
+        total = jnp.zeros((rows, step), jnp.float32)
         for part in range(parts):
             total += jnp.dot(
                 normed_ref[part],
@@ -117,69 +111,49 @@
                 preferred_element_type=jnp.float32,
             )
         for pair in range(0, step, LANES):
-            for span in spans:
-                queries_ref[span, start + pair : start + pair + LANES] = rotated(
-                    total[span, pair : pair + LANES], cosine, sine, in_first_half
-                ).astype(jnp.bfloat16)
-    for number, span in enumerate(spans):
-        for pair in range(pairs):
-            scores_ref[number * pairs + pair] = lax.dot_general(
-                all_keys[number],
-                queries_ref[span, pair * LANES : (pair + 1) * LANES],
-                (((1,), (1,)), ((), ())),
-                preferred_element_type=jnp.float32,
-            )
-    for number in range(visits):
-        for pair in range(number * pairs, (number + 1) * pairs):
-            for head in range(2):
-                mine = scores_ref[pair, head * rows : (head + 1) * rows] + biases[number][...]
-                top = jnp.max(mine, axis=0, keepdims=True)
-                weights = jnp.exp2((mine - top) * (LOG2E * HD**-0.5))
-                whole = jnp.sum(weights, axis=0, keepdims=True)
-                probabilities_ref[pair, head * rows : (head + 1) * rows] = (
-                    weights * (1.0 / whole)
-                ).astype(jnp.bfloat16)
-    for number in range(visits):
-        for pair in range(pairs):
-            place = slice(pair * LANES, (pair + 1) * LANES)
-            context = jnp.dot(
-                all_values[number],
-                probabilities_ref[number * pairs + pair],
-                preferred_element_type=jnp.float32,
-            )
-            context = context.T.astype(jnp.bfloat16)
-            outs[number][:, place] = context
-
-
-def visit_contexts(blocks, biases, name, gain, query, keyval, cosine, sine):
-    visits, parts = len(blocks), query.shape[0]
-    rows, features = blocks[0][0].shape
-    columns = query.shape[2]
+            queries_ref[:, start + pair : start + pair + LANES] = rotated(
+                total[:, pair : pair + LANES], cosine, sine, in_first_half
+            ).astype(jnp.bfloat16)
+    for pair in range(pairs):
+        scores_ref[pair] = lax.dot_general(
+            keys,
+            queries_ref[:, pair * LANES : (pair + 1) * LANES],
+            (((1,), (1,)), ((), ())),
+            preferred_element_type=jnp.float32,
+        )
+    for pair in range(pairs):
+        for head in range(2):
+            place = slice(head * rows, (head + 1) * rows)
+            mine = scores_ref[pair, place] + bias_ref[...]
+            top = jnp.max(mine, axis=0, keepdims=True)
+            weights = jnp.exp2((mine - top) * (LOG2E * HD**-0.5))
+            whole = jnp.sum(weights, axis=0, keepdims=True)
+            probabilities_ref[pair, place] = (weights * (1.0 / whole)).astype(jnp.bfloat16)
+    for pair in range(pairs):
+        context = jnp.dot(values, probabilities_ref[pair], preferred_element_type=jnp.float32)
+        out_ref[:, pair * LANES : (pair + 1) * LANES] = context.T.astype(jnp.bfloat16)
+
+
+def visit_context(visit, shards, gain, query, keyval, cosine, sine, bias):
+    parts, features, columns = query.shape
+    rows = shards[0].shape[0]
     vmem = pl.BlockSpec(memory_space=pltpu.VMEM)
-    operands = (
-        *(shard for shards in blocks for shard in shards),
-        gain,
-        query,
-        keyval,
-        cosine,
-        sine,
-        *biases,
-    )
-    scores = (visits * columns // LANES, 2 * rows, rows)
+    operands = (*shards, gain, query, keyval, cosine, sine, bias)
+    scores = (columns // LANES, 2 * rows, rows)
     return pl.pallas_call(
-        functools.partial(visit_kernel, parts, visits),
-        out_shape=[pltpu.VMEM((rows, columns), jnp.bfloat16)] * visits,
+        functools.partial(visit_kernel, parts, len(shards)),
+        out_shape=pltpu.VMEM((rows, columns), jnp.bfloat16),
         in_specs=[vmem] * len(operands),
-        out_specs=[vmem] * visits,
+        out_specs=vmem,
         scratch_shapes=[
-            pltpu.VMEM((parts, visits * rows, features), jnp.bfloat16),
-            pltpu.VMEM((visits * rows, columns), jnp.bfloat16),
+            pltpu.VMEM((parts, rows, features), jnp.bfloat16),
+            pltpu.VMEM((rows, columns), jnp.bfloat16),
             pltpu.VMEM(scores, jnp.float32),
             pltpu.VMEM(scores, jnp.bfloat16),
         ],
         compiler_params=pltpu.CompilerParams(vmem_limit_bytes=VMEM_LIMIT),
         cost_estimate=pl.CostEstimate(flops=1, bytes_accessed=1, transcendentals=0),
-        name=name,
+        name=f"visit_{visit}",
     )(*operands)
 
 
@@ -391,7 +365,7 @@
     arrived = [swapped(columns, 2 * (i + 1)) for i, columns in enumerate(chip_columns)]
     pieces = []
     for columns in arrived:
-        by_league = [kept_order(columns, token)]
+        by_league = [kept_order(columns, token, block_2)]
         for _ in range(1, leagues):
             by_league.append(lax.ppermute(by_league[-1], "league", [(i, (i + 1) % leagues) for i in range(leagues)]))
         pieces += by_league + [swapped(piece, 1) for piece in by_league]
@@ -402,26 +376,22 @@
 
     pairs_of_cores = [[i, i + 1] for i in range(0, parts, 2)]
 
-    def over_cores(shards, *earlier):
+    def over_cores(shards, *earlier, apart=False):
         own_shard, *chips = shards
         gathered = [own_shard, swapped(own_shard, 1)]
         for shard in chips:
             shard = kept_order(shard, *earlier) if earlier else shard
-            gathered.append(
-                lax.all_gather(shard, "tp", axis=0, tiled=True, axis_index_groups=pairs_of_cores)
-            )
+            if apart:
+                gathered += [shard, swapped(shard, 1)]
+            else:
+                gathered.append(
+                    lax.all_gather(shard, "tp", axis=0, tiled=True, axis_index_groups=pairs_of_cores)
+                )
         return gathered
 
-    def scored(visits, blocks):
-        return visit_contexts(
-            blocks,
-            [biases[visit] for visit in visits],
-            "visit_" + "_".join(str(visit) for visit in visits),
-            gain_held,
-            query_held,
-            keyval,
-            cosine_held,
-            sine_held,
+    def scored(visit, shards):
+        return visit_context(
+            visit, shards, gain_held, query_held, keyval, cosine_held, sine_held, biases[visit]
         )
 
     def sent_home(visit, array):
@@ -429,15 +399,15 @@
 
     shards_2 = over_chips(kept_order(block_2, token, *arrived))
     shards_3 = over_chips(kept_order(block_3, *shards_2[1:]))
-    [context_2] = scored([2], [over_cores(shards_2)])
-    shards_1 = over_chips(kept_order(block_1, context_2, *shards_3[1:]))
+    context_2 = scored(2, over_cores(shards_2, block_1, apart=True))
+    home_2 = sent_home(2, context_2)
+    shards_1 = over_chips(kept_order(block_1, context_2))
     shards_0 = over_chips(kept_order(own, *shards_1[1:]))
-    home_2 = sent_home(2, context_2)
-    [context_3] = scored([3], [over_cores(shards_3, context_2)])
+    context_3 = scored(3, over_cores(shards_3, context_2))
     home_3 = sent_home(3, context_3)
-    [context_1] = scored([1], [over_cores(shards_1, context_3)])
+    context_1 = scored(1, over_cores(shards_1, context_3))
     home_1 = sent_home(1, context_1)
-    [context_0] = scored([0], [over_cores(shards_0, context_1)])
+    context_0 = scored(0, over_cores(shards_0, context_1))
     return mean_of(keep, [context_0, home_1, home_2, home_3])[None]
 
 
@@ -456,5 +426,3 @@
         out_specs=P(("league", "snap"), None, "tp"),
         check_vma=False,
     )
-
-NEWGAIN=1

time: 65 us -> 60.5 us (0.931)
  waiting for transfers between devices: 15.7 us -> 11.1 us
  starting transfers between devices: 19.7 us -> 22 us
  blocking collectives: 8.99 us -> 6.84 us
    ppermute x12 -> x13, waiting for transfers between devices: 6 us -> 1.02 us  [swapped(): return lax.ppermute(array, 'tp', [(i, i ^ with_bits) for i in range(count)])]
    ppermute x1, waiting for transfers between devices: 0.01 us -> 3.14 us  [on_device(): lax.ppermute(by_league[-1], 'league', [(i, (i + 1) % leagues) for i in ra...]
    ppermute x3, starting transfers between devices: 5.26 us -> 7.62 us  [sent_home(): return lax.ppermute(array, 'snap', visit_pairs(snaps, visit, back=True))]
    all_gather x4 -> x3, blocking collectives: 8.99 us -> 6.84 us  [over_cores(): lax.all_gather(shard, 'tp', axis=0, tiled=True, axis_index_groups=pairs_o...]
    ppermute x3, waiting for transfers between devices: 5.26 us -> 3.61 us  [moved(): return lax.ppermute(block, 'snap', visit_pairs(snaps, visit))]
    ppermute x12 -> x13, starting transfers between devices: 7.74 us -> 6.5 us  [swapped(): return lax.ppermute(array, 'tp', [(i, i ^ with_bits) for i in range(count)])]
    ppermute x3, starting transfers between devices: 5.16 us -> 6.33 us  [moved(): return lax.ppermute(block, 'snap', visit_pairs(snaps, visit))]
    ppermute x3, waiting for transfers between devices: 4.43 us -> 3.33 us  [sent_home(): return lax.ppermute(array, 'snap', visit_pairs(snaps, visit, back=True))]
  transfers between devices with their start and end apart: 19 -> 20, of which waited for: 5 -> 5; matrix products, arithmetic and copies ran while one was open for 0% -> 0% of each run, Pallas kernels for 27% -> 29%
where the time goes in v3:
time: 60.5 us; the launch traced here: 60.3 us
  starting transfers between devices  22 us (36%)
  Pallas kernels  18.2 us (30%)
  waiting for transfers between devices  11.1 us (18%)
  blocking collectives  6.84 us (11%)
  local copies, waits for them, and re-layouts  1.89 us (3%)
    pallas_call x4, Pallas kernels, visit_context(): pl.pallas_call(functools.partial(visit_kernel, parts, len(shards)), out_s...  11.7 us
    ppermute x3, starting transfers between devices, sent_home(): return lax.ppermute(array, 'snap', visit_pairs(snaps, visit, back=True))  7.62 us
    all_gather x3, blocking collectives, over_cores(): lax.all_gather(shard, 'tp', axis=0, tiled=True, axis_index_groups=pairs_o...  6.84 us
    ppermute x13, starting transfers between devices, swapped(): return lax.ppermute(array, 'tp', [(i, i ^ with_bits) for i in range(count)])  6.5 us
    ppermute x3, starting transfers between devices, moved(): return lax.ppermute(block, 'snap', visit_pairs(snaps, visit))  6.33 us
    pallas_call x1, Pallas kernels, staged(): pl.pallas_call(stage_kernel, out_shape=[*(pltpu.VMEM(*each) for each in h...  4.74 us
    ppermute x3, waiting for transfers between devices, moved(): return lax.ppermute(block, 'snap', visit_pairs(snaps, visit))  3.61 us
    ppermute x3, waiting for transfers between devices, sent_home(): return lax.ppermute(array, 'snap', visit_pairs(snaps, visit, back=True))  3.33 us
  transfers between devices with their start and end apart: 20, of which 5 were waited for; matrix products, arithmetic and copies ran while one was open for 0% of the time, Pallas kernels for 29%

profile of v3, /device:TPU:0, one launch (start us, length us, event | category | flops | bytes accessed | tf_op | source)
XLA Modules:
  0.0 60.3 jit_solution(7112081557598001648)
XLA Ops:
  0.0 4.0 %collective-permute-start.1 = (bf16[128,1024]{1,0:T(8,128)(2,1)}, bf16[128,1024]{1,0:T(8,128)(2,1)S(1)}, u32[]{:S(2)}, u32[]{:S(2)}) collective-permute-start(bf16[128,1024]{1,0:T(8,128)(2,1)} %bitcast.5), channel_id=1, source_target_pairs={{0,8},{4,12},{8,0},{12,4},{1,9},{5,13},{9,1},{13,5},{2,10},{6,14},... | collective-permute-start | bytes 786440 | tf_op jit(solution)/shard_map/ppermute | solution.py:354
  4.0 1.2 %copy-done = bf16[1,1024,512]{2,1,0:T(8,128)(2,1)S(1)} copy-done((bf16[1,1024,512]{2,1,0:T(8,128)(2,1)S(1)}, bf16[1,1024,512]{2,1,0:T(8,128)(2,1)}, u32[]{:S(2)}) %copy-start) | copy-done | bytes 1048600
  5.4 1.6 %collective-permute-start.2 = (bf16[2,512,128]{2,1,0:T(8,128)(2,1)S(1)}, bf16[2,512,128]{2,1,0:T(8,128)(2,1)S(1)}, u32[]{:S(2)}, u32[]{:S(2)}) collective-permute-start(bf16[2,512,128]{2,1,0:T(8,128)(2,1)S(1)} %get-tuple-element.29), channel_id=1, source_target_pairs={{0,2},{1,3},{2,0},{3,1},{4,6},{5,7},{6,4},{7,5},{8,10},{9,11},{10,... | collective-permute-start | bytes 786440 | tf_op jit(solution)/shard_map/ppermute | solution.py:37
  7.0 1.6 %collective-permute-start = (bf16[128,1024]{1,0:T(8,128)(2,1)}, bf16[128,1024]{1,0:T(8,128)(2,1)S(1)}, u32[]{:S(2)}, u32[]{:S(2)}) collective-permute-start(bf16[128,1024]{1,0:T(8,128)(2,1)} %bitcast.6), channel_id=1, source_target_pairs={{0,4},{4,0},{8,12},{12,8},{1,5},{5,1},{9,13},{13,9},{2,6},{6,2},{1... | collective-permute-start | bytes 786440 | tf_op jit(solution)/shard_map/ppermute | solution.py:354
  9.2 4.7 %stage_weights.1 = (bf16[4,1024,1024]{2,1,0:T(8,128)(2,1)S(1)}, f32[1,4096]{1,0:T(1,128)S(1)}, f32[128,128]{1,0:T(8,128)S(1)}, f32[128,128]{1,0:T(8,128)S(1)}, f...) custom-call(s32[4]{0:T(128)S(1)} %copy-done.2, ...), custom_call_target="tpu_custom_call" | custom-call | tf_op jit(solution)/shard_map/stage_weights/pallas_call | solution.py:231
  13.9 2.3 %collective-permute-done.1.refs_0_ = bf16[128,1024]{1,0:T(8,128)(2,1)S(1)} collective-permute-done((bf16[128,1024]{1,0:T(8,128)(2,1)}, bf16[128,1024]{1,0:T(8,128)(2,1)S(1)}, u32[]{:S(2)}, u32[]{:S(2)}) %collective-permute-start.1) | collective-permute-done | bytes 262176 | tf_op jit(solution)/shard_map/ppermute | solution.py:354
  16.3 1.6 %collective-permute-start.7 = (bf16[2,512,128]{2,1,0:T(8,128)(2,1)S(1)}, bf16[2,512,128]{2,1,0:T(8,128)(2,1)S(1)}, u32[]{:S(2)}, u32[]{:S(2)}) collective-permute-start(bf16[2,512,128]{2,1,0:T(8,128)(2,1)S(1)} %collective-permute-done.2.refs_0_), channel_id=1, source_target_pairs={{0,16},{16,0},{1,17},{17,1},{2,18},{18,2},{3,19},{19,3},{4,20},{20... | collective-permute-start | bytes 786440 | tf_op jit(solution)/shard_map/ppermute | solution.py:370
  17.9 1.5 %collective-permute-start.4 = (bf16[128,1024]{1,0:T(8,128)(2,1)S(1)}, bf16[128,1024]{1,0:T(8,128)(2,1)S(1)}, u32[]{:S(2)}, u32[]{:S(2)}) collective-permute-start(bf16[128,1024]{1,0:T(8,128)(2,1)S(1)} %collective-permute-done.1.refs_0_), channel_id=1, source_target_pairs={{0,2},{1,3},{2,0},{3,1},{4,6},{5,7},{6,4},{7,5},{8,10},{9,11},{10,... | collective-permute-start | bytes 786440 | tf_op jit(solution)/shard_map/ppermute | solution.py:37
  20.6 3.1 %collective-permute-done.7.refs_1_ = bf16[2,512,128]{2,1,0:T(8,128)(2,1)S(1)} collective-permute-done((bf16[2,512,128]{2,1,0:T(8,128)(2,1)S(1)}, bf16[2,512,128]{2,1,0:T(8,128)(2,1)S(1)}, u32[]{:S(2)}, u32[]{:S(2)}) %collective-permute-start.7) | collective-permute-done | bytes 262176 | tf_op jit(solution)/shard_map/ppermute | solution.py:370
  23.7 1.0 %collective-permute-done.4.refs_2_ = bf16[128,1024]{1,0:T(8,128)(2,1)S(1)} collective-permute-done((bf16[128,1024]{1,0:T(8,128)(2,1)S(1)}, bf16[128,1024]{1,0:T(8,128)(2,1)S(1)}, u32[]{:S(2)}, u32[]{:S(2)}) %collective-permute-start.4) | collective-permute-done | bytes 262176 | tf_op jit(solution)/shard_map/ppermute | solution.py:37
  24.7 1.3 %collective-permute-done.14.refs_0_ = bf16[128,1024]{1,0:T(8,128)(2,1)S(1)} collective-permute-done((bf16[128,1024]{1,0:T(8,128)(2,1)S(1)}, bf16[128,1024]{1,0:T(8,128)(2,1)S(1)}, u32[]{:S(2)}, u32[]{:S(2)}) %collective-permute-start.14) | collective-permute-done | bytes 262176 | tf_op jit(solution)/shard_map/ppermute | solution.py:354
  26.8 0.8 %join_keyval.1.refs_6_.refs_5_ = bf16[4,1024,128]{2,1,0:T(8,128)(2,1)S(1)} custom-call(bf16[1024,128]{1,0:T(8,128)(2,1)S(1)} %get-tuple-element.34.own_ref, bf16[1024,128]{1,0:T(8,128)(2,1)S(1)} %collective-permute-done.6.beside_ref, bf16[2,512,128]{2,1,0:T(8,128)(2,1)S(1)} %collective-permute-done.2.refs_0_, ...), custom_call_target="tpu_custom_call" | custom-call | tf_op jit(solution)/shard_map/join_keyval/pallas_call | solution.py:322
  27.6 2.9 %visit_2.1 = bf16[128,1024]{1,0:T(8,128)(2,1)S(1)} custom-call(bf16[128,1024]{1,0:T(8,128)(2,1)S(1)} %collective-permute-done.1.refs_0_, bf16[128,1024]{1,0:T(8,128)(2,1)S(1)} %collective-permute-done.3.refs_1_, bf16[128,1024]{1,0:T(8,128)(2,1)S(1)} %collective-permute-done.4.refs_2_, bf16[128,1024]{1,0:T(8,128)(2,1)S(1)} %collective-permute-done.5.refs_3_, ...), custom_call_target="tpu_custom_call" | custom-call | flops 1 | bytes 1 | tf_op jit(solution)/shard_map/visit_2/pallas_call | solution.py:143
  30.5 1.6 %collective-permute-start.10 = (bf16[128,1024]{1,0:T(8,128)(2,1)S(1)}, bf16[128,1024]{1,0:T(8,128)(2,1)S(1)}, u32[]{:S(2)}, u32[]{:S(2)}) collective-permute-start(bf16[128,1024]{1,0:T(8,128)(2,1)S(1)} %collective-permute-done.refs_0_), channel_id=1, source_target_pairs={{0,2},{1,3},{2,0},{3,1},{4,6},{5,7},{6,4},{7,5},{8,10},{9,11},{10,... | collective-permute-start | bytes 786440 | tf_op jit(solution)/shard_map/ppermute | solution.py:37
  32.1 3.3 %collective-permute-start.18 = (bf16[128,1024]{1,0:T(8,128)(2,1)S(1)}, bf16[128,1024]{1,0:T(8,128)(2,1)S(1)}, u32[]{:S(2)}, u32[]{:S(2)}) collective-permute-start(bf16[128,1024]{1,0:T(8,128)(2,1)S(1)} %visit_2.1), channel_id=1, source_target_pairs={{0,8},{4,12},{8,0},{12,4},{1,9},{5,13},{9,1},{13,5},{2,10},{6,14},... | collective-permute-start | bytes 786440 | tf_op jit(solution)/shard_map/ppermute | solution.py:398
  35.3 2.2 %all_gather.9.refs_2_ = bf16[256,1024]{1,0:T(8,128)(2,1)S(1)} all-gather(bf16[128,1024]{1,0:T(8,128)(2,1)S(1)} %collective-permute-done.16), channel_id=1, replica_groups={{0,1},{2,3},{4,5},{6,7},{8,9},{10,11},{12,13},{14,15},{16,17},{18,19},{..., dimensions={0}, use_global_device_ids=true | all-gather | bytes 786432 | tf_op jit(solution)/shard_map/all_gather | solution.py:388
  37.5 2.9 %visit_3.1 = bf16[128,1024]{1,0:T(8,128)(2,1)S(1)} custom-call(bf16[128,1024]{1,0:T(8,128)(2,1)S(1)} %collective-permute-done.14.refs_0_, bf16[128,1024]{1,0:T(8,128)(2,1)S(1)} %collective-permute-done.15.refs_1_, bf16[256,1024]{1,0:T(8,128)(2,1)S(1)} %all_gather.9.refs_2_, f32[1,4096]{1,0:T(1,128)S(1)} %get-tuple-element.32.refs_4_.refs_3_, ...), custom_call_target="tpu_custom_call" | custom-call | flops 1 | bytes 1 | tf_op jit(solution)/shard_map/visit_3/pallas_call | solution.py:143
  41.1 4.3 %collective-permute-start.19 = (bf16[128,1024]{1,0:T(8,128)(2,1)S(1)}, bf16[128,1024]{1,0:T(8,128)(2,1)S(1)}, u32[]{:S(2)}, u32[]{:S(2)}) collective-permute-start(bf16[128,1024]{1,0:T(8,128)(2,1)S(1)} %visit_3.1), channel_id=1, source_target_pairs={{0,12},{4,8},{8,4},{12,0},{1,13},{5,9},{9,5},{13,1},{2,14},{6,10},... | collective-permute-start | bytes 786440 | tf_op jit(solution)/shard_map/ppermute | solution.py:398
  45.3 2.3 %all_gather.10.refs_2_ = bf16[256,1024]{1,0:T(8,128)(2,1)S(1)} all-gather(bf16[128,1024]{1,0:T(8,128)(2,1)S(1)} %collective-permute-done.10), channel_id=1, replica_groups={{0,1},{2,3},{4,5},{6,7},{8,9},{10,11},{12,13},{14,15},{16,17},{18,19},{..., dimensions={0}, use_global_device_ids=true | all-gather | bytes 786432 | tf_op jit(solution)/shard_map/all_gather | solution.py:388
  47.6 2.9 %visit_1.1 = bf16[128,1024]{1,0:T(8,128)(2,1)S(1)} custom-call(bf16[128,1024]{1,0:T(8,128)(2,1)S(1)} %collective-permute-done.refs_0_, bf16[128,1024]{1,0:T(8,128)(2,1)S(1)} %collective-permute-done.13.refs_1_, bf16[256,1024]{1,0:T(8,128)(2,1)S(1)} %all_gather.10.refs_2_, f32[1,4096]{1,0:T(1,128)S(1)} %get-tuple-element.32.refs_4_.refs_3_, ...), custom_call_target="tpu_custom_call" | custom-call | flops 1 | bytes 1 | tf_op jit(solution)/shard_map/visit_1/pallas_call | solution.py:143
  50.6 2.4 %all_gather.11.refs_2_ = bf16[256,1024]{1,0:T(8,128)(2,1)S(1)} all-gather(bf16[128,1024]{1,0:T(8,128)(2,1)S(1)} %collective-permute-done.12), channel_id=1, replica_groups={{0,1},{2,3},{4,5},{6,7},{8,9},{10,11},{12,13},{14,15},{16,17},{18,19},{..., dimensions={0}, use_global_device_ids=true | all-gather | bytes 786432 | tf_op jit(solution)/shard_map/all_gather | solution.py:388
  53.0 2.9 %visit_0.1.refs_0_ = bf16[128,1024]{1,0:T(8,128)(2,1)S(1)} custom-call(bf16[128,1024]{1,0:T(8,128)(2,1)S(1)} %bitcast.9, bf16[128,1024]{1,0:T(8,128)(2,1)S(1)} %collective-permute-done.11.refs_1_, bf16[256,1024]{1,0:T(8,128)(2,1)S(1)} %all_gather.11.refs_2_, f32[1,4096]{1,0:T(1,128)S(1)} %get-tuple-element.32.refs_4_.refs_3_, ...), custom_call_target="tpu_custom_call" | custom-call | flops 1 | bytes 1 | tf_op jit(solution)/shard_map/visit_0/pallas_call | solution.py:143
  56.0 3.3 %collective-permute-done.17.refs_1_ = bf16[128,1024]{1,0:T(8,128)(2,1)S(1)} collective-permute-done((bf16[128,1024]{1,0:T(8,128)(2,1)S(1)}, bf16[128,1024]{1,0:T(8,128)(2,1)S(1)}, u32[]{:S(2)}, u32[]{:S(2)}) %collective-permute-start.17) | collective-permute-done | bytes 262176 | tf_op jit(solution)/shard_map/ppermute | solution.py:398
  59.3 0.8 %mean_of_visits.1 = bf16[128,1024]{1,0:T(8,128)(2,1)} custom-call(f32[128,128]{1,0:T(8,128)S(1)} %get-tuple-element.27.keep_ref, bf16[128,1024]{1,0:T(8,128)(2,1)S(1)} %visit_0.1.refs_0_, bf16[128,1024]{1,0:T(8,128)(2,1)S(1)} %collective-permute-done.17.refs_1_, bf16[128,1024]{1,0:T(8,128)(2,1)S(1)} %collective-permute-done.18.refs_2_, ...), custom_call_target="tpu_custom_call" | custom-call | tf_op jit(solution)/shard_map/mean_of_visits/pallas_call | solution.py:184
  (33 shorter events, 3.5 us)
Async XLA Ops:
  0.0 16.3 %collective-permute-start.1 = (bf16[128,1024]{1,0:T(8,128)(2,1)}, bf16[128,1024]{1,0:T(8,128)(2,1)S(1)}, u32[]{:S(2)}, u32[]{:S(2)}) collective-permute-start(bf16[128,1024]{1,0:T(8,128)(2,1)} %bitcast.5), channel_id=1, source_target_pairs={{0,8},{4,12},{8,0},{12,4},{1,9},{5,13},{9,1},{13,5},{2,10},{6,14},... | collective-permute-start | bytes 786440 | tf_op jit(solution)/shard_map/ppermute | solution.py:354
  4.0 1.2 %copy-start = (bf16[1,1024,512]{2,1,0:T(8,128)(2,1)S(1)}, bf16[1,1024,512]{2,1,0:T(8,128)(2,1)}, u32[]{:S(2)}) copy-start(bf16[1,1024,512]{2,1,0:T(8,128)(2,1)} %param.11) | copy-start | bytes 3145732
  5.4 10.9 %collective-permute-start.2 = (bf16[2,512,128]{2,1,0:T(8,128)(2,1)S(1)}, bf16[2,512,128]{2,1,0:T(8,128)(2,1)S(1)}, u32[]{:S(2)}, u32[]{:S(2)}) collective-permute-start(bf16[2,512,128]{2,1,0:T(8,128)(2,1)S(1)} %get-tuple-element.29), channel_id=1, source_target_pairs={{0,2},{1,3},{2,0},{3,1},{4,6},{5,7},{6,4},{7,5},{8,10},{9,11},{10,... | collective-permute-start | bytes 786440 | tf_op jit(solution)/shard_map/ppermute | solution.py:37
  7.0 13.1 %collective-permute-start = (bf16[128,1024]{1,0:T(8,128)(2,1)}, bf16[128,1024]{1,0:T(8,128)(2,1)S(1)}, u32[]{:S(2)}, u32[]{:S(2)}) collective-permute-start(bf16[128,1024]{1,0:T(8,128)(2,1)} %bitcast.6), channel_id=1, source_target_pairs={{0,4},{4,0},{8,12},{12,8},{1,5},{5,1},{9,13},{13,9},{2,6},{6,2},{1... | collective-permute-start | bytes 786440 | tf_op jit(solution)/shard_map/ppermute | solution.py:354
  8.5 0.7 %copy-start.2 = (s32[4]{0:T(128)S(1)}, s32[4]{0:T(128)}, u32[]{:S(2)}) copy-start(s32[4]{0:T(128)} %lengths_ref.1) | copy-start | bytes 52
  16.3 7.4 %collective-permute-start.7 = (bf16[2,512,128]{2,1,0:T(8,128)(2,1)S(1)}, bf16[2,512,128]{2,1,0:T(8,128)(2,1)S(1)}, u32[]{:S(2)}, u32[]{:S(2)}) collective-permute-start(bf16[2,512,128]{2,1,0:T(8,128)(2,1)S(1)} %collective-permute-done.2.refs_0_), channel_id=1, source_target_pairs={{0,16},{16,0},{1,17},{17,1},{2,18},{18,2},{3,19},{19,3},{4,20},{20... | collective-permute-start | bytes 786440 | tf_op jit(solution)/shard_map/ppermute | solution.py:370
  17.9 6.9 %collective-permute-start.4 = (bf16[128,1024]{1,0:T(8,128)(2,1)S(1)}, bf16[128,1024]{1,0:T(8,128)(2,1)S(1)}, u32[]{:S(2)}, u32[]{:S(2)}) collective-permute-start(bf16[128,1024]{1,0:T(8,128)(2,1)S(1)} %collective-permute-done.1.refs_0_), channel_id=1, source_target_pairs={{0,2},{1,3},{2,0},{3,1},{4,6},{5,7},{6,4},{7,5},{8,10},{9,11},{10,... | collective-permute-start | bytes 786440 | tf_op jit(solution)/shard_map/ppermute | solution.py:37
  19.3 6.6 %collective-permute-start.14 = (bf16[128,1024]{1,0:T(8,128)(2,1)S(1)}, bf16[128,1024]{1,0:T(8,128)(2,1)S(1)}, u32[]{:S(2)}, u32[]{:S(2)}) collective-permute-start(bf16[128,1024]{1,0:T(8,128)(2,1)S(1)} %collective-permute-done.1.refs_0_), channel_id=1, source_target_pairs={{0,4},{4,0},{8,12},{12,8},{1,5},{5,1},{9,13},{13,9},{2,6},{6,2},{1... | collective-permute-start | bytes 786440 | tf_op jit(solution)/shard_map/ppermute | solution.py:354
  20.1 5.9 %collective-permute-start.6 = (bf16[1024,128]{1,0:T(8,128)(2,1)S(1)}, bf16[1024,128]{1,0:T(8,128)(2,1)S(1)}, u32[]{:S(2)}, u32[]{:S(2)}) collective-permute-start(bf16[1024,128]{1,0:T(8,128)(2,1)S(1)} %get-tuple-element.35), channel_id=1, source_target_pairs={{0,1},{1,0},{2,3},{3,2},{4,5},{5,4},{6,7},{7,6},{8,9},{9,8},{10,11... | collective-permute-start | bytes 786440 | tf_op jit(solution)/shard_map/ppermute | solution.py:37
  20.1 6.7 %collective-permute-start.8 = (bf16[2,512,128]{2,1,0:T(8,128)(2,1)S(1)}, bf16[2,512,128]{2,1,0:T(8,128)(2,1)S(1)}, u32[]{:S(2)}, u32[]{:S(2)}) collective-permute-start(bf16[2,512,128]{2,1,0:T(8,128)(2,1)S(1)} %collective-permute-done.2.refs_0_), channel_id=1, source_target_pairs={{0,1},{1,0},{2,3},{3,2},{4,5},{5,4},{6,7},{7,6},{8,9},{9,8},{10,11... | collective-permute-start | bytes 786440 | tf_op jit(solution)/shard_map/ppermute | solution.py:37
  23.7 3.8 %collective-permute-start.3 = (bf16[128,1024]{1,0:T(8,128)(2,1)S(1)}, bf16[128,1024]{1,0:T(8,128)(2,1)S(1)}, u32[]{:S(2)}, u32[]{:S(2)}) collective-permute-start(bf16[128,1024]{1,0:T(8,128)(2,1)S(1)} %collective-permute-done.1.refs_0_), channel_id=1, source_target_pairs={{0,1},{1,0},{2,3},{3,2},{4,5},{5,4},{6,7},{7,6},{8,9},{9,8},{10,11... | collective-permute-start | bytes 786440 | tf_op jit(solution)/shard_map/ppermute | solution.py:37
  24.7 2.1 %collective-permute-start.9 = (bf16[2,512,128]{2,1,0:T(8,128)(2,1)S(1)}, bf16[2,512,128]{2,1,0:T(8,128)(2,1)S(1)}, u32[]{:S(2)}, u32[]{:S(2)}) collective-permute-start(bf16[2,512,128]{2,1,0:T(8,128)(2,1)S(1)} %collective-permute-done.7.refs_1_), channel_id=1, source_target_pairs={{0,1},{1,0},{2,3},{3,2},{4,5},{5,4},{6,7},{7,6},{8,9},{9,8},{10,11... | collective-permute-start | bytes 786440 | tf_op jit(solution)/shard_map/ppermute | solution.py:37
  26.0 1.6 %collective-permute-start.5 = (bf16[128,1024]{1,0:T(8,128)(2,1)S(1)}, bf16[128,1024]{1,0:T(8,128)(2,1)S(1)}, u32[]{:S(2)}, u32[]{:S(2)}) collective-permute-start(bf16[128,1024]{1,0:T(8,128)(2,1)S(1)} %collective-permute-done.4.refs_2_), channel_id=1, source_target_pairs={{0,1},{1,0},{2,3},{3,2},{4,5},{5,4},{6,7},{7,6},{8,9},{9,8},{10,11... | collective-permute-start | bytes 786440 | tf_op jit(solution)/shard_map/ppermute | solution.py:37
  26.0 9.4 %collective-permute-start.16 = (bf16[128,1024]{1,0:T(8,128)(2,1)S(1)}, bf16[128,1024]{1,0:T(8,128)(2,1)S(1)}, u32[]{:S(2)}, u32[]{:S(2)}) collective-permute-start(bf16[128,1024]{1,0:T(8,128)(2,1)S(1)} %collective-permute-done.14.refs_0_), channel_id=1, source_target_pairs={{0,2},{1,3},{2,0},{3,1},{4,6},{5,7},{6,4},{7,5},{8,10},{9,11},{10,... | collective-permute-start | bytes 786440 | tf_op jit(solution)/shard_map/ppermute | solution.py:37
  26.7 10.8 %collective-permute-start.15 = (bf16[128,1024]{1,0:T(8,128)(2,1)S(1)}, bf16[128,1024]{1,0:T(8,128)(2,1)S(1)}, u32[]{:S(2)}, u32[]{:S(2)}) collective-permute-start(bf16[128,1024]{1,0:T(8,128)(2,1)S(1)} %collective-permute-done.14.refs_0_), channel_id=1, source_target_pairs={{0,1},{1,0},{2,3},{3,2},{4,5},{5,4},{6,7},{7,6},{8,9},{9,8},{10,11... | collective-permute-start | bytes 786440 | tf_op jit(solution)/shard_map/ppermute | solution.py:37
  30.5 10.0 %copy-start.1 = (bf16[1,128,1024]{2,1,0:T(8,128)(2,1)S(1)}, bf16[1,128,1024]{2,1,0:T(8,128)(2,1)}, u32[]{:S(2)}) copy-start(bf16[1,128,1024]{2,1,0:T(8,128)(2,1)} %param.7) | copy-start | bytes 786436
  30.5 9.9 %collective-permute-start.10 = (bf16[128,1024]{1,0:T(8,128)(2,1)S(1)}, bf16[128,1024]{1,0:T(8,128)(2,1)S(1)}, u32[]{:S(2)}, u32[]{:S(2)}) collective-permute-start(bf16[128,1024]{1,0:T(8,128)(2,1)S(1)} %collective-permute-done.refs_0_), channel_id=1, source_target_pairs={{0,2},{1,3},{2,0},{3,1},{4,6},{5,7},{6,4},{7,5},{8,10},{9,11},{10,... | collective-permute-start | bytes 786440 | tf_op jit(solution)/shard_map/ppermute | solution.py:37
  32.1 15.6 %collective-permute-start.13 = (bf16[128,1024]{1,0:T(8,128)(2,1)S(1)}, bf16[128,1024]{1,0:T(8,128)(2,1)S(1)}, u32[]{:S(2)}, u32[]{:S(2)}) collective-permute-start(bf16[128,1024]{1,0:T(8,128)(2,1)S(1)} %collective-permute-done.refs_0_), channel_id=1, source_target_pairs={{0,1},{1,0},{2,3},{3,2},{4,5},{5,4},{6,7},{7,6},{8,9},{9,8},{10,11... | collective-permute-start | bytes 786440 | tf_op jit(solution)/shard_map/ppermute | solution.py:37
  32.1 23.9 %collective-permute-start.18 = (bf16[128,1024]{1,0:T(8,128)(2,1)S(1)}, bf16[128,1024]{1,0:T(8,128)(2,1)S(1)}, u32[]{:S(2)}, u32[]{:S(2)}) collective-permute-start(bf16[128,1024]{1,0:T(8,128)(2,1)S(1)} %visit_2.1), channel_id=1, source_target_pairs={{0,8},{4,12},{8,0},{12,4},{1,9},{5,13},{9,1},{13,5},{2,10},{6,14},... | collective-permute-start | bytes 786440 | tf_op jit(solution)/shard_map/ppermute | solution.py:398
  40.5 10.2 %collective-permute-start.12 = (bf16[128,1024]{1,0:T(8,128)(2,1)S(1)}, bf16[128,1024]{1,0:T(8,128)(2,1)S(1)}, u32[]{:S(2)}, u32[]{:S(2)}) collective-permute-start(bf16[128,1024]{1,0:T(8,128)(2,1)S(1)} %bitcast.7), channel_id=1, source_target_pairs={{0,2},{1,3},{2,0},{3,1},{4,6},{5,7},{6,4},{7,5},{8,10},{9,11},{10,... | collective-permute-start | bytes 786440 | tf_op jit(solution)/shard_map/ppermute | solution.py:37
  41.1 14.9 %collective-permute-start.19 = (bf16[128,1024]{1,0:T(8,128)(2,1)S(1)}, bf16[128,1024]{1,0:T(8,128)(2,1)S(1)}, u32[]{:S(2)}, u32[]{:S(2)}) collective-permute-start(bf16[128,1024]{1,0:T(8,128)(2,1)S(1)} %visit_3.1), channel_id=1, source_target_pairs={{0,12},{4,8},{8,4},{12,0},{1,13},{5,9},{9,5},{13,1},{2,14},{6,10},... | collective-permute-start | bytes 786440 | tf_op jit(solution)/shard_map/ppermute | solution.py:398
  45.3 7.7 %collective-permute-start.11 = (bf16[128,1024]{1,0:T(8,128)(2,1)S(1)}, bf16[128,1024]{1,0:T(8,128)(2,1)S(1)}, u32[]{:S(2)}, u32[]{:S(2)}) collective-permute-start(bf16[128,1024]{1,0:T(8,128)(2,1)S(1)} %bitcast.8), channel_id=1, source_target_pairs={{0,1},{1,0},{2,3},{3,2},{4,5},{5,4},{6,7},{7,6},{8,9},{9,8},{10,11... | collective-permute-start | bytes 786440 | tf_op jit(solution)/shard_map/ppermute | solution.py:37
  50.6 8.7 %collective-permute-start.17 = (bf16[128,1024]{1,0:T(8,128)(2,1)S(1)}, bf16[128,1024]{1,0:T(8,128)(2,1)S(1)}, u32[]{:S(2)}, u32[]{:S(2)}) collective-permute-start(bf16[128,1024]{1,0:T(8,128)(2,1)S(1)} %visit_1.1), channel_id=1, source_target_pairs={{0,4},{4,0},{8,12},{12,8},{1,5},{5,1},{9,13},{13,9},{2,6},{6,2},{1... | collective-permute-start | bytes 786440 | tf_op jit(solution)/shard_map/ppermute | solution.py:398

commit v4 on v3

--- a/solution.py
+++ b/solution.py
@@ -13,6 +13,7 @@
 HD = 64
 VISITS = 4
 LANES = 128
+STRIPS = 4
 VMEM_LIMIT = 16 * 1024 * 1024
 
 EPSILON = 1e-05
@@ -61,7 +62,7 @@
 def visit_kernel(parts, held, *refs):
     (own, beside, *chips), refs = refs[:held], refs[held:]
     gain_ref, query_ref, keyval_ref, cosine_ref, sine_ref, bias_ref = refs[:6]
-    out_ref, normed_ref, queries_ref, scores_ref, probabilities_ref = refs[6:]
+    out_ref, total_ref, queries_ref, scores_ref, probabilities_ref = refs[6:]
     rows, features = own.shape
     columns = query_ref.shape[2]
     width = parts * features
@@ -84,13 +85,25 @@
         values = shard[start : start + rows].astype(jnp.float32)
         squares += jnp.sum(values * values, axis=1, keepdims=True)
     scale = lax.rsqrt(squares / width + EPSILON)
-    for shard, start, owner in shards:
+    keyval = jnp.zeros((rows, keyval_ref.shape[2]), jnp.float32)
+
+    def multiply(normed, owner, first):
+        for start in range(0, columns, step):
+            place = slice(start, start + step)
+            product = jnp.dot(
+                normed, query_ref[owner, :, place], preferred_element_type=jnp.float32
+            )
+            if first:
+                total_ref[:, place] = product
+            else:
+                total_ref[:, place] += product
+        return jnp.dot(normed, keyval_ref[owner], preferred_element_type=jnp.float32)
+
+    for number, (shard, start, owner) in enumerate(shards):
         values = shard[start : start + rows].astype(jnp.float32)
         gain = gain_ref[:, pl.ds(pl.multiple_of(owner * features, LANES), features)]
-        normed_ref[owner] = (values * scale * gain).astype(jnp.bfloat16)
-    keyval = jnp.zeros((rows, keyval_ref.shape[2]), jnp.float32)
-    for part in range(parts):
-        keyval += jnp.dot(normed_ref[part], keyval_ref[part], preferred_element_type=jnp.float32)
+        normed = (values * scale * gain).astype(jnp.bfloat16)
+        keyval += multiply(normed, owner, number == 0)
 
     cosine, sine = cosine_ref[...], sine_ref[...]
     lane = lax.broadcasted_iota(jnp.int32, (rows, LANES), 1)
@@ -102,18 +115,11 @@
     values = jnp.where(in_first_head, 0.0, keyval)
     values = jnp.concatenate([pltpu.roll(values, HD, 1), values], axis=0).T.astype(jnp.bfloat16)
 
-    for start in range(0, columns, step):
-        total = jnp.zeros((rows, step), jnp.float32)
-        for part in range(parts):
-            total += jnp.dot(
-                normed_ref[part],
-                query_ref[part, :, start : start + step],
-                preferred_element_type=jnp.float32,
-            )
-        for pair in range(0, step, LANES):
-            queries_ref[:, start + pair : start + pair + LANES] = rotated(
-                total[:, pair : pair + LANES], cosine, sine, in_first_half
-            ).astype(jnp.bfloat16)
+    for pair in range(pairs):
+        place = slice(pair * LANES, (pair + 1) * LANES)
+        queries_ref[:, place] = rotated(total_ref[:, place], cosine, sine, in_first_half).astype(
+            jnp.bfloat16
+        )
     for pair in range(pairs):
         scores_ref[pair] = lax.dot_general(
             keys,
@@ -146,7 +152,7 @@
         in_specs=[vmem] * len(operands),
         out_specs=vmem,
         scratch_shapes=[
-            pltpu.VMEM((parts, rows, features), jnp.bfloat16),
+            pltpu.VMEM((rows, columns), jnp.float32),
             pltpu.VMEM((rows, columns), jnp.bfloat16),
             pltpu.VMEM(scores, jnp.float32),
             pltpu.VMEM(scores, jnp.bfloat16),
@@ -200,7 +206,11 @@
     sems = refs[-1]
     parts = query_ref.shape[0]
     moves = [(gain_any, gain_ref), (cosine_any, cosine_ref), (sine_any, sine_ref)]
-    moves += [(query_any.at[part], query_ref.at[part]) for part in range(parts)]
+    strip = query_ref.shape[1] // STRIPS
+    for part in range(parts):
+        for number in range(STRIPS):
+            place = pl.ds(number * strip, strip)
+            moves.append((query_any.at[part, place], query_ref.at[part, place]))
     copies = [
         pltpu.make_async_copy(source, target, sems.at[number])
         for number, (source, target) in enumerate(moves)
@@ -237,7 +247,7 @@
         ],
         in_specs=[pl.BlockSpec(memory_space=pltpu.SMEM)] + [hbm] * 4,
         out_specs=[vmem] * (len(held) + 1 + len(biases)),
-        scratch_shapes=[pltpu.SemaphoreType.DMA((3 + query.shape[0],))],
+        scratch_shapes=[pltpu.SemaphoreType.DMA((3 + STRIPS * query.shape[0],))],
         compiler_params=pltpu.CompilerParams(vmem_limit_bytes=VMEM_LIMIT),
         name="stage_weights",
     )(
@@ -253,81 +263,81 @@
     return (rank * heads_here) // (QHEADS // KVHEADS)
 
 
-def cut_kernel(heads_here, keyval_ref, own_ref, beside_ref, *chip_refs):
+def cut_kernel(heads_here, keyval_ref, *out_refs):
     rank = lax.axis_index("tp")
     league = lax.axis_index("league")
-    width = own_ref.shape[1]
-
-    def columns(other):
-        head = head_of(lax.bitwise_xor(rank, jnp.int32(other)), heads_here)
-        return pl.ds(pl.multiple_of(head * width, LANES), width)
-
-    own_ref[...] = keyval_ref[:, columns(0)]
-    beside_ref[...] = keyval_ref[:, columns(1)]
-    core = lax.rem(rank, 2)
-    for number, chip_ref in enumerate(chip_refs):
-        rows = chip_ref.shape[1]
-        mine = pl.ds(pl.multiple_of(league * rows, 16), rows)
-        for beside in range(2):
-            chip_ref[lax.bitwise_xor(core, jnp.int32(beside))] = keyval_ref[
-                mine, columns(2 * (number + 1) + beside)
-            ]
+    for bits, out_ref in enumerate(out_refs):
+        rows, width = out_ref.shape
+        head = head_of(lax.bitwise_xor(rank, jnp.int32(bits)), heads_here)
+        columns = pl.ds(pl.multiple_of(head * width, LANES), width)
+        if bits < 2:
+            out_ref[...] = keyval_ref[:, columns]
+        else:
+            out_ref[...] = keyval_ref[pl.ds(pl.multiple_of(league * rows, 16), rows), columns]
 
 
 def cut_keyval(keyval, heads_here, parts, leagues):
     features, width = keyval.shape[0], 2 * HD
-    column = jax.ShapeDtypeStruct((features, width), keyval.dtype)
-    chip = jax.ShapeDtypeStruct((2, features // leagues, width), keyval.dtype)
-    chips = parts // 2 - 1
+    rows = [features // (1 if bits < 2 else leagues) for bits in range(parts)]
     vmem = pl.BlockSpec(memory_space=pltpu.VMEM)
     return pl.pallas_call(
         functools.partial(cut_kernel, heads_here),
-        out_shape=[column, column] + [chip] * chips,
+        out_shape=[jax.ShapeDtypeStruct((count, width), keyval.dtype) for count in rows],
         in_specs=[vmem],
-        out_specs=[vmem] * (2 + chips),
+        out_specs=[vmem] * parts,
         compiler_params=pltpu.CompilerParams(vmem_limit_bytes=VMEM_LIMIT),
         name="cut_keyval",
     )(keyval)
 
 
-def join_kernel(leagues, own_ref, beside_ref, *refs):
-    pieces, out_ref, sems = refs[:-2], refs[-2], refs[-1]
+def join_kernel(counts, *refs):
+    passed = (len(refs) - 2 - sum(counts)) // 2
+    pieces, refs = refs[: sum(counts)], refs[sum(counts) :]
+    sources, out_ref, targets, sems = (
+        refs[:passed],
+        refs[passed],
+        refs[passed + 1 : -1],
+        refs[-1],
+    )
     rank = lax.axis_index("tp")
     league = lax.axis_index("league")
-    core = lax.rem(rank, 2)
-    copies = [(own_ref, out_ref.at[rank]), (beside_ref, out_ref.at[lax.bitwise_xor(rank, 1)])]
-    number = 0
-    for chip in range(1, out_ref.shape[0] // 2):
-        for beside in range(2):
-            owner = lax.bitwise_xor(rank, jnp.int32(2 * chip + beside))
-            for by in range(leagues):
-                piece = pieces[number]
-                rows = piece.shape[1]
-                source = lax.rem(league + (leagues - by), leagues)
-                place = pl.ds(pl.multiple_of(source * rows, 16), rows)
-                copies.append((piece.at[core], out_ref.at[owner, place]))
-                number += 1
-    started = [
-        pltpu.make_async_copy(source, target, sems.at[i])
-        for i, (source, target) in enumerate(copies)
+    moves = []
+    for bits, count in enumerate(counts):
+        owner = lax.bitwise_xor(rank, jnp.int32(bits))
+        for by in range(count):
+            piece = pieces[len(moves)]
+            rows = piece.shape[0]
+            source = lax.rem(league + (count - by), count)
+            place = pl.ds(pl.multiple_of(source * rows, 16), rows)
+            moves.append((piece, out_ref.at[owner, place]))
+    moves += list(zip(sources, targets))
+    copies = [
+        pltpu.make_async_copy(source, target, sems.at[number])
+        for number, (source, target) in enumerate(moves)
     ]
-    for copy in started:
+    for copy in copies:
         copy.start()
-    for copy in started:
+    for copy in copies:
         copy.wait()
 
 
-def join_keyval(own, beside, pieces, parts, leagues):
+def join_keyval(groups, passed):
     any_space = pl.BlockSpec(memory_space=pl.ANY)
-    return pl.pallas_call(
-        functools.partial(join_kernel, leagues),
-        out_shape=pltpu.VMEM((parts, *own.shape), own.dtype),
-        in_specs=[any_space] * (2 + len(pieces)),
-        out_specs=pl.BlockSpec(memory_space=pltpu.VMEM),
-        scratch_shapes=[pltpu.SemaphoreType.DMA((2 + len(pieces),))],
+    pieces = [piece for group in groups for piece in group]
+    features, width = pieces[0].shape
+    keyval, *held = pl.pallas_call(
+        functools.partial(join_kernel, [len(group) for group in groups]),
+        out_shape=[
+            pltpu.VMEM((len(groups), features, width), pieces[0].dtype),
+            *(pltpu.VMEM(array.shape, array.dtype) for array in passed),
+        ],
+        in_specs=[any_space] * (len(pieces) + len(passed)),
+        out_specs=[pl.BlockSpec(memory_space=pltpu.VMEM)] * (1 + len(passed)),
+        scratch_shapes=[pltpu.SemaphoreType.DMA((len(pieces) + len(passed),))],
         compiler_params=pltpu.CompilerParams(vmem_limit_bytes=VMEM_LIMIT),
         name="join_keyval",
-    )(own, beside, *pieces)
+    )(*pieces, *passed)
+    return keyval, held
 
 
 def kept_order(array, *earlier):
@@ -344,14 +354,11 @@
     heads_here = query.shape[2] // HD
     cosine, sine = rope_tables(rows)
 
-    own_columns, beside_columns, *chip_columns = cut_keyval(
-        keyval_weight[0], heads_here, parts, leagues
-    )
-    query_held, gain_held, cosine_held, sine_held, keep, token, *biases = staged(
-        lengths, query, norm_gain, cosine, sine, rows
-    )
     def moved(block, visit):
         return lax.ppermute(block, "snap", visit_pairs(snaps, visit))
+
+    def sent_home(visit, array):
+        return lax.ppermute(array, "snap", visit_pairs(snaps, visit, back=True))
 
     if snaps == VISITS:
         block_2 = moved(own, 2)
@@ -361,15 +368,23 @@
         block_1 = moved(own, 1)
         block_2 = moved(block_1, 1)
         block_3 = moved(block_2, 1)
-    beside = swapped(beside_columns, 1)
-    arrived = [swapped(columns, 2 * (i + 1)) for i, columns in enumerate(chip_columns)]
-    pieces = []
-    for columns in arrived:
-        by_league = [kept_order(columns, token, block_2)]
+
+    query_held, gain_held, cosine_held, sine_held, keep, token, *biases = staged(
+        lengths, query, norm_gain, cosine, sine, rows
+    )
+
+    columns = cut_keyval(keyval_weight[0], heads_here, parts, leagues)
+    groups = [[columns[0]], [swapped(columns[1], 1)]]
+    arrived = [swapped(columns[bits], bits) for bits in range(2, parts)]
+    for piece in arrived:
+        by_league = [kept_order(piece, token, block_1, block_2)]
         for _ in range(1, leagues):
-            by_league.append(lax.ppermute(by_league[-1], "league", [(i, (i + 1) % leagues) for i in range(leagues)]))
-        pieces += by_league + [swapped(piece, 1) for piece in by_league]
-    keyval = join_keyval(own_columns, beside, pieces, parts, leagues)
+            by_league.append(
+                lax.ppermute(
+                    by_league[-1], "league", [(i, (i + 1) % leagues) for i in range(leagues)]
+                )
+            )
+        groups.append(by_league)
 
     def over_chips(block):
         return [block] + [swapped(block, bits) for bits in range(2, parts, 2)]
@@ -380,7 +395,7 @@
         own_shard, *chips = shards
         gathered = [own_shard, swapped(own_shard, 1)]
         for shard in chips:
-            shard = kept_order(shard, *earlier) if earlier else shard
+            shard = kept_order(shard, *earlier)
             if apart:
                 gathered += [shard, swapped(shard, 1)]
             else:
@@ -389,26 +404,25 @@
                 )
         return gathered
 
+    shards_2 = over_chips(kept_order(block_2, token, *arrived))
+    shards_3 = over_chips(kept_order(block_3, *shards_2[1:]))
+    keyval, held = join_keyval(groups, shards_2[1:])
+
     def scored(visit, shards):
         return visit_context(
             visit, shards, gain_held, query_held, keyval, cosine_held, sine_held, biases[visit]
         )
 
-    def sent_home(visit, array):
-        return lax.ppermute(array, "snap", visit_pairs(snaps, visit, back=True))
-
-    shards_2 = over_chips(kept_order(block_2, token, *arrived))
-    shards_3 = over_chips(kept_order(block_3, *shards_2[1:]))
-    context_2 = scored(2, over_cores(shards_2, block_1, apart=True))
+    context_2 = scored(2, over_cores([shards_2[0], *held], block_1, apart=True))
     home_2 = sent_home(2, context_2)
     shards_1 = over_chips(kept_order(block_1, context_2))
-    shards_0 = over_chips(kept_order(own, *shards_1[1:]))
+    shards_0 = over_chips(kept_order(own, context_2, *shards_1[1:]))
     context_3 = scored(3, over_cores(shards_3, context_2))
     home_3 = sent_home(3, context_3)
     context_1 = scored(1, over_cores(shards_1, context_3))
     home_1 = sent_home(1, context_1)
-    context_0 = scored(0, over_cores(shards_0, context_1))
-    return mean_of(keep, [context_0, home_1, home_2, home_3])[None]
+    context_0 = scored(0, over_cores(shards_0, context_3))
+    return mean_of(keep, [context_0, home_2, home_3, home_1])[None]
 
 
 def solution(mesh):

time: 60.5 us -> 59.9 us (0.990)
  Pallas kernels: 18.2 us -> 17.5 us
    ppermute x3, waiting for transfers between devices: 3.61 us -> 2.29 us  [moved(): return lax.ppermute(block, 'snap', visit_pairs(snaps, visit))]
    ppermute x1 -> x2, waiting for transfers between devices: 3.14 us -> 4.15 us  [on_device(): lax.ppermute(by_league[-1], 'league', [(i, (i + 1) % leagues) for i in ra...]
    pallas_call x4, Pallas kernels: 11.7 us -> 10.9 us  [visit_context(): pl.pallas_call(functools.partial(visit_kernel, parts, len(shards)), out_s...]
    ppermute x1 -> x2, starting transfers between devices: 1.57 us -> 2.03 us  [on_device(): lax.ppermute(by_league[-1], 'league', [(i, (i + 1) % leagues) for i in ra...]
    ppermute x13 -> x12, starting transfers between devices: 6.5 us -> 6.51 us  [swapped(): return lax.ppermute(array, 'tp', [(i, i ^ with_bits) for i in range(count)])]
  transfers between devices with their start and end apart: 20 -> 20, of which waited for: 5 -> 7; matrix products, arithmetic and copies ran while one was open for 0% -> 0% of each run, Pallas kernels for 29% -> 28%
where the time goes in v4:
time: 59.9 us; the launch traced here: 59.6 us
  starting transfers between devices  22.2 us (37%)
  Pallas kernels  17.5 us (29%)
  waiting for transfers between devices  11 us (18%)
  blocking collectives  6.84 us (11%)
  local copies, waits for them, and re-layouts  1.89 us (3%)
    pallas_call x4, Pallas kernels, visit_context(): pl.pallas_call(functools.partial(visit_kernel, parts, len(shards)), out_s...  10.9 us
    ppermute x3, starting transfers between devices, sent_home(): return lax.ppermute(array, 'snap', visit_pairs(snaps, visit, back=True))  7.35 us
    all_gather x3, blocking collectives, over_cores(): lax.all_gather(shard, 'tp', axis=0, tiled=True, axis_index_groups=pairs_o...  6.84 us
    ppermute x12, starting transfers between devices, swapped(): return lax.ppermute(array, 'tp', [(i, i ^ with_bits) for i in range(count)])  6.51 us
    ppermute x3, starting transfers between devices, moved(): return lax.ppermute(block, 'snap', visit_pairs(snaps, visit))  6.28 us
    pallas_call x1, Pallas kernels, staged(): pl.pallas_call(stage_kernel, out_shape=[*(pltpu.VMEM(*each) for each in h...  4.76 us
    ppermute x2, waiting for transfers between devices, on_device(): lax.ppermute(by_league[-1], 'league', [(i, (i + 1) % leagues) for i in ra...  4.15 us
    ppermute x3, waiting for transfers between devices, sent_home(): return lax.ppermute(array, 'snap', visit_pairs(snaps, visit, back=True))  3.44 us
  transfers between devices with their start and end apart: 20, of which 7 were waited for; matrix products, arithmetic and copies ran while one was open for 0% of the time, Pallas kernels for 28%

profile of v4, /device:TPU:0, one launch (start us, length us, event | category | flops | bytes accessed | tf_op | source)
XLA Modules:
  0.0 59.6 jit_solution(9373776194866854564)
XLA Ops:
  0.0 4.0 %collective-permute-start = (bf16[128,1024]{1,0:T(8,128)(2,1)}, bf16[128,1024]{1,0:T(8,128)(2,1)S(1)}, u32[]{:S(2)}, u32[]{:S(2)}) collective-permute-start(bf16[128,1024]{1,0:T(8,128)(2,1)} %bitcast.5), channel_id=1, source_target_pairs={{0,8},{4,12},{8,0},{12,4},{1,9},{5,13},{9,1},{13,5},{2,10},{6,14},... | collective-permute-start | bytes 786440 | tf_op jit(solution)/shard_map/ppermute | solution.py:358
  4.0 1.6 %collective-permute-start.5 = (bf16[128,1024]{1,0:T(8,128)(2,1)}, bf16[128,1024]{1,0:T(8,128)(2,1)S(1)}, u32[]{:S(2)}, u32[]{:S(2)}) collective-permute-start(bf16[128,1024]{1,0:T(8,128)(2,1)} %bitcast.6), channel_id=1, source_target_pairs={{0,4},{4,0},{8,12},{12,8},{1,5},{5,1},{9,13},{13,9},{2,6},{6,2},{1... | collective-permute-start | bytes 786440 | tf_op jit(solution)/shard_map/ppermute | solution.py:358
  5.6 1.2 %copy-done = bf16[1,1024,512]{2,1,0:T(8,128)(2,1)S(1)} copy-done((bf16[1,1024,512]{2,1,0:T(8,128)(2,1)S(1)}, bf16[1,1024,512]{2,1,0:T(8,128)(2,1)}, u32[]{:S(2)}) %copy-start) | copy-done | bytes 1048600
  7.0 1.6 %collective-permute-start.1 = (bf16[512,128]{1,0:T(8,128)(2,1)S(1)}, bf16[512,128]{1,0:T(8,128)(2,1)S(1)}, u32[]{:S(2)}, u32[]{:S(2)}) collective-permute-start(bf16[512,128]{1,0:T(8,128)(2,1)S(1)} %get-tuple-element.33), channel_id=1, source_target_pairs={{0,2},{1,3},{2,0},{3,1},{4,6},{5,7},{6,4},{7,5},{8,10},{9,11},{10,... | collective-permute-start | bytes 393224 | tf_op jit(solution)/shard_map/ppermute | solution.py:38
  9.9 4.8 %stage_weights.1 = (bf16[4,1024,1024]{2,1,0:T(8,128)(2,1)S(1)}, f32[1,4096]{1,0:T(1,128)S(1)}, f32[128,128]{1,0:T(8,128)S(1)}, f32[128,128]{1,0:T(8,128)S(1)}, f...) custom-call(s32[4]{0:T(128)S(1)} %copy-done.2, ...), custom_call_target="tpu_custom_call" | custom-call | tf_op jit(solution)/shard_map/stage_weights/pallas_call | solution.py:241
  14.6 1.6 %collective-permute-done.refs_0_ = bf16[128,1024]{1,0:T(8,128)(2,1)S(1)} collective-permute-done((bf16[128,1024]{1,0:T(8,128)(2,1)}, bf16[128,1024]{1,0:T(8,128)(2,1)S(1)}, u32[]{:S(2)}, u32[]{:S(2)}) %collective-permute-start) | collective-permute-done | bytes 262176 | tf_op jit(solution)/shard_map/ppermute | solution.py:358
  16.3 1.5 %collective-permute-start.8 = (bf16[128,1024]{1,0:T(8,128)(2,1)S(1)}, bf16[128,1024]{1,0:T(8,128)(2,1)S(1)}, u32[]{:S(2)}, u32[]{:S(2)}) collective-permute-start(bf16[128,1024]{1,0:T(8,128)(2,1)S(1)} %collective-permute-done.refs_0_), channel_id=1, source_target_pairs={{0,2},{1,3},{2,0},{3,1},{4,6},{5,7},{6,4},{7,5},{8,10},{9,11},{10,... | collective-permute-start | bytes 786440 | tf_op jit(solution)/shard_map/ppermute | solution.py:38
  17.8 1.5 %collective-permute-start.6 = (bf16[512,128]{1,0:T(8,128)(2,1)S(1)}, bf16[512,128]{1,0:T(8,128)(2,1)S(1)}, u32[]{:S(2)}, u32[]{:S(2)}) collective-permute-start(bf16[512,128]{1,0:T(8,128)(2,1)S(1)} %collective-permute-done.1.refs_2_), channel_id=1, source_target_pairs={{0,16},{16,0},{1,17},{17,1},{2,18},{18,2},{3,19},{19,3},{4,20},{20... | collective-permute-start | bytes 393224 | tf_op jit(solution)/shard_map/ppermute | solution.py:383
  20.5 2.7 %collective-permute-done.6.refs_3_ = bf16[512,128]{1,0:T(8,128)(2,1)S(1)} collective-permute-done((bf16[512,128]{1,0:T(8,128)(2,1)S(1)}, bf16[512,128]{1,0:T(8,128)(2,1)S(1)}, u32[]{:S(2)}, u32[]{:S(2)}) %collective-permute-start.6) | collective-permute-done | bytes 131104 | tf_op jit(solution)/shard_map/ppermute | solution.py:383
  23.3 1.4 %collective-permute-done.7.refs_5_ = bf16[512,128]{1,0:T(8,128)(2,1)S(1)} collective-permute-done((bf16[512,128]{1,0:T(8,128)(2,1)S(1)}, bf16[512,128]{1,0:T(8,128)(2,1)S(1)}, u32[]{:S(2)}, u32[]{:S(2)}) %collective-permute-start.7) | collective-permute-done | bytes 131104 | tf_op jit(solution)/shard_map/ppermute | solution.py:383
  24.7 0.8 %join_keyval.1 = (bf16[4,1024,128]{2,1,0:T(8,128)(2,1)S(1)}, bf16[128,1024]{1,0:T(8,128)(2,1)S(1)}) custom-call(bf16[1024,128]{1,0:T(8,128)(2,1)S(1)} %get-tuple-element.36.refs_0_, bf16[1024,128]{1,0:T(8,128)(2,1)S(1)} %collective-permute-done.4.refs_1_, bf16[512,128]{1,0:T(8,128)(2,1)S(1)} %collective-permute-done.1.refs_2_, ...), custom_call_target="tpu_custom_call" | custom-call | tf_op jit(solution)/shard_map/join_keyval/pallas_call | solution.py:328
  27.1 2.7 %visit_2.1 = bf16[128,1024]{1,0:T(8,128)(2,1)S(1)} custom-call(bf16[128,1024]{1,0:T(8,128)(2,1)S(1)} %collective-permute-done.refs_0_, bf16[128,1024]{1,0:T(8,128)(2,1)S(1)} %collective-permute-done.3.refs_1_, bf16[128,1024]{1,0:T(8,128)(2,1)S(1)} %get-tuple-element.41.refs_2_, bf16[128,1024]{1,0:T(8,128)(2,1)S(1)} %collective-permute-done.9.refs_3_, ...), custom_call_target="tpu_custom_call" | custom-call | flops 1 | bytes 1 | tf_op jit(solution)/shard_map/visit_2/pallas_call | solution.py:149
  29.8 1.2 %collective-permute-start.10 = (bf16[128,1024]{1,0:T(8,128)(2,1)S(1)}, bf16[128,1024]{1,0:T(8,128)(2,1)S(1)}, u32[]{:S(2)}, u32[]{:S(2)}) collective-permute-start(bf16[128,1024]{1,0:T(8,128)(2,1)S(1)} %collective-permute-done.5.refs_0_), channel_id=1, source_target_pairs={{0,2},{1,3},{2,0},{3,1},{4,6},{5,7},{6,4},{7,5},{8,10},{9,11},{10,... | collective-permute-start | bytes 786440 | tf_op jit(solution)/shard_map/ppermute | solution.py:38
  31.3 3.2 %collective-permute-start.16 = (bf16[128,1024]{1,0:T(8,128)(2,1)S(1)}, bf16[128,1024]{1,0:T(8,128)(2,1)S(1)}, u32[]{:S(2)}, u32[]{:S(2)}) collective-permute-start(bf16[128,1024]{1,0:T(8,128)(2,1)S(1)} %visit_2.1), channel_id=1, source_target_pairs={{0,8},{4,12},{8,0},{12,4},{1,9},{5,13},{9,1},{13,5},{2,10},{6,14},... | collective-permute-start | bytes 786440 | tf_op jit(solution)/shard_map/ppermute | solution.py:361
  34.5 0.9 %collective-permute-done.15 = bf16[128,1024]{1,0:T(8,128)(2,1)S(1)} collective-permute-done((bf16[128,1024]{1,0:T(8,128)(2,1)S(1)}, bf16[128,1024]{1,0:T(8,128)(2,1)S(1)}, u32[]{:S(2)}, u32[]{:S(2)}) %collective-permute-start.15) | collective-permute-done | bytes 262176 | tf_op jit(solution)/shard_map/ppermute | solution.py:38
  35.4 2.2 %all_gather.9.refs_2_ = bf16[256,1024]{1,0:T(8,128)(2,1)S(1)} all-gather(bf16[128,1024]{1,0:T(8,128)(2,1)S(1)} %collective-permute-done.15), channel_id=1, replica_groups={{0,1},{2,3},{4,5},{6,7},{8,9},{10,11},{12,13},{14,15},{16,17},{18,19},{..., dimensions={0}, use_global_device_ids=true | all-gather | bytes 786432 | tf_op jit(solution)/shard_map/all_gather | solution.py:403
  37.6 2.7 %visit_3.1 = bf16[128,1024]{1,0:T(8,128)(2,1)S(1)} custom-call(bf16[128,1024]{1,0:T(8,128)(2,1)S(1)} %collective-permute-done.13.refs_0_, bf16[128,1024]{1,0:T(8,128)(2,1)S(1)} %collective-permute-done.14.refs_1_, bf16[256,1024]{1,0:T(8,128)(2,1)S(1)} %all_gather.9.refs_2_, f32[1,4096]{1,0:T(1,128)S(1)} %get-tuple-element.42.refs_4_.refs_3_, ...), custom_call_target="tpu_custom_call" | custom-call | flops 1 | bytes 1 | tf_op jit(solution)/shard_map/visit_3/pallas_call | solution.py:149
  40.9 4.1 %collective-permute-start.17 = (bf16[128,1024]{1,0:T(8,128)(2,1)S(1)}, bf16[128,1024]{1,0:T(8,128)(2,1)S(1)}, u32[]{:S(2)}, u32[]{:S(2)}) collective-permute-start(bf16[128,1024]{1,0:T(8,128)(2,1)S(1)} %visit_3.1), channel_id=1, source_target_pairs={{0,12},{4,8},{8,4},{12,0},{1,13},{5,9},{9,5},{13,1},{2,14},{6,10},... | collective-permute-start | bytes 786440 | tf_op jit(solution)/shard_map/ppermute | solution.py:361
  44.9 2.3 %all_gather.11.refs_2_ = bf16[256,1024]{1,0:T(8,128)(2,1)S(1)} all-gather(bf16[128,1024]{1,0:T(8,128)(2,1)S(1)} %collective-permute-done.10), channel_id=1, replica_groups={{0,1},{2,3},{4,5},{6,7},{8,9},{10,11},{12,13},{14,15},{16,17},{18,19},{..., dimensions={0}, use_global_device_ids=true | all-gather | bytes 786432 | tf_op jit(solution)/shard_map/all_gather | solution.py:403
  47.2 2.7 %visit_1.1 = bf16[128,1024]{1,0:T(8,128)(2,1)S(1)} custom-call(bf16[128,1024]{1,0:T(8,128)(2,1)S(1)} %collective-permute-done.5.refs_0_, bf16[128,1024]{1,0:T(8,128)(2,1)S(1)} %collective-permute-done.18.refs_1_, bf16[256,1024]{1,0:T(8,128)(2,1)S(1)} %all_gather.11.refs_2_, f32[1,4096]{1,0:T(1,128)S(1)} %get-tuple-element.42.refs_4_.refs_3_, ...), custom_call_target="tpu_custom_call" | custom-call | flops 1 | bytes 1 | tf_op jit(solution)/shard_map/visit_1/pallas_call | solution.py:149
  50.1 2.4 %all_gather.10.refs_2_ = bf16[256,1024]{1,0:T(8,128)(2,1)S(1)} all-gather(bf16[128,1024]{1,0:T(8,128)(2,1)S(1)} %collective-permute-done.12), channel_id=1, replica_groups={{0,1},{2,3},{4,5},{6,7},{8,9},{10,11},{12,13},{14,15},{16,17},{18,19},{..., dimensions={0}, use_global_device_ids=true | all-gather | bytes 786432 | tf_op jit(solution)/shard_map/all_gather | solution.py:403
  52.4 2.7 %visit_0.1.refs_0_ = bf16[128,1024]{1,0:T(8,128)(2,1)S(1)} custom-call(bf16[128,1024]{1,0:T(8,128)(2,1)S(1)} %bitcast.9, bf16[128,1024]{1,0:T(8,128)(2,1)S(1)} %collective-permute-done.11.refs_1_, bf16[256,1024]{1,0:T(8,128)(2,1)S(1)} %all_gather.10.refs_2_, f32[1,4096]{1,0:T(1,128)S(1)} %get-tuple-element.42.refs_4_.refs_3_, ...), custom_call_target="tpu_custom_call" | custom-call | flops 1 | bytes 1 | tf_op jit(solution)/shard_map/visit_0/pallas_call | solution.py:149
  55.2 3.4 %collective-permute-done.19.refs_3_ = bf16[128,1024]{1,0:T(8,128)(2,1)S(1)} collective-permute-done((bf16[128,1024]{1,0:T(8,128)(2,1)S(1)}, bf16[128,1024]{1,0:T(8,128)(2,1)S(1)}, u32[]{:S(2)}, u32[]{:S(2)}) %collective-permute-start.19) | collective-permute-done | bytes 262176 | tf_op jit(solution)/shard_map/ppermute | solution.py:361
  58.6 0.8 %mean_of_visits.1 = bf16[128,1024]{1,0:T(8,128)(2,1)} custom-call(f32[128,128]{1,0:T(8,128)S(1)} %get-tuple-element.31.keep_ref, bf16[128,1024]{1,0:T(8,128)(2,1)S(1)} %visit_0.1.refs_0_, bf16[128,1024]{1,0:T(8,128)(2,1)S(1)} %collective-permute-done.16.refs_1_, bf16[128,1024]{1,0:T(8,128)(2,1)S(1)} %collective-permute-done.17.refs_2_, ...), custom_call_target="tpu_custom_call" | custom-call | tf_op jit(solution)/shard_map/mean_of_visits/pallas_call | solution.py:190
  (33 shorter events, 5.1 us)
Async XLA Ops:
  0.0 16.3 %collective-permute-start = (bf16[128,1024]{1,0:T(8,128)(2,1)}, bf16[128,1024]{1,0:T(8,128)(2,1)S(1)}, u32[]{:S(2)}, u32[]{:S(2)}) collective-permute-start(bf16[128,1024]{1,0:T(8,128)(2,1)} %bitcast.5), channel_id=1, source_target_pairs={{0,8},{4,12},{8,0},{12,4},{1,9},{5,13},{9,1},{13,5},{2,10},{6,14},... | collective-permute-start | bytes 786440 | tf_op jit(solution)/shard_map/ppermute | solution.py:358
  4.0 13.8 %collective-permute-start.5 = (bf16[128,1024]{1,0:T(8,128)(2,1)}, bf16[128,1024]{1,0:T(8,128)(2,1)S(1)}, u32[]{:S(2)}, u32[]{:S(2)}) collective-permute-start(bf16[128,1024]{1,0:T(8,128)(2,1)} %bitcast.6), channel_id=1, source_target_pairs={{0,4},{4,0},{8,12},{12,8},{1,5},{5,1},{9,13},{13,9},{2,6},{6,2},{1... | collective-permute-start | bytes 786440 | tf_op jit(solution)/shard_map/ppermute | solution.py:358
  5.6 1.2 %copy-start = (bf16[1,1024,512]{2,1,0:T(8,128)(2,1)S(1)}, bf16[1,1024,512]{2,1,0:T(8,128)(2,1)}, u32[]{:S(2)}) copy-start(bf16[1,1024,512]{2,1,0:T(8,128)(2,1)} %param.11) | copy-start | bytes 3145732
  7.0 7.6 %collective-permute-start.1 = (bf16[512,128]{1,0:T(8,128)(2,1)S(1)}, bf16[512,128]{1,0:T(8,128)(2,1)S(1)}, u32[]{:S(2)}, u32[]{:S(2)}) collective-permute-start(bf16[512,128]{1,0:T(8,128)(2,1)S(1)} %get-tuple-element.33), channel_id=1, source_target_pairs={{0,2},{1,3},{2,0},{3,1},{4,6},{5,7},{6,4},{7,5},{8,10},{9,11},{10,... | collective-permute-start | bytes 393224 | tf_op jit(solution)/shard_map/ppermute | solution.py:38
  8.6 6.1 %collective-permute-start.2 = (bf16[512,128]{1,0:T(8,128)(2,1)S(1)}, bf16[512,128]{1,0:T(8,128)(2,1)S(1)}, u32[]{:S(2)}, u32[]{:S(2)}) collective-permute-start(bf16[512,128]{1,0:T(8,128)(2,1)S(1)} %get-tuple-element.34), channel_id=1, source_target_pairs={{0,3},{1,2},{2,1},{3,0},{4,7},{5,6},{6,5},{7,4},{8,11},{9,10},{10,... | collective-permute-start | bytes 393224 | tf_op jit(solution)/shard_map/ppermute | solution.py:38
  8.6 12.0 %collective-permute-start.4 = (bf16[1024,128]{1,0:T(8,128)(2,1)S(1)}, bf16[1024,128]{1,0:T(8,128)(2,1)S(1)}, u32[]{:S(2)}, u32[]{:S(2)}) collective-permute-start(bf16[1024,128]{1,0:T(8,128)(2,1)S(1)} %get-tuple-element.37), channel_id=1, source_target_pairs={{0,1},{1,0},{2,3},{3,2},{4,5},{5,4},{6,7},{7,6},{8,9},{9,8},{10,11... | collective-permute-start | bytes 786440 | tf_op jit(solution)/shard_map/ppermute | solution.py:38
  9.2 0.7 %copy-start.2 = (s32[4]{0:T(128)S(1)}, s32[4]{0:T(128)}, u32[]{:S(2)}) copy-start(s32[4]{0:T(128)} %lengths_ref.1) | copy-start | bytes 52
  16.3 8.4 %collective-permute-start.8 = (bf16[128,1024]{1,0:T(8,128)(2,1)S(1)}, bf16[128,1024]{1,0:T(8,128)(2,1)S(1)}, u32[]{:S(2)}, u32[]{:S(2)}) collective-permute-start(bf16[128,1024]{1,0:T(8,128)(2,1)S(1)} %collective-permute-done.refs_0_), channel_id=1, source_target_pairs={{0,2},{1,3},{2,0},{3,1},{4,6},{5,7},{6,4},{7,5},{8,10},{9,11},{10,... | collective-permute-start | bytes 786440 | tf_op jit(solution)/shard_map/ppermute | solution.py:38
  17.8 5.5 %collective-permute-start.6 = (bf16[512,128]{1,0:T(8,128)(2,1)S(1)}, bf16[512,128]{1,0:T(8,128)(2,1)S(1)}, u32[]{:S(2)}, u32[]{:S(2)}) collective-permute-start(bf16[512,128]{1,0:T(8,128)(2,1)S(1)} %collective-permute-done.1.refs_2_), channel_id=1, source_target_pairs={{0,16},{16,0},{1,17},{17,1},{2,18},{18,2},{3,19},{19,3},{4,20},{20... | collective-permute-start | bytes 393224 | tf_op jit(solution)/shard_map/ppermute | solution.py:383
  19.3 5.3 %collective-permute-start.7 = (bf16[512,128]{1,0:T(8,128)(2,1)S(1)}, bf16[512,128]{1,0:T(8,128)(2,1)S(1)}, u32[]{:S(2)}, u32[]{:S(2)}) collective-permute-start(bf16[512,128]{1,0:T(8,128)(2,1)S(1)} %collective-permute-done.2.refs_4_), channel_id=1, source_target_pairs={{0,16},{16,0},{1,17},{17,1},{2,18},{18,2},{3,19},{19,3},{4,20},{20... | collective-permute-start | bytes 393224 | tf_op jit(solution)/shard_map/ppermute | solution.py:383
  19.8 6.4 %collective-permute-start.13 = (bf16[128,1024]{1,0:T(8,128)(2,1)S(1)}, bf16[128,1024]{1,0:T(8,128)(2,1)S(1)}, u32[]{:S(2)}, u32[]{:S(2)}) collective-permute-start(bf16[128,1024]{1,0:T(8,128)(2,1)S(1)} %collective-permute-done.refs_0_), channel_id=1, source_target_pairs={{0,4},{4,0},{8,12},{12,8},{1,5},{5,1},{9,13},{13,9},{2,6},{6,2},{1... | collective-permute-start | bytes 786440 | tf_op jit(solution)/shard_map/ppermute | solution.py:358
  20.5 6.4 %collective-permute-start.3 = (bf16[128,1024]{1,0:T(8,128)(2,1)S(1)}, bf16[128,1024]{1,0:T(8,128)(2,1)S(1)}, u32[]{:S(2)}, u32[]{:S(2)}) collective-permute-start(bf16[128,1024]{1,0:T(8,128)(2,1)S(1)} %collective-permute-done.refs_0_), channel_id=1, source_target_pairs={{0,1},{1,0},{2,3},{3,2},{4,5},{5,4},{6,7},{7,6},{8,9},{9,8},{10,11... | collective-permute-start | bytes 786440 | tf_op jit(solution)/shard_map/ppermute | solution.py:38
  25.5 1.6 %collective-permute-start.9 = (bf16[128,1024]{1,0:T(8,128)(2,1)S(1)}, bf16[128,1024]{1,0:T(8,128)(2,1)S(1)}, u32[]{:S(2)}, u32[]{:S(2)}) collective-permute-start(bf16[128,1024]{1,0:T(8,128)(2,1)S(1)} %get-tuple-element.41.refs_2_), channel_id=1, source_target_pairs={{0,1},{1,0},{2,3},{3,2},{4,5},{5,4},{6,7},{7,6},{8,9},{9,8},{10,11... | collective-permute-start | bytes 786440 | tf_op jit(solution)/shard_map/ppermute | solution.py:38
  26.2 9.2 %collective-permute-start.15 = (bf16[128,1024]{1,0:T(8,128)(2,1)S(1)}, bf16[128,1024]{1,0:T(8,128)(2,1)S(1)}, u32[]{:S(2)}, u32[]{:S(2)}) collective-permute-start(bf16[128,1024]{1,0:T(8,128)(2,1)S(1)} %collective-permute-done.13.refs_0_), channel_id=1, source_target_pairs={{0,2},{1,3},{2,0},{3,1},{4,6},{5,7},{6,4},{7,5},{8,10},{9,11},{10,... | collective-permute-start | bytes 786440 | tf_op jit(solution)/shard_map/ppermute | solution.py:38
  26.9 10.7 %collective-permute-start.14 = (bf16[128,1024]{1,0:T(8,128)(2,1)S(1)}, bf16[128,1024]{1,0:T(8,128)(2,1)S(1)}, u32[]{:S(2)}, u32[]{:S(2)}) collective-permute-start(bf16[128,1024]{1,0:T(8,128)(2,1)S(1)} %collective-permute-done.13.refs_0_), channel_id=1, source_target_pairs={{0,1},{1,0},{2,3},{3,2},{4,5},{5,4},{6,7},{7,6},{8,9},{9,8},{10,11... | collective-permute-start | bytes 786440 | tf_op jit(solution)/shard_map/ppermute | solution.py:38
  29.8 10.5 %copy-start.1 = (bf16[1,128,1024]{2,1,0:T(8,128)(2,1)S(1)}, bf16[1,128,1024]{2,1,0:T(8,128)(2,1)}, u32[]{:S(2)}) copy-start(bf16[1,128,1024]{2,1,0:T(8,128)(2,1)} %param.7) | copy-start | bytes 786436
  29.8 10.5 %collective-permute-start.10 = (bf16[128,1024]{1,0:T(8,128)(2,1)S(1)}, bf16[128,1024]{1,0:T(8,128)(2,1)S(1)}, u32[]{:S(2)}, u32[]{:S(2)}) collective-permute-start(bf16[128,1024]{1,0:T(8,128)(2,1)S(1)} %collective-permute-done.5.refs_0_), channel_id=1, source_target_pairs={{0,2},{1,3},{2,0},{3,1},{4,6},{5,7},{6,4},{7,5},{8,10},{9,11},{10,... | collective-permute-start | bytes 786440 | tf_op jit(solution)/shard_map/ppermute | solution.py:38
  31.1 16.2 %collective-permute-start.18 = (bf16[128,1024]{1,0:T(8,128)(2,1)S(1)}, bf16[128,1024]{1,0:T(8,128)(2,1)S(1)}, u32[]{:S(2)}, u32[]{:S(2)}) collective-permute-start(bf16[128,1024]{1,0:T(8,128)(2,1)S(1)} %collective-permute-done.5.refs_0_), channel_id=1, source_target_pairs={{0,1},{1,0},{2,3},{3,2},{4,5},{5,4},{6,7},{7,6},{8,9},{9,8},{10,11... | collective-permute-start | bytes 786440 | tf_op jit(solution)/shard_map/ppermute | solution.py:38
  31.3 23.9 %collective-permute-start.16 = (bf16[128,1024]{1,0:T(8,128)(2,1)S(1)}, bf16[128,1024]{1,0:T(8,128)(2,1)S(1)}, u32[]{:S(2)}, u32[]{:S(2)}) collective-permute-start(bf16[128,1024]{1,0:T(8,128)(2,1)S(1)} %visit_2.1), channel_id=1, source_target_pairs={{0,8},{4,12},{8,0},{12,4},{1,9},{5,13},{9,1},{13,5},{2,10},{6,14},... | collective-permute-start | bytes 786440 | tf_op jit(solution)/shard_map/ppermute | solution.py:361
  40.4 9.7 %collective-permute-start.12 = (bf16[128,1024]{1,0:T(8,128)(2,1)S(1)}, bf16[128,1024]{1,0:T(8,128)(2,1)S(1)}, u32[]{:S(2)}, u32[]{:S(2)}) collective-permute-start(bf16[128,1024]{1,0:T(8,128)(2,1)S(1)} %bitcast.7), channel_id=1, source_target_pairs={{0,2},{1,3},{2,0},{3,1},{4,6},{5,7},{6,4},{7,5},{8,10},{9,11},{10,... | collective-permute-start | bytes 786440 | tf_op jit(solution)/shard_map/ppermute | solution.py:38
  40.9 14.3 %collective-permute-start.17 = (bf16[128,1024]{1,0:T(8,128)(2,1)S(1)}, bf16[128,1024]{1,0:T(8,128)(2,1)S(1)}, u32[]{:S(2)}, u32[]{:S(2)}) collective-permute-start(bf16[128,1024]{1,0:T(8,128)(2,1)S(1)} %visit_3.1), channel_id=1, source_target_pairs={{0,12},{4,8},{8,4},{12,0},{1,13},{5,9},{9,5},{13,1},{2,14},{6,10},... | collective-permute-start | bytes 786440 | tf_op jit(solution)/shard_map/ppermute | solution.py:361
  44.9 7.5 %collective-permute-start.11 = (bf16[128,1024]{1,0:T(8,128)(2,1)S(1)}, bf16[128,1024]{1,0:T(8,128)(2,1)S(1)}, u32[]{:S(2)}, u32[]{:S(2)}) collective-permute-start(bf16[128,1024]{1,0:T(8,128)(2,1)S(1)} %bitcast.8), channel_id=1, source_target_pairs={{0,1},{1,0},{2,3},{3,2},{4,5},{5,4},{6,7},{7,6},{8,9},{9,8},{10,11... | collective-permute-start | bytes 786440 | tf_op jit(solution)/shard_map/ppermute | solution.py:38
  50.0 8.7 %collective-permute-start.19 = (bf16[128,1024]{1,0:T(8,128)(2,1)S(1)}, bf16[128,1024]{1,0:T(8,128)(2,1)S(1)}, u32[]{:S(2)}, u32[]{:S(2)}) collective-permute-start(bf16[128,1024]{1,0:T(8,128)(2,1)S(1)} %visit_1.1), channel_id=1, source_target_pairs={{0,4},{4,0},{8,12},{12,8},{1,5},{5,1},{9,13},{13,9},{2,6},{6,2},{1... | collective-permute-start | bytes 786440 | tf_op jit(solution)/shard_map/ppermute | solution.py:361

commit v5 on v4

--- a/solution.py
+++ b/solution.py
@@ -416,12 +416,13 @@
     context_2 = scored(2, over_cores([shards_2[0], *held], block_1, apart=True))
     home_2 = sent_home(2, context_2)
     shards_1 = over_chips(kept_order(block_1, context_2))
-    shards_0 = over_chips(kept_order(own, context_2, *shards_1[1:]))
-    context_3 = scored(3, over_cores(shards_3, context_2))
+    gathered_3 = over_cores(shards_3, context_2)
+    shards_0 = over_chips(kept_order(own, gathered_3[-1], *shards_1[1:]))
+    context_3 = scored(3, gathered_3)
     home_3 = sent_home(3, context_3)
     context_1 = scored(1, over_cores(shards_1, context_3))
     home_1 = sent_home(1, context_1)
-    context_0 = scored(0, over_cores(shards_0, context_3))
+    context_0 = scored(0, over_cores(shards_0, context_1))
     return mean_of(keep, [context_0, home_2, home_3, home_1])[None]
 
 

time: 59.9 us -> 59.9 us (level)
  no operation moved by 1% of the time
where the time goes in v5:
time: 59.9 us; the launch traced here: 59.6 us
  starting transfers between devices  22.2 us (37%)
  Pallas kernels  17.5 us (29%)
  waiting for transfers between devices  11 us (18%)
  blocking collectives  6.84 us (11%)
  local copies, waits for them, and re-layouts  1.89 us (3%)
    pallas_call x4, Pallas kernels, visit_context(): pl.pallas_call(functools.partial(visit_kernel, parts, len(shards)), out_s...  10.9 us
    ppermute x3, starting transfers between devices, sent_home(): return lax.ppermute(array, 'snap', visit_pairs(snaps, visit, back=True))  7.35 us
    all_gather x3, blocking collectives, over_cores(): lax.all_gather(shard, 'tp', axis=0, tiled=True, axis_index_groups=pairs_o...  6.84 us
    ppermute x12, starting transfers between devices, swapped(): return lax.ppermute(array, 'tp', [(i, i ^ with_bits) for i in range(count)])  6.51 us
    ppermute x3, starting transfers between devices, moved(): return lax.ppermute(block, 'snap', visit_pairs(snaps, visit))  6.28 us
    pallas_call x1, Pallas kernels, staged(): pl.pallas_call(stage_kernel, out_shape=[*(pltpu.VMEM(*each) for each in h...  4.76 us
    ppermute x2, waiting for transfers between devices, on_device(): lax.ppermute(by_league[-1], 'league', [(i, (i + 1) % leagues) for i in ra...  4.15 us
    ppermute x3, waiting for transfers between devices, sent_home(): return lax.ppermute(array, 'snap', visit_pairs(snaps, visit, back=True))  3.44 us
  transfers between devices with their start and end apart: 20, of which 7 were waited for; matrix products, arithmetic and copies ran while one was open for 0% of the time, Pallas kernels for 28%

profile of v5, /device:TPU:0, one launch (start us, length us, event | category | flops | bytes accessed | tf_op | source)
XLA Modules:
  0.0 59.6 jit_solution(9622638664164911599)
XLA Ops:
  0.0 4.0 %collective-permute-start = (bf16[128,1024]{1,0:T(8,128)(2,1)}, bf16[128,1024]{1,0:T(8,128)(2,1)S(1)}, u32[]{:S(2)}, u32[]{:S(2)}) collective-permute-start(bf16[128,1024]{1,0:T(8,128)(2,1)} %bitcast.5), channel_id=1, source_target_pairs={{0,8},{4,12},{8,0},{12,4},{1,9},{5,13},{9,1},{13,5},{2,10},{6,14},... | collective-permute-start | bytes 786440 | tf_op jit(solution)/shard_map/ppermute | solution.py:358
  4.0 1.6 %collective-permute-start.8 = (bf16[128,1024]{1,0:T(8,128)(2,1)}, bf16[128,1024]{1,0:T(8,128)(2,1)S(1)}, u32[]{:S(2)}, u32[]{:S(2)}) collective-permute-start(bf16[128,1024]{1,0:T(8,128)(2,1)} %bitcast.6), channel_id=1, source_target_pairs={{0,4},{4,0},{8,12},{12,8},{1,5},{5,1},{9,13},{13,9},{2,6},{6,2},{1... | collective-permute-start | bytes 786440 | tf_op jit(solution)/shard_map/ppermute | solution.py:358
  5.6 1.2 %copy-done = bf16[1,1024,512]{2,1,0:T(8,128)(2,1)S(1)} copy-done((bf16[1,1024,512]{2,1,0:T(8,128)(2,1)S(1)}, bf16[1,1024,512]{2,1,0:T(8,128)(2,1)}, u32[]{:S(2)}) %copy-start) | copy-done | bytes 1048600
  7.0 1.6 %collective-permute-start.2 = (bf16[512,128]{1,0:T(8,128)(2,1)S(1)}, bf16[512,128]{1,0:T(8,128)(2,1)S(1)}, u32[]{:S(2)}, u32[]{:S(2)}) collective-permute-start(bf16[512,128]{1,0:T(8,128)(2,1)S(1)} %get-tuple-element.33), channel_id=1, source_target_pairs={{0,2},{1,3},{2,0},{3,1},{4,6},{5,7},{6,4},{7,5},{8,10},{9,11},{10,... | collective-permute-start | bytes 393224 | tf_op jit(solution)/shard_map/ppermute | solution.py:38
  9.9 4.8 %stage_weights.1 = (bf16[4,1024,1024]{2,1,0:T(8,128)(2,1)S(1)}, f32[1,4096]{1,0:T(1,128)S(1)}, f32[128,128]{1,0:T(8,128)S(1)}, f32[128,128]{1,0:T(8,128)S(1)}, f...) custom-call(s32[4]{0:T(128)S(1)} %copy-done.2, ...), custom_call_target="tpu_custom_call" | custom-call | tf_op jit(solution)/shard_map/stage_weights/pallas_call | solution.py:241
  14.6 1.6 %collective-permute-done.refs_0_ = bf16[128,1024]{1,0:T(8,128)(2,1)S(1)} collective-permute-done((bf16[128,1024]{1,0:T(8,128)(2,1)}, bf16[128,1024]{1,0:T(8,128)(2,1)S(1)}, u32[]{:S(2)}, u32[]{:S(2)}) %collective-permute-start) | collective-permute-done | bytes 262176 | tf_op jit(solution)/shard_map/ppermute | solution.py:358
  16.3 1.5 %collective-permute-start.4 = (bf16[128,1024]{1,0:T(8,128)(2,1)S(1)}, bf16[128,1024]{1,0:T(8,128)(2,1)S(1)}, u32[]{:S(2)}, u32[]{:S(2)}) collective-permute-start(bf16[128,1024]{1,0:T(8,128)(2,1)S(1)} %collective-permute-done.refs_0_), channel_id=1, source_target_pairs={{0,2},{1,3},{2,0},{3,1},{4,6},{5,7},{6,4},{7,5},{8,10},{9,11},{10,... | collective-permute-start | bytes 786440 | tf_op jit(solution)/shard_map/ppermute | solution.py:38
  17.8 1.5 %collective-permute-start.10 = (bf16[512,128]{1,0:T(8,128)(2,1)S(1)}, bf16[512,128]{1,0:T(8,128)(2,1)S(1)}, u32[]{:S(2)}, u32[]{:S(2)}) collective-permute-start(bf16[512,128]{1,0:T(8,128)(2,1)S(1)} %collective-permute-done.3.refs_4_), channel_id=1, source_target_pairs={{0,16},{16,0},{1,17},{17,1},{2,18},{18,2},{3,19},{19,3},{4,20},{20... | collective-permute-start | bytes 393224 | tf_op jit(solution)/shard_map/ppermute | solution.py:383
  20.5 2.7 %collective-permute-done.10.refs_5_ = bf16[512,128]{1,0:T(8,128)(2,1)S(1)} collective-permute-done((bf16[512,128]{1,0:T(8,128)(2,1)S(1)}, bf16[512,128]{1,0:T(8,128)(2,1)S(1)}, u32[]{:S(2)}, u32[]{:S(2)}) %collective-permute-start.10) | collective-permute-done | bytes 131104 | tf_op jit(solution)/shard_map/ppermute | solution.py:383
  23.3 1.4 %collective-permute-done.9.refs_3_ = bf16[512,128]{1,0:T(8,128)(2,1)S(1)} collective-permute-done((bf16[512,128]{1,0:T(8,128)(2,1)S(1)}, bf16[512,128]{1,0:T(8,128)(2,1)S(1)}, u32[]{:S(2)}, u32[]{:S(2)}) %collective-permute-start.9) | collective-permute-done | bytes 131104 | tf_op jit(solution)/shard_map/ppermute | solution.py:383
  24.7 0.8 %join_keyval.1 = (bf16[4,1024,128]{2,1,0:T(8,128)(2,1)S(1)}, bf16[128,1024]{1,0:T(8,128)(2,1)S(1)}) custom-call(bf16[1024,128]{1,0:T(8,128)(2,1)S(1)} %get-tuple-element.37.refs_0_, bf16[1024,128]{1,0:T(8,128)(2,1)S(1)} %collective-permute-done.7.refs_1_, bf16[512,128]{1,0:T(8,128)(2,1)S(1)} %collective-permute-done.2.refs_2_, ...), custom_call_target="tpu_custom_call" | custom-call | tf_op jit(solution)/shard_map/join_keyval/pallas_call | solution.py:328
  27.1 2.7 %visit_2.1 = bf16[128,1024]{1,0:T(8,128)(2,1)S(1)} custom-call(bf16[128,1024]{1,0:T(8,128)(2,1)S(1)} %collective-permute-done.refs_0_, bf16[128,1024]{1,0:T(8,128)(2,1)S(1)} %collective-permute-done.6.refs_1_, bf16[128,1024]{1,0:T(8,128)(2,1)S(1)} %get-tuple-element.42.refs_2_, bf16[128,1024]{1,0:T(8,128)(2,1)S(1)} %collective-permute-done.11.refs_3_, ...), custom_call_target="tpu_custom_call" | custom-call | flops 1 | bytes 1 | tf_op jit(solution)/shard_map/visit_2/pallas_call | solution.py:149
  29.8 1.2 %collective-permute-start.12 = (bf16[128,1024]{1,0:T(8,128)(2,1)S(1)}, bf16[128,1024]{1,0:T(8,128)(2,1)S(1)}, u32[]{:S(2)}, u32[]{:S(2)}) collective-permute-start(bf16[128,1024]{1,0:T(8,128)(2,1)S(1)} %collective-permute-done.8.refs_0_), channel_id=1, source_target_pairs={{0,2},{1,3},{2,0},{3,1},{4,6},{5,7},{6,4},{7,5},{8,10},{9,11},{10,... | collective-permute-start | bytes 786440 | tf_op jit(solution)/shard_map/ppermute | solution.py:38
  31.3 3.2 %collective-permute-start.17 = (bf16[128,1024]{1,0:T(8,128)(2,1)S(1)}, bf16[128,1024]{1,0:T(8,128)(2,1)S(1)}, u32[]{:S(2)}, u32[]{:S(2)}) collective-permute-start(bf16[128,1024]{1,0:T(8,128)(2,1)S(1)} %visit_2.1), channel_id=1, source_target_pairs={{0,8},{4,12},{8,0},{12,4},{1,9},{5,13},{9,1},{13,5},{2,10},{6,14},... | collective-permute-start | bytes 786440 | tf_op jit(solution)/shard_map/ppermute | solution.py:361
  34.5 0.9 %collective-permute-done.5 = bf16[128,1024]{1,0:T(8,128)(2,1)S(1)} collective-permute-done((bf16[128,1024]{1,0:T(8,128)(2,1)S(1)}, bf16[128,1024]{1,0:T(8,128)(2,1)S(1)}, u32[]{:S(2)}, u32[]{:S(2)}) %collective-permute-start.5) | collective-permute-done | bytes 262176 | tf_op jit(solution)/shard_map/ppermute | solution.py:38
  35.4 2.2 %all_gather.9.refs_2_ = bf16[256,1024]{1,0:T(8,128)(2,1)S(1)} all-gather(bf16[128,1024]{1,0:T(8,128)(2,1)S(1)} %collective-permute-done.5), channel_id=1, replica_groups={{0,1},{2,3},{4,5},{6,7},{8,9},{10,11},{12,13},{14,15},{16,17},{18,19},{..., dimensions={0}, use_global_device_ids=true | all-gather | bytes 786432 | tf_op jit(solution)/shard_map/all_gather | solution.py:403
  37.6 2.7 %visit_3.1 = bf16[128,1024]{1,0:T(8,128)(2,1)S(1)} custom-call(bf16[128,1024]{1,0:T(8,128)(2,1)S(1)} %collective-permute-done.1.refs_0_, bf16[128,1024]{1,0:T(8,128)(2,1)S(1)} %collective-permute-done.16.refs_1_, bf16[256,1024]{1,0:T(8,128)(2,1)S(1)} %all_gather.9.refs_2_, f32[1,4096]{1,0:T(1,128)S(1)} %get-tuple-element.43.refs_4_.refs_3_, ...), custom_call_target="tpu_custom_call" | custom-call | flops 1 | bytes 1 | tf_op jit(solution)/shard_map/visit_3/pallas_call | solution.py:149
  40.9 4.1 %collective-permute-start.18 = (bf16[128,1024]{1,0:T(8,128)(2,1)S(1)}, bf16[128,1024]{1,0:T(8,128)(2,1)S(1)}, u32[]{:S(2)}, u32[]{:S(2)}) collective-permute-start(bf16[128,1024]{1,0:T(8,128)(2,1)S(1)} %visit_3.1), channel_id=1, source_target_pairs={{0,12},{4,8},{8,4},{12,0},{1,13},{5,9},{9,5},{13,1},{2,14},{6,10},... | collective-permute-start | bytes 786440 | tf_op jit(solution)/shard_map/ppermute | solution.py:361
  44.9 2.3 %all_gather.10.refs_2_ = bf16[256,1024]{1,0:T(8,128)(2,1)S(1)} all-gather(bf16[128,1024]{1,0:T(8,128)(2,1)S(1)} %collective-permute-done.12), channel_id=1, replica_groups={{0,1},{2,3},{4,5},{6,7},{8,9},{10,11},{12,13},{14,15},{16,17},{18,19},{..., dimensions={0}, use_global_device_ids=true | all-gather | bytes 786432 | tf_op jit(solution)/shard_map/all_gather | solution.py:403
  47.2 2.7 %visit_1.1 = bf16[128,1024]{1,0:T(8,128)(2,1)S(1)} custom-call(bf16[128,1024]{1,0:T(8,128)(2,1)S(1)} %collective-permute-done.8.refs_0_, bf16[128,1024]{1,0:T(8,128)(2,1)S(1)} %collective-permute-done.15.refs_1_, bf16[256,1024]{1,0:T(8,128)(2,1)S(1)} %all_gather.10.refs_2_, f32[1,4096]{1,0:T(1,128)S(1)} %get-tuple-element.43.refs_4_.refs_3_, ...), custom_call_target="tpu_custom_call" | custom-call | flops 1 | bytes 1 | tf_op jit(solution)/shard_map/visit_1/pallas_call | solution.py:149
  50.1 2.4 %all_gather.11.refs_2_ = bf16[256,1024]{1,0:T(8,128)(2,1)S(1)} all-gather(bf16[128,1024]{1,0:T(8,128)(2,1)S(1)} %collective-permute-done.14), channel_id=1, replica_groups={{0,1},{2,3},{4,5},{6,7},{8,9},{10,11},{12,13},{14,15},{16,17},{18,19},{..., dimensions={0}, use_global_device_ids=true | all-gather | bytes 786432 | tf_op jit(solution)/shard_map/all_gather | solution.py:403
  52.4 2.7 %visit_0.1.refs_0_ = bf16[128,1024]{1,0:T(8,128)(2,1)S(1)} custom-call(bf16[128,1024]{1,0:T(8,128)(2,1)S(1)} %bitcast.9, bf16[128,1024]{1,0:T(8,128)(2,1)S(1)} %collective-permute-done.13.refs_1_, bf16[256,1024]{1,0:T(8,128)(2,1)S(1)} %all_gather.11.refs_2_, f32[1,4096]{1,0:T(1,128)S(1)} %get-tuple-element.43.refs_4_.refs_3_, ...), custom_call_target="tpu_custom_call" | custom-call | flops 1 | bytes 1 | tf_op jit(solution)/shard_map/visit_0/pallas_call | solution.py:149
  55.2 3.4 %collective-permute-done.19.refs_3_ = bf16[128,1024]{1,0:T(8,128)(2,1)S(1)} collective-permute-done((bf16[128,1024]{1,0:T(8,128)(2,1)S(1)}, bf16[128,1024]{1,0:T(8,128)(2,1)S(1)}, u32[]{:S(2)}, u32[]{:S(2)}) %collective-permute-start.19) | collective-permute-done | bytes 262176 | tf_op jit(solution)/shard_map/ppermute | solution.py:361
  58.6 0.8 %mean_of_visits.1 = bf16[128,1024]{1,0:T(8,128)(2,1)} custom-call(f32[128,128]{1,0:T(8,128)S(1)} %get-tuple-element.31.keep_ref, bf16[128,1024]{1,0:T(8,128)(2,1)S(1)} %visit_0.1.refs_0_, bf16[128,1024]{1,0:T(8,128)(2,1)S(1)} %collective-permute-done.17.refs_1_, bf16[128,1024]{1,0:T(8,128)(2,1)S(1)} %collective-permute-done.18.refs_2_, ...), custom_call_target="tpu_custom_call" | custom-call | tf_op jit(solution)/shard_map/mean_of_visits/pallas_call | solution.py:190
  (33 shorter events, 5.1 us)
Async XLA Ops:
  0.0 16.3 %collective-permute-start = (bf16[128,1024]{1,0:T(8,128)(2,1)}, bf16[128,1024]{1,0:T(8,128)(2,1)S(1)}, u32[]{:S(2)}, u32[]{:S(2)}) collective-permute-start(bf16[128,1024]{1,0:T(8,128)(2,1)} %bitcast.5), channel_id=1, source_target_pairs={{0,8},{4,12},{8,0},{12,4},{1,9},{5,13},{9,1},{13,5},{2,10},{6,14},... | collective-permute-start | bytes 786440 | tf_op jit(solution)/shard_map/ppermute | solution.py:358
  4.0 13.8 %collective-permute-start.8 = (bf16[128,1024]{1,0:T(8,128)(2,1)}, bf16[128,1024]{1,0:T(8,128)(2,1)S(1)}, u32[]{:S(2)}, u32[]{:S(2)}) collective-permute-start(bf16[128,1024]{1,0:T(8,128)(2,1)} %bitcast.6), channel_id=1, source_target_pairs={{0,4},{4,0},{8,12},{12,8},{1,5},{5,1},{9,13},{13,9},{2,6},{6,2},{1... | collective-permute-start | bytes 786440 | tf_op jit(solution)/shard_map/ppermute | solution.py:358
  5.6 1.2 %copy-start = (bf16[1,1024,512]{2,1,0:T(8,128)(2,1)S(1)}, bf16[1,1024,512]{2,1,0:T(8,128)(2,1)}, u32[]{:S(2)}) copy-start(bf16[1,1024,512]{2,1,0:T(8,128)(2,1)} %param.11) | copy-start | bytes 3145732
  7.0 7.6 %collective-permute-start.2 = (bf16[512,128]{1,0:T(8,128)(2,1)S(1)}, bf16[512,128]{1,0:T(8,128)(2,1)S(1)}, u32[]{:S(2)}, u32[]{:S(2)}) collective-permute-start(bf16[512,128]{1,0:T(8,128)(2,1)S(1)} %get-tuple-element.33), channel_id=1, source_target_pairs={{0,2},{1,3},{2,0},{3,1},{4,6},{5,7},{6,4},{7,5},{8,10},{9,11},{10,... | collective-permute-start | bytes 393224 | tf_op jit(solution)/shard_map/ppermute | solution.py:38
  8.6 6.1 %collective-permute-start.3 = (bf16[512,128]{1,0:T(8,128)(2,1)S(1)}, bf16[512,128]{1,0:T(8,128)(2,1)S(1)}, u32[]{:S(2)}, u32[]{:S(2)}) collective-permute-start(bf16[512,128]{1,0:T(8,128)(2,1)S(1)} %get-tuple-element.34), channel_id=1, source_target_pairs={{0,3},{1,2},{2,1},{3,0},{4,7},{5,6},{6,5},{7,4},{8,11},{9,10},{10,... | collective-permute-start | bytes 393224 | tf_op jit(solution)/shard_map/ppermute | solution.py:38
  8.6 12.0 %collective-permute-start.7 = (bf16[1024,128]{1,0:T(8,128)(2,1)S(1)}, bf16[1024,128]{1,0:T(8,128)(2,1)S(1)}, u32[]{:S(2)}, u32[]{:S(2)}) collective-permute-start(bf16[1024,128]{1,0:T(8,128)(2,1)S(1)} %get-tuple-element.38), channel_id=1, source_target_pairs={{0,1},{1,0},{2,3},{3,2},{4,5},{5,4},{6,7},{7,6},{8,9},{9,8},{10,11... | collective-permute-start | bytes 786440 | tf_op jit(solution)/shard_map/ppermute | solution.py:38
  9.2 0.7 %copy-start.2 = (s32[4]{0:T(128)S(1)}, s32[4]{0:T(128)}, u32[]{:S(2)}) copy-start(s32[4]{0:T(128)} %lengths_ref.1) | copy-start | bytes 52
  16.3 8.4 %collective-permute-start.4 = (bf16[128,1024]{1,0:T(8,128)(2,1)S(1)}, bf16[128,1024]{1,0:T(8,128)(2,1)S(1)}, u32[]{:S(2)}, u32[]{:S(2)}) collective-permute-start(bf16[128,1024]{1,0:T(8,128)(2,1)S(1)} %collective-permute-done.refs_0_), channel_id=1, source_target_pairs={{0,2},{1,3},{2,0},{3,1},{4,6},{5,7},{6,4},{7,5},{8,10},{9,11},{10,... | collective-permute-start | bytes 786440 | tf_op jit(solution)/shard_map/ppermute | solution.py:38
  17.8 5.5 %collective-permute-start.10 = (bf16[512,128]{1,0:T(8,128)(2,1)S(1)}, bf16[512,128]{1,0:T(8,128)(2,1)S(1)}, u32[]{:S(2)}, u32[]{:S(2)}) collective-permute-start(bf16[512,128]{1,0:T(8,128)(2,1)S(1)} %collective-permute-done.3.refs_4_), channel_id=1, source_target_pairs={{0,16},{16,0},{1,17},{17,1},{2,18},{18,2},{3,19},{19,3},{4,20},{20... | collective-permute-start | bytes 393224 | tf_op jit(solution)/shard_map/ppermute | solution.py:383
  19.3 5.3 %collective-permute-start.9 = (bf16[512,128]{1,0:T(8,128)(2,1)S(1)}, bf16[512,128]{1,0:T(8,128)(2,1)S(1)}, u32[]{:S(2)}, u32[]{:S(2)}) collective-permute-start(bf16[512,128]{1,0:T(8,128)(2,1)S(1)} %collective-permute-done.2.refs_2_), channel_id=1, source_target_pairs={{0,16},{16,0},{1,17},{17,1},{2,18},{18,2},{3,19},{19,3},{4,20},{20... | collective-permute-start | bytes 393224 | tf_op jit(solution)/shard_map/ppermute | solution.py:383
  19.8 6.4 %collective-permute-start.1 = (bf16[128,1024]{1,0:T(8,128)(2,1)S(1)}, bf16[128,1024]{1,0:T(8,128)(2,1)S(1)}, u32[]{:S(2)}, u32[]{:S(2)}) collective-permute-start(bf16[128,1024]{1,0:T(8,128)(2,1)S(1)} %collective-permute-done.refs_0_), channel_id=1, source_target_pairs={{0,4},{4,0},{8,12},{12,8},{1,5},{5,1},{9,13},{13,9},{2,6},{6,2},{1... | collective-permute-start | bytes 786440 | tf_op jit(solution)/shard_map/ppermute | solution.py:358
  20.5 6.4 %collective-permute-start.6 = (bf16[128,1024]{1,0:T(8,128)(2,1)S(1)}, bf16[128,1024]{1,0:T(8,128)(2,1)S(1)}, u32[]{:S(2)}, u32[]{:S(2)}) collective-permute-start(bf16[128,1024]{1,0:T(8,128)(2,1)S(1)} %collective-permute-done.refs_0_), channel_id=1, source_target_pairs={{0,1},{1,0},{2,3},{3,2},{4,5},{5,4},{6,7},{7,6},{8,9},{9,8},{10,11... | collective-permute-start | bytes 786440 | tf_op jit(solution)/shard_map/ppermute | solution.py:38
  25.5 1.6 %collective-permute-start.11 = (bf16[128,1024]{1,0:T(8,128)(2,1)S(1)}, bf16[128,1024]{1,0:T(8,128)(2,1)S(1)}, u32[]{:S(2)}, u32[]{:S(2)}) collective-permute-start(bf16[128,1024]{1,0:T(8,128)(2,1)S(1)} %get-tuple-element.42.refs_2_), channel_id=1, source_target_pairs={{0,1},{1,0},{2,3},{3,2},{4,5},{5,4},{6,7},{7,6},{8,9},{9,8},{10,11... | collective-permute-start | bytes 786440 | tf_op jit(solution)/shard_map/ppermute | solution.py:38
  26.2 9.2 %collective-permute-start.5 = (bf16[128,1024]{1,0:T(8,128)(2,1)S(1)}, bf16[128,1024]{1,0:T(8,128)(2,1)S(1)}, u32[]{:S(2)}, u32[]{:S(2)}) collective-permute-start(bf16[128,1024]{1,0:T(8,128)(2,1)S(1)} %collective-permute-done.1.refs_0_), channel_id=1, source_target_pairs={{0,2},{1,3},{2,0},{3,1},{4,6},{5,7},{6,4},{7,5},{8,10},{9,11},{10,... | collective-permute-start | bytes 786440 | tf_op jit(solution)/shard_map/ppermute | solution.py:38
  26.9 10.7 %collective-permute-start.16 = (bf16[128,1024]{1,0:T(8,128)(2,1)S(1)}, bf16[128,1024]{1,0:T(8,128)(2,1)S(1)}, u32[]{:S(2)}, u32[]{:S(2)}) collective-permute-start(bf16[128,1024]{1,0:T(8,128)(2,1)S(1)} %collective-permute-done.1.refs_0_), channel_id=1, source_target_pairs={{0,1},{1,0},{2,3},{3,2},{4,5},{5,4},{6,7},{7,6},{8,9},{9,8},{10,11... | collective-permute-start | bytes 786440 | tf_op jit(solution)/shard_map/ppermute | solution.py:38
  29.8 10.5 %copy-start.1 = (bf16[1,128,1024]{2,1,0:T(8,128)(2,1)S(1)}, bf16[1,128,1024]{2,1,0:T(8,128)(2,1)}, u32[]{:S(2)}) copy-start(bf16[1,128,1024]{2,1,0:T(8,128)(2,1)} %param.7) | copy-start | bytes 786436
  29.8 10.5 %collective-permute-start.12 = (bf16[128,1024]{1,0:T(8,128)(2,1)S(1)}, bf16[128,1024]{1,0:T(8,128)(2,1)S(1)}, u32[]{:S(2)}, u32[]{:S(2)}) collective-permute-start(bf16[128,1024]{1,0:T(8,128)(2,1)S(1)} %collective-permute-done.8.refs_0_), channel_id=1, source_target_pairs={{0,2},{1,3},{2,0},{3,1},{4,6},{5,7},{6,4},{7,5},{8,10},{9,11},{10,... | collective-permute-start | bytes 786440 | tf_op jit(solution)/shard_map/ppermute | solution.py:38
  31.1 16.2 %collective-permute-start.15 = (bf16[128,1024]{1,0:T(8,128)(2,1)S(1)}, bf16[128,1024]{1,0:T(8,128)(2,1)S(1)}, u32[]{:S(2)}, u32[]{:S(2)}) collective-permute-start(bf16[128,1024]{1,0:T(8,128)(2,1)S(1)} %collective-permute-done.8.refs_0_), channel_id=1, source_target_pairs={{0,1},{1,0},{2,3},{3,2},{4,5},{5,4},{6,7},{7,6},{8,9},{9,8},{10,11... | collective-permute-start | bytes 786440 | tf_op jit(solution)/shard_map/ppermute | solution.py:38
  31.3 23.9 %collective-permute-start.17 = (bf16[128,1024]{1,0:T(8,128)(2,1)S(1)}, bf16[128,1024]{1,0:T(8,128)(2,1)S(1)}, u32[]{:S(2)}, u32[]{:S(2)}) collective-permute-start(bf16[128,1024]{1,0:T(8,128)(2,1)S(1)} %visit_2.1), channel_id=1, source_target_pairs={{0,8},{4,12},{8,0},{12,4},{1,9},{5,13},{9,1},{13,5},{2,10},{6,14},... | collective-permute-start | bytes 786440 | tf_op jit(solution)/shard_map/ppermute | solution.py:361
  40.4 9.7 %collective-permute-start.14 = (bf16[128,1024]{1,0:T(8,128)(2,1)S(1)}, bf16[128,1024]{1,0:T(8,128)(2,1)S(1)}, u32[]{:S(2)}, u32[]{:S(2)}) collective-permute-start(bf16[128,1024]{1,0:T(8,128)(2,1)S(1)} %bitcast.7), channel_id=1, source_target_pairs={{0,2},{1,3},{2,0},{3,1},{4,6},{5,7},{6,4},{7,5},{8,10},{9,11},{10,... | collective-permute-start | bytes 786440 | tf_op jit(solution)/shard_map/ppermute | solution.py:38
  40.9 14.3 %collective-permute-start.18 = (bf16[128,1024]{1,0:T(8,128)(2,1)S(1)}, bf16[128,1024]{1,0:T(8,128)(2,1)S(1)}, u32[]{:S(2)}, u32[]{:S(2)}) collective-permute-start(bf16[128,1024]{1,0:T(8,128)(2,1)S(1)} %visit_3.1), channel_id=1, source_target_pairs={{0,12},{4,8},{8,4},{12,0},{1,13},{5,9},{9,5},{13,1},{2,14},{6,10},... | collective-permute-start | bytes 786440 | tf_op jit(solution)/shard_map/ppermute | solution.py:361
  44.9 7.5 %collective-permute-start.13 = (bf16[128,1024]{1,0:T(8,128)(2,1)S(1)}, bf16[128,1024]{1,0:T(8,128)(2,1)S(1)}, u32[]{:S(2)}, u32[]{:S(2)}) collective-permute-start(bf16[128,1024]{1,0:T(8,128)(2,1)S(1)} %bitcast.8), channel_id=1, source_target_pairs={{0,1},{1,0},{2,3},{3,2},{4,5},{5,4},{6,7},{7,6},{8,9},{9,8},{10,11... | collective-permute-start | bytes 786440 | tf_op jit(solution)/shard_map/ppermute | solution.py:38
  50.0 8.7 %collective-permute-start.19 = (bf16[128,1024]{1,0:T(8,128)(2,1)S(1)}, bf16[128,1024]{1,0:T(8,128)(2,1)S(1)}, u32[]{:S(2)}, u32[]{:S(2)}) collective-permute-start(bf16[128,1024]{1,0:T(8,128)(2,1)S(1)} %visit_1.1), channel_id=1, source_target_pairs={{0,4},{4,0},{8,12},{12,8},{1,5},{5,1},{9,13},{13,9},{2,6},{6,2},{1... | collective-permute-start | bytes 786440 | tf_op jit(solution)/shard_map/ppermute | solution.py:361

commit v6 on v5

--- a/solution.py
+++ b/solution.py
@@ -182,6 +182,28 @@
         leaving[-1].start()
     for copy in leaving:
         copy.wait()
+
+
+def early_kernel(*refs):
+    terms, out_ref = refs[:-1], refs[-1]
+    total = terms[0][...].astype(jnp.float32)
+    for term in terms[1:]:
+        total += term[...].astype(jnp.float32)
+    out_ref[...] = total
+
+
+def early_sum(terms):
+    vmem = pl.BlockSpec(memory_space=pltpu.VMEM)
+    operands = [pltpu.with_memory_space_constraint(term, pltpu.VMEM) for term in terms]
+    return pl.pallas_call(
+        early_kernel,
+        out_shape=pltpu.VMEM(terms[0].shape, jnp.float32),
+        in_specs=[vmem] * len(operands),
+        out_specs=vmem,
+        compiler_params=pltpu.CompilerParams(vmem_limit_bytes=VMEM_LIMIT),
+        cost_estimate=pl.CostEstimate(flops=1, bytes_accessed=1, transcendentals=0),
+        name="early_sum",
+    )(*operands)
 
 
 def mean_of(keep, terms):
@@ -423,7 +445,7 @@
     context_1 = scored(1, over_cores(shards_1, context_3))
     home_1 = sent_home(1, context_1)
     context_0 = scored(0, over_cores(shards_0, context_1))
-    return mean_of(keep, [context_0, home_2, home_3, home_1])[None]
+    return mean_of(keep, [home_1, early_sum([context_0, home_2, home_3])])[None]
 
 
 def solution(mesh):

time: 59.9 us -> 62.6 us (1.045)
  waiting for transfers between devices: 11 us -> 12.9 us
  starting transfers between devices: 22.2 us -> 22.9 us
    ppermute x12, waiting for transfers between devices: 1.08 us -> 3.13 us  [swapped(): return lax.ppermute(array, 'tp', [(i, i ^ with_bits) for i in range(count)])]
  transfers between devices with their start and end apart: 20 -> 20, of which waited for: 7 -> 8; matrix products, arithmetic and copies ran while one was open for 0% -> 0% of each run, Pallas kernels for 28% -> 27%
where the time goes in v6:
time: 62.6 us; the launch traced here: 62.4 us
  starting transfers between devices  22.9 us (37%)
  Pallas kernels  17.5 us (28%)
  waiting for transfers between devices  12.9 us (21%)
  blocking collectives  6.84 us (11%)
  local copies, waits for them, and re-layouts  1.89 us (3%)
    pallas_call x4, Pallas kernels, visit_context(): pl.pallas_call(functools.partial(visit_kernel, parts, len(shards)), out_s...  10.9 us
    ppermute x3, starting transfers between devices, sent_home(): return lax.ppermute(array, 'snap', visit_pairs(snaps, visit, back=True))  7.59 us
    ppermute x12, starting transfers between devices, swapped(): return lax.ppermute(array, 'tp', [(i, i ^ with_bits) for i in range(count)])  7.04 us
    all_gather x3, blocking collectives, over_cores(): lax.all_gather(shard, 'tp', axis=0, tiled=True, axis_index_groups=pairs_o...  6.84 us
    ppermute x3, starting transfers between devices, moved(): return lax.ppermute(block, 'snap', visit_pairs(snaps, visit))  6.28 us
    pallas_call x1, Pallas kernels, staged(): pl.pallas_call(stage_kernel, out_shape=[*(pltpu.VMEM(*each) for each in h...  4.76 us
    ppermute x2, waiting for transfers between devices, on_device(): lax.ppermute(by_league[-1], 'league', [(i, (i + 1) % leagues) for i in ra...  4.15 us
    ppermute x3, waiting for transfers between devices, sent_home(): return lax.ppermute(array, 'snap', visit_pairs(snaps, visit, back=True))  3.34 us
  transfers between devices with their start and end apart: 20, of which 8 were waited for; matrix products, arithmetic and copies ran while one was open for 0% of the time, Pallas kernels for 27%

profile of v6, /device:TPU:0, one launch (start us, length us, event | category | flops | bytes accessed | tf_op | source)
XLA Modules:
  0.0 62.4 jit_solution(913815619435141967)
XLA Ops:
  0.0 4.0 %collective-permute-start.1 = (bf16[128,1024]{1,0:T(8,128)(2,1)}, bf16[128,1024]{1,0:T(8,128)(2,1)S(1)}, u32[]{:S(2)}, u32[]{:S(2)}) collective-permute-start(bf16[128,1024]{1,0:T(8,128)(2,1)} %bitcast.5), channel_id=1, source_target_pairs={{0,8},{4,12},{8,0},{12,4},{1,9},{5,13},{9,1},{13,5},{2,10},{6,14},... | collective-permute-start | bytes 786440 | tf_op jit(solution)/shard_map/ppermute | solution.py:380
  4.0 1.6 %collective-permute-start = (bf16[128,1024]{1,0:T(8,128)(2,1)}, bf16[128,1024]{1,0:T(8,128)(2,1)S(1)}, u32[]{:S(2)}, u32[]{:S(2)}) collective-permute-start(bf16[128,1024]{1,0:T(8,128)(2,1)} %bitcast.6), channel_id=1, source_target_pairs={{0,4},{4,0},{8,12},{12,8},{1,5},{5,1},{9,13},{13,9},{2,6},{6,2},{1... | collective-permute-start | bytes 786440 | tf_op jit(solution)/shard_map/ppermute | solution.py:380
  5.6 1.2 %copy-done = bf16[1,1024,512]{2,1,0:T(8,128)(2,1)S(1)} copy-done((bf16[1,1024,512]{2,1,0:T(8,128)(2,1)S(1)}, bf16[1,1024,512]{2,1,0:T(8,128)(2,1)}, u32[]{:S(2)}) %copy-start) | copy-done | bytes 1048600
  7.0 1.6 %collective-permute-start.2 = (bf16[512,128]{1,0:T(8,128)(2,1)S(1)}, bf16[512,128]{1,0:T(8,128)(2,1)S(1)}, u32[]{:S(2)}, u32[]{:S(2)}) collective-permute-start(bf16[512,128]{1,0:T(8,128)(2,1)S(1)} %get-tuple-element.33), channel_id=1, source_target_pairs={{0,2},{1,3},{2,0},{3,1},{4,6},{5,7},{6,4},{7,5},{8,10},{9,11},{10,... | collective-permute-start | bytes 393224 | tf_op jit(solution)/shard_map/ppermute | solution.py:38
  9.9 4.8 %stage_weights.1 = (bf16[4,1024,1024]{2,1,0:T(8,128)(2,1)S(1)}, f32[1,4096]{1,0:T(1,128)S(1)}, f32[128,128]{1,0:T(8,128)S(1)}, f32[128,128]{1,0:T(8,128)S(1)}, f...) custom-call(s32[4]{0:T(128)S(1)} %copy-done.2, ...), custom_call_target="tpu_custom_call" | custom-call | tf_op jit(solution)/shard_map/stage_weights/pallas_call | solution.py:263
  14.7 1.6 %collective-permute-done.1.refs_0_ = bf16[128,1024]{1,0:T(8,128)(2,1)S(1)} collective-permute-done((bf16[128,1024]{1,0:T(8,128)(2,1)}, bf16[128,1024]{1,0:T(8,128)(2,1)S(1)}, u32[]{:S(2)}, u32[]{:S(2)}) %collective-permute-start.1) | collective-permute-done | bytes 262176 | tf_op jit(solution)/shard_map/ppermute | solution.py:380
  16.3 1.5 %collective-permute-start.8 = (bf16[128,1024]{1,0:T(8,128)(2,1)S(1)}, bf16[128,1024]{1,0:T(8,128)(2,1)S(1)}, u32[]{:S(2)}, u32[]{:S(2)}) collective-permute-start(bf16[128,1024]{1,0:T(8,128)(2,1)S(1)} %collective-permute-done.1.refs_0_), channel_id=1, source_target_pairs={{0,2},{1,3},{2,0},{3,1},{4,6},{5,7},{6,4},{7,5},{8,10},{9,11},{10,... | collective-permute-start | bytes 786440 | tf_op jit(solution)/shard_map/ppermute | solution.py:38
  17.8 1.5 %collective-permute-start.6 = (bf16[512,128]{1,0:T(8,128)(2,1)S(1)}, bf16[512,128]{1,0:T(8,128)(2,1)S(1)}, u32[]{:S(2)}, u32[]{:S(2)}) collective-permute-start(bf16[512,128]{1,0:T(8,128)(2,1)S(1)} %collective-permute-done.2.refs_2_), channel_id=1, source_target_pairs={{0,16},{16,0},{1,17},{17,1},{2,18},{18,2},{3,19},{19,3},{4,20},{20... | collective-permute-start | bytes 393224 | tf_op jit(solution)/shard_map/ppermute | solution.py:405
  20.5 2.7 %collective-permute-done.6.refs_3_ = bf16[512,128]{1,0:T(8,128)(2,1)S(1)} collective-permute-done((bf16[512,128]{1,0:T(8,128)(2,1)S(1)}, bf16[512,128]{1,0:T(8,128)(2,1)S(1)}, u32[]{:S(2)}, u32[]{:S(2)}) %collective-permute-start.6) | collective-permute-done | bytes 131104 | tf_op jit(solution)/shard_map/ppermute | solution.py:405
  23.3 1.4 %collective-permute-done.7.refs_5_ = bf16[512,128]{1,0:T(8,128)(2,1)S(1)} collective-permute-done((bf16[512,128]{1,0:T(8,128)(2,1)S(1)}, bf16[512,128]{1,0:T(8,128)(2,1)S(1)}, u32[]{:S(2)}, u32[]{:S(2)}) %collective-permute-start.7) | collective-permute-done | bytes 131104 | tf_op jit(solution)/shard_map/ppermute | solution.py:405
  24.7 0.8 %join_keyval.1 = (bf16[4,1024,128]{2,1,0:T(8,128)(2,1)S(1)}, bf16[128,1024]{1,0:T(8,128)(2,1)S(1)}) custom-call(bf16[1024,128]{1,0:T(8,128)(2,1)S(1)} %get-tuple-element.36.refs_0_, bf16[1024,128]{1,0:T(8,128)(2,1)S(1)} %collective-permute-done.5.refs_1_, bf16[512,128]{1,0:T(8,128)(2,1)S(1)} %collective-permute-done.2.refs_2_, ...), custom_call_target="tpu_custom_call" | custom-call | tf_op jit(solution)/shard_map/join_keyval/pallas_call | solution.py:350
  27.1 2.7 %visit_2.1 = bf16[128,1024]{1,0:T(8,128)(2,1)S(1)} custom-call(bf16[128,1024]{1,0:T(8,128)(2,1)S(1)} %collective-permute-done.1.refs_0_, bf16[128,1024]{1,0:T(8,128)(2,1)S(1)} %collective-permute-done.4.refs_1_, bf16[128,1024]{1,0:T(8,128)(2,1)S(1)} %get-tuple-element.41.refs_2_, bf16[128,1024]{1,0:T(8,128)(2,1)S(1)} %collective-permute-done.9.refs_3_, ...), custom_call_target="tpu_custom_call" | custom-call | flops 1 | bytes 1 | tf_op jit(solution)/shard_map/visit_2/pallas_call | solution.py:149
  29.8 1.2 %collective-permute-start.11 = (bf16[128,1024]{1,0:T(8,128)(2,1)S(1)}, bf16[128,1024]{1,0:T(8,128)(2,1)S(1)}, u32[]{:S(2)}, u32[]{:S(2)}) collective-permute-start(bf16[128,1024]{1,0:T(8,128)(2,1)S(1)} %collective-permute-done.refs_0_), channel_id=1, source_target_pairs={{0,2},{1,3},{2,0},{3,1},{4,6},{5,7},{6,4},{7,5},{8,10},{9,11},{10,... | collective-permute-start | bytes 786440 | tf_op jit(solution)/shard_map/ppermute | solution.py:38
  31.6 3.2 %collective-permute-start.18 = (bf16[128,1024]{1,0:T(8,128)(2,1)S(1)}, bf16[128,1024]{1,0:T(8,128)(2,1)S(1)}, u32[]{:S(2)}, u32[]{:S(2)}) collective-permute-start(bf16[128,1024]{1,0:T(8,128)(2,1)S(1)} %visit_2.1), channel_id=1, source_target_pairs={{0,8},{4,12},{8,0},{12,4},{1,9},{5,13},{9,1},{13,5},{2,10},{6,14},... | collective-permute-start | bytes 786440 | tf_op jit(solution)/shard_map/ppermute | solution.py:383
  35.4 2.2 %all_gather.9.refs_2_ = bf16[256,1024]{1,0:T(8,128)(2,1)S(1)} all-gather(bf16[128,1024]{1,0:T(8,128)(2,1)S(1)} %collective-permute-done.14), channel_id=1, replica_groups={{0,1},{2,3},{4,5},{6,7},{8,9},{10,11},{12,13},{14,15},{16,17},{18,19},{..., dimensions={0}, use_global_device_ids=true | all-gather | bytes 786432 | tf_op jit(solution)/shard_map/all_gather | solution.py:425
  37.6 2.3 %collective-permute-done.11 = bf16[128,1024]{1,0:T(8,128)(2,1)S(1)} collective-permute-done((bf16[128,1024]{1,0:T(8,128)(2,1)S(1)}, bf16[128,1024]{1,0:T(8,128)(2,1)S(1)}, u32[]{:S(2)}, u32[]{:S(2)}) %collective-permute-start.11) | collective-permute-done | bytes 262176 | tf_op jit(solution)/shard_map/ppermute | solution.py:38
  40.7 2.7 %visit_3.1 = bf16[128,1024]{1,0:T(8,128)(2,1)S(1)} custom-call(bf16[128,1024]{1,0:T(8,128)(2,1)S(1)} %collective-permute-done.12.refs_0_, bf16[128,1024]{1,0:T(8,128)(2,1)S(1)} %collective-permute-done.13.refs_1_, bf16[256,1024]{1,0:T(8,128)(2,1)S(1)} %all_gather.9.refs_2_, f32[1,4096]{1,0:T(1,128)S(1)} %get-tuple-element.42.refs_4_.refs_3_, ...), custom_call_target="tpu_custom_call" | custom-call | flops 1 | bytes 1 | tf_op jit(solution)/shard_map/visit_3/pallas_call | solution.py:149
  43.4 4.3 %collective-permute-start.19 = (bf16[128,1024]{1,0:T(8,128)(2,1)S(1)}, bf16[128,1024]{1,0:T(8,128)(2,1)S(1)}, u32[]{:S(2)}, u32[]{:S(2)}) collective-permute-start(bf16[128,1024]{1,0:T(8,128)(2,1)S(1)} %visit_3.1), channel_id=1, source_target_pairs={{0,12},{4,8},{8,4},{12,0},{1,13},{5,9},{9,5},{13,1},{2,14},{6,10},... | collective-permute-start | bytes 786440 | tf_op jit(solution)/shard_map/ppermute | solution.py:383
  47.7 2.3 %all_gather.10.refs_2_ = bf16[256,1024]{1,0:T(8,128)(2,1)S(1)} all-gather(bf16[128,1024]{1,0:T(8,128)(2,1)S(1)} %collective-permute-done.11), channel_id=1, replica_groups={{0,1},{2,3},{4,5},{6,7},{8,9},{10,11},{12,13},{14,15},{16,17},{18,19},{..., dimensions={0}, use_global_device_ids=true | all-gather | bytes 786432 | tf_op jit(solution)/shard_map/all_gather | solution.py:425
  50.0 2.7 %visit_1.1 = bf16[128,1024]{1,0:T(8,128)(2,1)S(1)} custom-call(bf16[128,1024]{1,0:T(8,128)(2,1)S(1)} %collective-permute-done.refs_0_, bf16[128,1024]{1,0:T(8,128)(2,1)S(1)} %collective-permute-done.10.refs_1_, bf16[256,1024]{1,0:T(8,128)(2,1)S(1)} %all_gather.10.refs_2_, f32[1,4096]{1,0:T(1,128)S(1)} %get-tuple-element.42.refs_4_.refs_3_, ...), custom_call_target="tpu_custom_call" | custom-call | flops 1 | bytes 1 | tf_op jit(solution)/shard_map/visit_1/pallas_call | solution.py:149
  52.9 2.4 %all_gather.11.refs_2_ = bf16[256,1024]{1,0:T(8,128)(2,1)S(1)} all-gather(bf16[128,1024]{1,0:T(8,128)(2,1)S(1)} %collective-permute-done.17), channel_id=1, replica_groups={{0,1},{2,3},{4,5},{6,7},{8,9},{10,11},{12,13},{14,15},{16,17},{18,19},{..., dimensions={0}, use_global_device_ids=true | all-gather | bytes 786432 | tf_op jit(solution)/shard_map/all_gather | solution.py:425
  55.2 2.7 %visit_0.1.refs_0_ = bf16[128,1024]{1,0:T(8,128)(2,1)S(1)} custom-call(bf16[128,1024]{1,0:T(8,128)(2,1)S(1)} %bitcast.9, bf16[128,1024]{1,0:T(8,128)(2,1)S(1)} %collective-permute-done.16.refs_1_, bf16[256,1024]{1,0:T(8,128)(2,1)S(1)} %all_gather.11.refs_2_, f32[1,4096]{1,0:T(1,128)S(1)} %get-tuple-element.42.refs_4_.refs_3_, ...), custom_call_target="tpu_custom_call" | custom-call | flops 1 | bytes 1 | tf_op jit(solution)/shard_map/visit_0/pallas_call | solution.py:149
  58.1 3.3 %collective-permute-done.15.refs_0_ = bf16[128,1024]{1,0:T(8,128)(2,1)S(1)} collective-permute-done((bf16[128,1024]{1,0:T(8,128)(2,1)S(1)}, bf16[128,1024]{1,0:T(8,128)(2,1)S(1)}, u32[]{:S(2)}, u32[]{:S(2)}) %collective-permute-start.15) | collective-permute-done | bytes 262176 | tf_op jit(solution)/shard_map/ppermute | solution.py:383
  61.4 0.8 %mean_of_visits.1 = bf16[128,1024]{1,0:T(8,128)(2,1)} custom-call(f32[128,128]{1,0:T(8,128)S(1)} %get-tuple-element.31.keep_ref, bf16[128,1024]{1,0:T(8,128)(2,1)S(1)} %collective-permute-done.15.refs_0_, f32[128,1024]{1,0:T(8,128)S(1)} %early_sum.1.refs_1_), custom_call_target="tpu_custom_call" | custom-call | tf_op jit(solution)/shard_map/mean_of_visits/pallas_call | solution.py:212
  (34 shorter events, 6.3 us)
Async XLA Ops:
  0.0 16.3 %collective-permute-start.1 = (bf16[128,1024]{1,0:T(8,128)(2,1)}, bf16[128,1024]{1,0:T(8,128)(2,1)S(1)}, u32[]{:S(2)}, u32[]{:S(2)}) collective-permute-start(bf16[128,1024]{1,0:T(8,128)(2,1)} %bitcast.5), channel_id=1, source_target_pairs={{0,8},{4,12},{8,0},{12,4},{1,9},{5,13},{9,1},{13,5},{2,10},{6,14},... | collective-permute-start | bytes 786440 | tf_op jit(solution)/shard_map/ppermute | solution.py:380
  4.0 13.8 %collective-permute-start = (bf16[128,1024]{1,0:T(8,128)(2,1)}, bf16[128,1024]{1,0:T(8,128)(2,1)S(1)}, u32[]{:S(2)}, u32[]{:S(2)}) collective-permute-start(bf16[128,1024]{1,0:T(8,128)(2,1)} %bitcast.6), channel_id=1, source_target_pairs={{0,4},{4,0},{8,12},{12,8},{1,5},{5,1},{9,13},{13,9},{2,6},{6,2},{1... | collective-permute-start | bytes 786440 | tf_op jit(solution)/shard_map/ppermute | solution.py:380
  5.6 1.2 %copy-start = (bf16[1,1024,512]{2,1,0:T(8,128)(2,1)S(1)}, bf16[1,1024,512]{2,1,0:T(8,128)(2,1)}, u32[]{:S(2)}) copy-start(bf16[1,1024,512]{2,1,0:T(8,128)(2,1)} %param.11) | copy-start | bytes 3145732
  7.0 7.6 %collective-permute-start.2 = (bf16[512,128]{1,0:T(8,128)(2,1)S(1)}, bf16[512,128]{1,0:T(8,128)(2,1)S(1)}, u32[]{:S(2)}, u32[]{:S(2)}) collective-permute-start(bf16[512,128]{1,0:T(8,128)(2,1)S(1)} %get-tuple-element.33), channel_id=1, source_target_pairs={{0,2},{1,3},{2,0},{3,1},{4,6},{5,7},{6,4},{7,5},{8,10},{9,11},{10,... | collective-permute-start | bytes 393224 | tf_op jit(solution)/shard_map/ppermute | solution.py:38
  8.6 6.1 %collective-permute-start.3 = (bf16[512,128]{1,0:T(8,128)(2,1)S(1)}, bf16[512,128]{1,0:T(8,128)(2,1)S(1)}, u32[]{:S(2)}, u32[]{:S(2)}) collective-permute-start(bf16[512,128]{1,0:T(8,128)(2,1)S(1)} %get-tuple-element.34), channel_id=1, source_target_pairs={{0,3},{1,2},{2,1},{3,0},{4,7},{5,6},{6,5},{7,4},{8,11},{9,10},{10,... | collective-permute-start | bytes 393224 | tf_op jit(solution)/shard_map/ppermute | solution.py:38
  8.6 12.0 %collective-permute-start.5 = (bf16[1024,128]{1,0:T(8,128)(2,1)S(1)}, bf16[1024,128]{1,0:T(8,128)(2,1)S(1)}, u32[]{:S(2)}, u32[]{:S(2)}) collective-permute-start(bf16[1024,128]{1,0:T(8,128)(2,1)S(1)} %get-tuple-element.37), channel_id=1, source_target_pairs={{0,1},{1,0},{2,3},{3,2},{4,5},{5,4},{6,7},{7,6},{8,9},{9,8},{10,11... | collective-permute-start | bytes 786440 | tf_op jit(solution)/shard_map/ppermute | solution.py:38
  9.2 0.7 %copy-start.2 = (s32[4]{0:T(128)S(1)}, s32[4]{0:T(128)}, u32[]{:S(2)}) copy-start(s32[4]{0:T(128)} %lengths_ref.1) | copy-start | bytes 52
  14.6 25.3 %copy-start.1 = (bf16[1,128,1024]{2,1,0:T(8,128)(2,1)S(1)}, bf16[1,128,1024]{2,1,0:T(8,128)(2,1)}, u32[]{:S(2)}) copy-start(bf16[1,128,1024]{2,1,0:T(8,128)(2,1)} %param.7) | copy-start | bytes 786436
  16.3 8.4 %collective-permute-start.8 = (bf16[128,1024]{1,0:T(8,128)(2,1)S(1)}, bf16[128,1024]{1,0:T(8,128)(2,1)S(1)}, u32[]{:S(2)}, u32[]{:S(2)}) collective-permute-start(bf16[128,1024]{1,0:T(8,128)(2,1)S(1)} %collective-permute-done.1.refs_0_), channel_id=1, source_target_pairs={{0,2},{1,3},{2,0},{3,1},{4,6},{5,7},{6,4},{7,5},{8,10},{9,11},{10,... | collective-permute-start | bytes 786440 | tf_op jit(solution)/shard_map/ppermute | solution.py:38
  17.8 5.5 %collective-permute-start.6 = (bf16[512,128]{1,0:T(8,128)(2,1)S(1)}, bf16[512,128]{1,0:T(8,128)(2,1)S(1)}, u32[]{:S(2)}, u32[]{:S(2)}) collective-permute-start(bf16[512,128]{1,0:T(8,128)(2,1)S(1)} %collective-permute-done.2.refs_2_), channel_id=1, source_target_pairs={{0,16},{16,0},{1,17},{17,1},{2,18},{18,2},{3,19},{19,3},{4,20},{20... | collective-permute-start | bytes 393224 | tf_op jit(solution)/shard_map/ppermute | solution.py:405
  19.3 5.3 %collective-permute-start.7 = (bf16[512,128]{1,0:T(8,128)(2,1)S(1)}, bf16[512,128]{1,0:T(8,128)(2,1)S(1)}, u32[]{:S(2)}, u32[]{:S(2)}) collective-permute-start(bf16[512,128]{1,0:T(8,128)(2,1)S(1)} %collective-permute-done.3.refs_4_), channel_id=1, source_target_pairs={{0,16},{16,0},{1,17},{17,1},{2,18},{18,2},{3,19},{19,3},{4,20},{20... | collective-permute-start | bytes 393224 | tf_op jit(solution)/shard_map/ppermute | solution.py:405
  19.8 6.4 %collective-permute-start.12 = (bf16[128,1024]{1,0:T(8,128)(2,1)S(1)}, bf16[128,1024]{1,0:T(8,128)(2,1)S(1)}, u32[]{:S(2)}, u32[]{:S(2)}) collective-permute-start(bf16[128,1024]{1,0:T(8,128)(2,1)S(1)} %collective-permute-done.1.refs_0_), channel_id=1, source_target_pairs={{0,4},{4,0},{8,12},{12,8},{1,5},{5,1},{9,13},{13,9},{2,6},{6,2},{1... | collective-permute-start | bytes 786440 | tf_op jit(solution)/shard_map/ppermute | solution.py:380
  20.5 6.4 %collective-permute-start.4 = (bf16[128,1024]{1,0:T(8,128)(2,1)S(1)}, bf16[128,1024]{1,0:T(8,128)(2,1)S(1)}, u32[]{:S(2)}, u32[]{:S(2)}) collective-permute-start(bf16[128,1024]{1,0:T(8,128)(2,1)S(1)} %collective-permute-done.1.refs_0_), channel_id=1, source_target_pairs={{0,1},{1,0},{2,3},{3,2},{4,5},{5,4},{6,7},{7,6},{8,9},{9,8},{10,11... | collective-permute-start | bytes 786440 | tf_op jit(solution)/shard_map/ppermute | solution.py:38
  25.5 1.6 %collective-permute-start.9 = (bf16[128,1024]{1,0:T(8,128)(2,1)S(1)}, bf16[128,1024]{1,0:T(8,128)(2,1)S(1)}, u32[]{:S(2)}, u32[]{:S(2)}) collective-permute-start(bf16[128,1024]{1,0:T(8,128)(2,1)S(1)} %get-tuple-element.41.refs_2_), channel_id=1, source_target_pairs={{0,1},{1,0},{2,3},{3,2},{4,5},{5,4},{6,7},{7,6},{8,9},{9,8},{10,11... | collective-permute-start | bytes 786440 | tf_op jit(solution)/shard_map/ppermute | solution.py:38
  26.2 9.2 %collective-permute-start.14 = (bf16[128,1024]{1,0:T(8,128)(2,1)S(1)}, bf16[128,1024]{1,0:T(8,128)(2,1)S(1)}, u32[]{:S(2)}, u32[]{:S(2)}) collective-permute-start(bf16[128,1024]{1,0:T(8,128)(2,1)S(1)} %collective-permute-done.12.refs_0_), channel_id=1, source_target_pairs={{0,2},{1,3},{2,0},{3,1},{4,6},{5,7},{6,4},{7,5},{8,10},{9,11},{10,... | collective-permute-start | bytes 786440 | tf_op jit(solution)/shard_map/ppermute | solution.py:38
  29.8 10.1 %collective-permute-start.11 = (bf16[128,1024]{1,0:T(8,128)(2,1)S(1)}, bf16[128,1024]{1,0:T(8,128)(2,1)S(1)}, u32[]{:S(2)}, u32[]{:S(2)}) collective-permute-start(bf16[128,1024]{1,0:T(8,128)(2,1)S(1)} %collective-permute-done.refs_0_), channel_id=1, source_target_pairs={{0,2},{1,3},{2,0},{3,1},{4,6},{5,7},{6,4},{7,5},{8,10},{9,11},{10,... | collective-permute-start | bytes 786440 | tf_op jit(solution)/shard_map/ppermute | solution.py:38
  31.1 9.6 %collective-permute-start.13 = (bf16[128,1024]{1,0:T(8,128)(2,1)S(1)}, bf16[128,1024]{1,0:T(8,128)(2,1)S(1)}, u32[]{:S(2)}, u32[]{:S(2)}) collective-permute-start(bf16[128,1024]{1,0:T(8,128)(2,1)S(1)} %collective-permute-done.12.refs_0_), channel_id=1, source_target_pairs={{0,1},{1,0},{2,3},{3,2},{4,5},{5,4},{6,7},{7,6},{8,9},{9,8},{10,11... | collective-permute-start | bytes 786440 | tf_op jit(solution)/shard_map/ppermute | solution.py:38
  31.1 19.0 %collective-permute-start.10 = (bf16[128,1024]{1,0:T(8,128)(2,1)S(1)}, bf16[128,1024]{1,0:T(8,128)(2,1)S(1)}, u32[]{:S(2)}, u32[]{:S(2)}) collective-permute-start(bf16[128,1024]{1,0:T(8,128)(2,1)S(1)} %collective-permute-done.refs_0_), channel_id=1, source_target_pairs={{0,1},{1,0},{2,3},{3,2},{4,5},{5,4},{6,7},{7,6},{8,9},{9,8},{10,11... | collective-permute-start | bytes 786440 | tf_op jit(solution)/shard_map/ppermute | solution.py:38
  31.6 26.4 %collective-permute-start.18 = (bf16[128,1024]{1,0:T(8,128)(2,1)S(1)}, bf16[128,1024]{1,0:T(8,128)(2,1)S(1)}, u32[]{:S(2)}, u32[]{:S(2)}) collective-permute-start(bf16[128,1024]{1,0:T(8,128)(2,1)S(1)} %visit_2.1), channel_id=1, source_target_pairs={{0,8},{4,12},{8,0},{12,4},{1,9},{5,13},{9,1},{13,5},{2,10},{6,14},... | collective-permute-start | bytes 786440 | tf_op jit(solution)/shard_map/ppermute | solution.py:383
  39.9 12.9 %collective-permute-start.17 = (bf16[128,1024]{1,0:T(8,128)(2,1)S(1)}, bf16[128,1024]{1,0:T(8,128)(2,1)S(1)}, u32[]{:S(2)}, u32[]{:S(2)}) collective-permute-start(bf16[128,1024]{1,0:T(8,128)(2,1)S(1)} %bitcast.7), channel_id=1, source_target_pairs={{0,2},{1,3},{2,0},{3,1},{4,6},{5,7},{6,4},{7,5},{8,10},{9,11},{10,... | collective-permute-start | bytes 786440 | tf_op jit(solution)/shard_map/ppermute | solution.py:38
  43.4 14.5 %collective-permute-start.19 = (bf16[128,1024]{1,0:T(8,128)(2,1)S(1)}, bf16[128,1024]{1,0:T(8,128)(2,1)S(1)}, u32[]{:S(2)}, u32[]{:S(2)}) collective-permute-start(bf16[128,1024]{1,0:T(8,128)(2,1)S(1)} %visit_3.1), channel_id=1, source_target_pairs={{0,12},{4,8},{8,4},{12,0},{1,13},{5,9},{9,5},{13,1},{2,14},{6,10},... | collective-permute-start | bytes 786440 | tf_op jit(solution)/shard_map/ppermute | solution.py:383
  47.7 7.5 %collective-permute-start.16 = (bf16[128,1024]{1,0:T(8,128)(2,1)S(1)}, bf16[128,1024]{1,0:T(8,128)(2,1)S(1)}, u32[]{:S(2)}, u32[]{:S(2)}) collective-permute-start(bf16[128,1024]{1,0:T(8,128)(2,1)S(1)} %bitcast.8), channel_id=1, source_target_pairs={{0,1},{1,0},{2,3},{3,2},{4,5},{5,4},{6,7},{7,6},{8,9},{9,8},{10,11... | collective-permute-start | bytes 786440 | tf_op jit(solution)/shard_map/ppermute | solution.py:38
  52.8 8.7 %collective-permute-start.15 = (bf16[128,1024]{1,0:T(8,128)(2,1)S(1)}, bf16[128,1024]{1,0:T(8,128)(2,1)S(1)}, u32[]{:S(2)}, u32[]{:S(2)}) collective-permute-start(bf16[128,1024]{1,0:T(8,128)(2,1)S(1)} %visit_1.1), channel_id=1, source_target_pairs={{0,4},{4,0},{8,12},{12,8},{1,5},{5,1},{9,13},{13,9},{2,6},{6,2},{1... | collective-permute-start | bytes 786440 | tf_op jit(solution)/shard_map/ppermute | solution.py:383
